TPU v7x, 32 devices: a whole 2x2x4 slice. The times are simulated.
32 devices in a mesh: pts: 8 (over z, x), grp: 4 (over y, core).
Axes of the slice: x: 2, y: 2, z: 4, core: 2. Of those that a mesh axis runs over, the one named last changes fastest.
Arguments:
- vertex_features: bfloat16 [16384, 256], P(('pts', 'grp')), may hold values from -6 to 6
- result_cotangent: bfloat16 [16384, 256], P(('pts', 'grp')), may hold values from -6 to 6
- entry_matrix: bfloat16 [256, 256], replicated, may hold values from -0.375 to 0.375
- exit_matrix: bfloat16 [256, 256], replicated, may hold values from -0.375 to 0.375
- cluster_matrix: bfloat16 [32, 64], replicated, may hold values from -4 to 4
- softmax_sharpness: float32 [8], replicated, may hold values from 0.1 to 2
- cluster_attention_matrices: float32 [3, 32, 32], replicated, may hold values from -2 to 2
- occupied_tally: int32 [32], replicated, may hold values from 170 to 512, as said below
Outputs:
- x_grad: bfloat16 [16384, 256], P(('pts', 'grp'))
- weight_grads: float32 [2, 256, 256], P(None, 'grp')
- slice_grad: float32 [32, 64], replicated
- temp_grad: float32 [8], replicated
- token_grads: float32 [3, 32, 32], replicated
Inputs may be any that keep to these rules, and one draw needn't show every extreme that they name: occupied_tally[i] is the number of valid points of the i-th block of 512 point slots; they come first in the block. Some block is full and some holds 170 in every draw.
All inputs are finite; a program needn't handle non-finite values.
Results may differ from a plain program's by a relative error of at most 0.012.
The roundings to bfloat16 on the way count: a program that leaves them out, or rounds other values in their place, can miss the bound.
Values may be sent and summed in bfloat16 or wider, within the bound.
No kernel may reach another device: no remote copies, remote signals or barrier semaphores. Data moves between devices by JAX's collectives and lax.ppermute only.
A program may use at most 64 MiB of HBM per device.

v0:
```python
import jax
import jax.numpy as jnp
from jax import lax
from jax.sharding import PartitionSpec as P


def block_diagonal(parts):
    attention_channels, inner, outer = parts.shape
    unit_matrix = jnp.eye(attention_channels, dtype=parts.dtype)
    spread_out = unit_matrix[:, None, :, None] * parts[:, :, None, :]
    return spread_out.reshape(attention_channels * inner, attention_channels * outer)


def segment_forward_sweep(
    feature_segment,
    result_cotangent_segment,
    validity_flags,
    entry_matrix,
    exit_matrix,
    slice_wide_weights,
    softmax_sharpness,
):
    point_rows = feature_segment.shape[0]
    attention_channels = softmax_sharpness.shape[0]
    xm = jnp.dot(feature_segment, entry_matrix, preferred_element_type=jnp.float32).astype(
        jnp.bfloat16
    )
    unscaled_product = jnp.dot(xm, slice_wide_weights, preferred_element_type=jnp.float32).reshape(
        point_rows, attention_channels, -1
    )
    cluster_scores = unscaled_product / softmax_sharpness[None, :, None]
    cluster_likelihood = jax.nn.softmax(cluster_scores, axis=-1)
    matrix_sequence = (cluster_likelihood * validity_flags[:, None, None]).astype(jnp.bfloat16)
    exit_cotangent = lax.dot_general(
        result_cotangent_segment,
        exit_matrix,
        (((1,), (1,)), ((), ())),
        preferred_element_type=jnp.float32,
    ).astype(jnp.bfloat16)
    return (xm, cluster_scores, cluster_likelihood, matrix_sequence, exit_cotangent)


def slice_middle(
    cluster_dividend, cluster_normalizer, blended_cotangent, cluster_attention_matrices
):
    highest_precision = lax.Precision.HIGHEST
    clip = jnp.maximum(cluster_normalizer, 1.0)
    slice_tokens = cluster_dividend / clip[..., None]
    scale = slice_tokens.shape[-1] ** (-0.5)
    query_rows = jnp.einsum(
        "cui,it->cut", slice_tokens, cluster_attention_matrices[0], precision=highest_precision
    )
    key_rows = jnp.einsum(
        "cui,it->cut", slice_tokens, cluster_attention_matrices[1], precision=highest_precision
    )
    value_rows = jnp.einsum(
        "cui,it->cut", slice_tokens, cluster_attention_matrices[2], precision=highest_precision
    )
    scores = jnp.einsum("hme,hne->hmn", query_rows, key_rows, precision=highest_precision) * scale
    attn = jax.nn.softmax(scores, axis=-1)
    mixed = jnp.einsum("hmn,hne->hme", attn, value_rows, precision=highest_precision)
    value_gradient = jnp.einsum(
        "hmn,hme->hne", attn, blended_cotangent, precision=highest_precision
    )
    g_attn = jnp.einsum("hme,hne->hmn", blended_cotangent, value_rows, precision=highest_precision)
    g_scores = attn * (g_attn - jnp.sum(g_attn * attn, axis=-1, keepdims=True)) * scale
    query_gradient = jnp.einsum("hmn,hne->hme", g_scores, key_rows, precision=highest_precision)
    key_gradient = jnp.einsum("hmn,hme->hne", g_scores, query_rows, precision=highest_precision)
    query_map_gradient = jnp.einsum(
        "sul,suv->lv", slice_tokens, query_gradient, precision=highest_precision
    )
    key_map_gradient = jnp.einsum(
        "sul,suv->lv", slice_tokens, key_gradient, precision=highest_precision
    )
    value_map_gradient = jnp.einsum(
        "sul,suv->lv", slice_tokens, value_gradient, precision=highest_precision
    )
    token_gradient = jnp.einsum(
        "cqr,jr->cqj", query_gradient, cluster_attention_matrices[0], precision=highest_precision
    )
    token_gradient = token_gradient + jnp.einsum(
        "cqr,jr->cqj", key_gradient, cluster_attention_matrices[1], precision=highest_precision
    )
    token_gradient = token_gradient + jnp.einsum(
        "cqr,jr->cqj", value_gradient, cluster_attention_matrices[2], precision=highest_precision
    )
    g_num = token_gradient / clip[..., None]
    normalizer_cotangent = jnp.where(
        cluster_normalizer > 1.0, -jnp.sum(token_gradient * slice_tokens, axis=-1) / clip, 0.0
    )
    return (
        mixed,
        g_num,
        normalizer_cotangent,
        jnp.stack([query_map_gradient, key_map_gradient, value_map_gradient]),
    )


def local(
    vertex_features,
    result_cotangent,
    entry_matrix,
    exit_matrix,
    cluster_matrix,
    softmax_sharpness,
    cluster_attention_matrices,
    occupied_tally,
):
    point_rows = vertex_features.shape[0]
    width = vertex_features.shape[1]
    attention_channels = softmax_sharpness.shape[0]
    head = width // attention_channels
    slices = cluster_matrix.shape[1]
    block = min(512, point_rows)
    groups = lax.axis_size("grp")
    device = lax.axis_index("pts") * groups + lax.axis_index("grp")
    owner_pick = jnp.arange(occupied_tally.shape[0], dtype=jnp.int32) == device
    valid = jnp.sum(jnp.where(owner_pick, occupied_tally, 0))
    x_rows, y_rows = (vertex_features, result_cotangent)
    trips = point_rows // block
    slice_wide_weights = block_diagonal(
        jnp.broadcast_to(cluster_matrix, (attention_channels, head, slices))
    )
    slice_back = block_diagonal(
        jnp.broadcast_to(cluster_matrix.T, (attention_channels, slices, head))
    )

    def take(index):
        begin = index * block
        validity_flags = (begin + jnp.arange(block, dtype=jnp.int32) < valid).astype(jnp.float32)
        return (begin, x_rows, y_rows, validity_flags)

    def first(index, loop_state):
        begin, feature_segment, result_cotangent_segment, validity_flags = take(index)
        xm, cluster_scores, cluster_likelihood, matrix_sequence, exit_cotangent = (
            segment_forward_sweep(
                feature_segment,
                result_cotangent_segment,
                validity_flags,
                entry_matrix,
                exit_matrix,
                slice_wide_weights,
                softmax_sharpness,
            )
        )
        cluster_dividend = jnp.einsum(
            "fzs,fzb->zsb",
            matrix_sequence,
            xm.reshape(block, attention_channels, head),
            preferred_element_type=jnp.float32,
        )
        cluster_normalizer = jnp.sum(matrix_sequence, axis=0, dtype=jnp.float32)
        blended_cotangent = jnp.einsum(
            "fzs,fzb->zsb",
            matrix_sequence,
            exit_cotangent.reshape(block, attention_channels, head),
            preferred_element_type=jnp.float32,
        )
        return (
            loop_state[0] + cluster_dividend,
            loop_state[1] + cluster_normalizer,
            loop_state[2] + blended_cotangent,
        )

    start = (
        jnp.zeros((attention_channels, slices, head), jnp.float32),
        jnp.zeros((attention_channels, slices), jnp.float32),
        jnp.zeros((attention_channels, slices, head), jnp.float32),
    )
    partial_sums = lax.fori_loop(0, trips, first, start)
    cluster_dividend, cluster_normalizer, blended_cotangent = lax.psum(
        (partial_sums[0], partial_sums[1], partial_sums[2]), ("pts", "grp")
    )
    mixed, g_num, normalizer_cotangent, token_grads = slice_middle(
        cluster_dividend, cluster_normalizer, blended_cotangent, cluster_attention_matrices
    )
    blended_bottom_share = mixed.astype(jnp.bfloat16)
    dividend_bottom_share = g_num.astype(jnp.bfloat16)
    merge_table = block_diagonal(blended_bottom_share)
    score_mixed = block_diagonal(jnp.swapaxes(blended_bottom_share, 1, 2))
    score_num = block_diagonal(jnp.swapaxes(dividend_bottom_share, 1, 2))
    back_num = block_diagonal(dividend_bottom_share)

    def second(index, loop_state):
        features_finished, cotangent_sequence, cluster_matrix_cotangent, sharpness_cotangent = (
            loop_state
        )
        begin, feature_segment, result_cotangent_segment, validity_flags = take(index)
        xm, cluster_scores, cluster_likelihood, matrix_sequence, exit_cotangent = (
            segment_forward_sweep(
                feature_segment,
                result_cotangent_segment,
                validity_flags,
                entry_matrix,
                exit_matrix,
                slice_wide_weights,
                softmax_sharpness,
            )
        )
        flat_weights = matrix_sequence.reshape(block, -1)
        merged_heads = jnp.dot(
            flat_weights, merge_table, preferred_element_type=jnp.float32
        ).astype(jnp.bfloat16)
        exit_matrix_cotangent = lax.dot_general(
            merged_heads,
            result_cotangent_segment,
            (((0,), (0,)), ((), ())),
            preferred_element_type=jnp.float32,
        )
        assign_weight_gradient = jnp.dot(
            exit_cotangent, score_mixed, preferred_element_type=jnp.float32
        )
        assign_weight_gradient = assign_weight_gradient + jnp.dot(
            xm, score_num, preferred_element_type=jnp.float32
        )
        assign_weight_gradient = (
            assign_weight_gradient.reshape(block, attention_channels, slices)
            + normalizer_cotangent[None]
        ) * validity_flags[:, None, None]
        score_cotangent = cluster_likelihood * (
            assign_weight_gradient
            - jnp.sum(assign_weight_gradient * cluster_likelihood, axis=-1, keepdims=True)
        )
        unscaled_cotangent = (score_cotangent / softmax_sharpness[None, :, None]).astype(
            jnp.bfloat16
        )
        g_xm = jnp.dot(flat_weights, back_num, preferred_element_type=jnp.float32)
        g_xm = g_xm + jnp.dot(
            unscaled_cotangent.reshape(block, -1), slice_back, preferred_element_type=jnp.float32
        )
        g_xm = g_xm.astype(jnp.bfloat16)
        slice_part = lax.dot_general(
            xm.reshape(block, attention_channels, head),
            unscaled_cotangent,
            (((0, 1), (0, 1)), ((), ())),
            preferred_element_type=jnp.float32,
        )
        sharpness_share = (
            -jnp.sum(score_cotangent * cluster_scores, axis=(0, 2)) / softmax_sharpness
        )
        feature_cotangent = lax.dot_general(
            g_xm, entry_matrix, (((1,), (1,)), ((), ())), preferred_element_type=jnp.float32
        ).astype(jnp.bfloat16)
        entry_matrix_cotangent = lax.dot_general(
            feature_segment, g_xm, (((0,), (0,)), ((), ())), preferred_element_type=jnp.float32
        )
        features_finished = feature_cotangent
        cotangent_sequence = cotangent_sequence + jnp.stack(
            [entry_matrix_cotangent, exit_matrix_cotangent]
        )
        return (
            features_finished,
            cotangent_sequence,
            cluster_matrix_cotangent + slice_part,
            sharpness_cotangent + sharpness_share,
        )

    start2 = (
        jnp.zeros((point_rows, width), jnp.bfloat16),
        jnp.zeros((2, width, width), jnp.float32),
        jnp.zeros((head, slices), jnp.float32),
        jnp.zeros((attention_channels,), jnp.float32),
    )
    features_finished, local_grads, slice_local, temp_local = lax.fori_loop(
        0, trips, second, start2
    )
    slice_grad, temp_grad = lax.psum((slice_local, temp_local), ("pts", "grp"))
    summed = lax.psum(local_grads, "pts")
    weight_grads = lax.psum_scatter(
        summed.astype(jnp.bfloat16), "grp", scatter_dimension=1, tiled=True
    ).astype(jnp.float32)
    return (features_finished, weight_grads, slice_grad, temp_grad, token_grads)


def solution(mesh):
    return jax.shard_map(
        local,
        mesh=mesh,
        in_specs=(P(("pts", "grp"), None), P(("pts", "grp"), None), P(), P(), P(), P(), P(), P()),
        out_specs=(P(("pts", "grp"), None), P(None, "grp", None), P(), P(), P()),
        check_vma=False,
    )
```

profile of v0, /device:TPU:0, one launch (start us, length us, event | category | flops | bytes accessed | tf_op | source)
XLA Modules:
  0.0 257.5 jit_solution(8679822582706256946)
XLA Ops:
  7.3 0.8 broadcast_multiply_fusion.5
  13.0 0.9 fusion.49
  14.2 0.9 fusion.50
  15.2 1.3 convolution_divide_fusion
  16.6 42.2 %psum.43 = f32[8,64]{1,0:T(8,128)S(1)} all-reduce(f32[8,64]{1,0:T(8,128)S(1)} %get-tuple-element.102), channel_id=1, replica_groups=mesh['pts'=8,'grp'=4] {'pts','grp'}, use_global_device_ids=true, to_apply=%region_5.6 | all-reduce | flops 512 | bytes 4096 | tf_op jit(solution)/shard_map/psum | solution.py:171
  60.0 83.2 %all-reduce.9.cloned.1.call-done = (f32[8,64,32]{1,2,0:T(8,128)}, f32[8,64,32]{1,2,0:T(8,128)}) async-done(((f32[8,64,32]{1,2,0:T(8,128)}, f32[8,64,32]{1,2,0:T(8,128)}), (f32[8,64,32]{1,2,0:T(8,128)}, f32[8,64,32]{1,2,0:T(8,128)})) %all-reduce.9.cloned.1.call-update) | async-done | bytes 131088 | tf_op jit(solution)/shard_map/psum | solution.py:171
  143.2 1.3 fusion.23
  145.9 0.8 copy-done.18
  148.9 0.9 convolution_bitcast_fusion.3
  150.4 0.9 convolution_bitcast_fusion.1
  151.3 0.8 convolution_bitcast_fusion.2
  152.4 0.9 multiply_reduce_fusion.3
  153.3 0.7 copy.79
  153.9 0.7 copy.81
  156.4 1.8 broadcast_multiply_fusion
  158.3 2.1 mul.184
  160.4 1.0 mul.196
  163.5 0.7 multiply_reduce_fusion
  165.0 1.0 convolution_convert_fusion.1
  167.6 42.5 %all-reduce.10 = bf16[2,256,256]{1,2,0:T(8,128)(2,1)S(1)} all-reduce(f32[2,256,256]{1,2,0:T(8,128)S(1)} %pad_maximum_fusion), channel_id=1, replica_groups=mesh['pts'=8,'grp'=4] {'pts'}, use_global_device_ids=true, to_apply=%region_12.13 | all-reduce | flops 131072 | bytes 786432 | tf_op jit(solution)/shard_map/psum | solution.py:268
  210.1 0.9 copy.83
  211.2 37.2 %all-reduce.1 = (f32[32,64]{1,0:T(8,128)}, f32[8]{0:T(128)}) all-reduce(f32[32,64]{1,0:T(8,128)S(1)} %convolution_bitcast_fusion.4, f32[8]{0:T(128)S(1)} %negate_divide_fusion), channel_id=1, replica_groups=mesh['pts'=8,'grp'=4] {'pts','grp'}, use_global_device_ids=true, to_apply=%region_14.15 | all-reduce | flops 2056 | bytes 16448 | tf_op jit(solution)/shard_map/psum | solution.py:267
  249.1 0.9 dynamic-slice_convert_fusion
  250.0 0.7 copy.84
  (90 shorter events, 17.4 us)
Async XLA Ops:
  7.2 3.4 %copy-start = (bf16[512,256]{1,0:T(8,128)(2,1)S(1)}, bf16[512,256]{1,0:T(8,128)(2,1)}, u32[]{:S(2)}) copy-start(bf16[512,256]{1,0:T(8,128)(2,1)} %param.8) | copy-start | bytes 786436
  7.2 136.0 %all-reduce.9.cloned.1.call-start = ((), (), s32[]{:S(2)}) async-start(), calls=%async_computation.1 | async-start | bytes 524288 | tf_op jit(solution)/shard_map/psum | solution.py:171
  8.5 2.1 copy-start.7
  8.6 0.7 copy-start.19
  12.0 1.0 copy-start.4
  13.0 0.9 copy-start.2
  13.0 1.0 copy-start.8
  15.2 233.9 %all-reduce.7.cloned.1.call-start = ((), (), s32[]{:S(2)}) async-start(), calls=%async_computation | async-start | bytes 524288
  15.2 43.6 %copy-start.22 = (u32[32]{0:T(128)S(1)}, u32[32]{0:T(128)}, u32[]{:S(2)}) copy-start(u32[32]{0:T(128)} %constant.28) | copy-start | bytes 388
  16.6 126.6 %copy-start.10 = (f32[3,32,32]{2,1,0:T(8,128)S(1)}, f32[3,32,32]{2,1,0:T(8,128)}, u32[]{:S(2)}) copy-start(f32[3,32,32]{2,1,0:T(8,128)} %param.14) | copy-start | bytes 36868
  143.2 1.3 copy-start.17
  145.8 0.9 copy-start.18
  155.4 0.7 copy-start.16
  155.7 0.7 copy-start.9
  161.4 0.9 copy-start.1
  161.4 1.3 copy-start.23
  161.8 1.4 copy-start.5
  162.4 0.9 copy-start.12
  162.7 0.7 copy-start.21
  163.5 0.9 copy-start.6
  166.0 1.0 copy-start.3
  210.9 37.5 %copy-start.14 = (f32[1,32,32]{2,1,0:T(8,128)S(1)}, f32[1,32,32]{2,1,0:T(8,128)}, u32[]{:S(2)}) copy-start(f32[1,32,32]{2,1,0:T(8,128)} %convolution_bitcast_fusion.1) | copy-start | bytes 12292
  211.0 37.5 %copy-start.15 = (f32[1,32,32]{2,1,0:T(8,128)S(1)}, f32[1,32,32]{2,1,0:T(8,128)}, u32[]{:S(2)}) copy-start(f32[1,32,32]{2,1,0:T(8,128)} %convolution_bitcast_fusion.2) | copy-start | bytes 12292
  211.2 37.2 %copy-start.13 = (f32[1,32,32]{2,1,0:T(8,128)S(1)}, f32[1,32,32]{2,1,0:T(8,128)}, u32[]{:S(2)}) copy-start(f32[1,32,32]{2,1,0:T(8,128)} %convolution_bitcast_fusion.3) | copy-start | bytes 12292
  (2 other events, 1.3 us)
Sparse Core Ops, SparseCore 0:
  15.3 127.8 all-reduce.8
  211.1 29.7 all-reduce.6
where the time goes:
time: 259 us; the launch traced here: 257 us
  blocking collectives  122 us (47%)
  waiting for transfers between devices  83.2 us (32%)
  matrix products  16.7 us (6%)
  between operations  15.1 us (6%)
  local copies, waits for them, and re-layouts  13.9 us (5%)
  other arithmetic  6.62 us (3%)
    psum x1, waiting for transfers between devices, local(): lax.psum((partial_sums[0], partial_sums[1], partial_sums[2]), ('pts', 'gr...  83.2 us
    psum x1, blocking collectives, local(): summed = lax.psum(local_grads, 'pts')  42.5 us
    psum x1, blocking collectives, local(): lax.psum((partial_sums[0], partial_sums[1], partial_sums[2]), ('pts', 'gr...  42.2 us
    psum x1, blocking collectives, local(): slice_grad, temp_grad = lax.psum((slice_local, temp_local), ('pts', 'grp'))  37.2 us
    unnamed x50, local copies, waits for them, and re-layouts  7.11 us
  transfers between devices with their start and end apart: 2, of which 1 were waited for; matrix products, arithmetic and copies ran while one was open for 1% of the time, Pallas kernels for 0%

commit v1 on v0

v1 whole, which is shorter than its diff:
```python
import jax
import jax.numpy as jnp
from jax import lax
from jax.experimental import pallas as pl
from jax.experimental.pallas import tpu as pltpu
from jax.sharding import PartitionSpec as P

F32 = jnp.float32
BF16 = jnp.bfloat16
ALL = ("pts", "grp")
LANES = 128
VMEM_LIMIT = 48 * 1024 * 1024
POINTS_LIMIT = 60 * 1024 * 1024


def dot(a, b):
    return lax.dot_general(a, b, (((1,), (0,)), ((), ())), preferred_element_type=F32)


def dot_nt(a, b):
    return lax.dot_general(a, b, (((1,), (1,)), ((), ())), preferred_element_type=F32)


def dot_tn(a, b):
    return lax.dot_general(a, b, (((0,), (0,)), ((), ())), preferred_element_type=F32)


def split(a):
    high = a.astype(BF16)
    return high, (a - high.astype(F32)).astype(BF16)


def dot3(product, a, b):
    return product(a[0], b[0]) + (product(a[1], b[0]) + product(a[0], b[1]))


def head_mask(shape, row_size, lane_size):
    rows = lax.broadcasted_iota(jnp.int32, shape, 0) // row_size
    lanes = lax.broadcasted_iota(jnp.int32, shape, 1) // lane_size
    return rows == lanes


def inverse_row(scalar_ref, index, length):
    return 1.0 / jnp.full((1, length), scalar_ref[index], F32)


def assign(sharp, x, entry, cluster, valid, xmt, weights, live_probs):
    points, width = x.shape
    heads = sharp.shape[0]
    head = width // heads
    slices = cluster.shape[1]
    xm = dot(x[...], entry[...]).astype(BF16)
    xmt[...] = xm.T
    cluster_t = cluster[...].T
    live = (lax.broadcasted_iota(jnp.int32, (1, points), 1) < valid).astype(F32)
    for h in range(heads):
        raw = dot(cluster_t, xmt[h * head : (h + 1) * head, :])
        logits = raw * inverse_row(sharp, h, points)
        e = jnp.exp(logits - jnp.max(logits, axis=0, keepdims=True))
        probs = e * (live / jnp.sum(e, axis=0, keepdims=True))
        if live_probs is not None:
            live_probs[h * slices : (h + 1) * slices, :] = probs
        weights[h * slices : (h + 1) * slices, :] = probs.astype(BF16)
    return xm


def valid_points(tally):
    return tally[lax.axis_index("pts") * lax.axis_size("grp") + lax.axis_index("grp")]


def points_kernel(
    tally_in,
    sharp_in,
    x_in,
    rc_in,
    entry_in,
    exit_in,
    cluster_in,
    payload,
    tally,
    sharp,
    x,
    rc,
    entry,
    exit_,
    cluster,
    xmt,
    weights,
    arrived,
):
    pairs = [
        (entry_in, entry),
        (x_in, x),
        (cluster_in, cluster),
        (sharp_in, sharp),
        (tally_in, tally),
        (exit_in, exit_),
        (rc_in, rc),
    ]
    copies = [
        pltpu.make_async_copy(source, target, arrived.at[i])
        for i, (source, target) in enumerate(pairs)
    ]
    for copy in copies:
        copy.start()
    points, width = x.shape
    heads = sharp.shape[0]
    head = width // heads
    slices = cluster.shape[1]
    per = LANES // head
    groups = heads // per
    for copy in copies:
        copy.wait()
    go = dot_nt(rc[...], exit_[...]).astype(BF16)
    xm = assign(sharp, x, entry, cluster, valid_points(tally), xmt, weights, None)
    rows = groups * slices
    lane_head = lax.broadcasted_iota(jnp.int32, (slices, 2 * LANES), 1) % LANES // head
    for g in range(groups):
        w = weights[g * per * slices : (g + 1) * per * slices, :]
        cut = slice(g * LANES, (g + 1) * LANES)
        full = dot(w, jnp.concatenate([xm[:, cut], go[:, cut]], axis=1))
        own = jnp.zeros((slices, 2 * LANES), F32)
        for j in range(per):
            own = jnp.where(lane_head == j, full[j * slices : (j + 1) * slices, :], own)
        payload[g * slices : (g + 1) * slices, :] = own[:, :LANES].astype(BF16)
        payload[rows + g * slices : rows + (g + 1) * slices, :] = own[:, LANES:].astype(BF16)
    ones = jnp.ones((heads, points), BF16)
    den = jnp.zeros((heads, rows), F32)
    head_row = lax.broadcasted_iota(jnp.int32, (heads, rows), 0)
    lane_group = lax.broadcasted_iota(jnp.int32, (heads, rows), 1) // slices
    for j in range(per):
        w = jnp.concatenate(
            [
                weights[(g * per + j) * slices : (g * per + j + 1) * slices, :]
                for g in range(groups)
            ],
            axis=0,
        )
        den = jnp.where(head_row == lane_group * per + j, dot_nt(ones, w), den)
    high = den.astype(BF16).astype(F32)
    payload[2 * rows :, :] = jnp.concatenate([high, den - high], axis=0).astype(BF16)


def shadow_kernel(
    tally,
    sharp,
    x,
    rc,
    entry,
    exit_,
    cluster,
    maps,
    payload_in,
    payload,
    xmt,
    got,
    weights,
    live_probs,
    maps_high,
    maps_low,
    cluster_rows,
):
    payload[...] = payload_in[...]
    assign(sharp, x, entry, cluster, valid_points(tally), xmt, weights, live_probs)
    got[...] = dot_nt(rc[...], exit_[...]).astype(BF16).T
    head = maps.shape[1]
    slices = cluster.shape[1]
    per = LANES // head
    mask = head_mask((LANES, LANES), head, head)
    for i in range(maps.shape[0]):
        a = jnp.concatenate([maps[i]] * per, axis=0)
        a = jnp.where(mask, jnp.concatenate([a] * per, axis=1), 0.0)
        high, low = split(a)
        maps_high[:, i * LANES : (i + 1) * LANES] = high
        maps_low[:, i * LANES : (i + 1) * LANES] = low
    c = cluster[...].astype(F32).T
    c = jnp.concatenate([c] * per, axis=1)
    c = jnp.concatenate([c] * per, axis=0)
    c = jnp.where(head_mask(c.shape, slices, head), c, 0.0)
    cluster_rows[...] = c.astype(BF16)


def middle_kernel(
    sharp,
    mine,
    other,
    maps_high,
    maps_low,
    cluster_rows,
    xmt,
    got,
    weights,
    live_probs,
    x,
    rc,
    keep,
    send,
    gxmt,
    tokens_out,
    grads_out,
    grad_rows,
):
    points, width = x.shape
    heads = sharp.shape[0]
    head = width // heads
    per = LANES // head
    groups = heads // per
    slices = cluster_rows.shape[0] // per
    rows = groups * slices
    scale = head**-0.5
    total = mine[...].astype(F32) + other[...].astype(F32)
    num = total[:rows]
    mixed_cotangent = total[rows : 2 * rows]
    den_rows = total[2 * rows : 2 * rows + heads] + total[2 * rows + heads : 2 * rows + 2 * heads]
    spread = (
        lax.broadcasted_iota(jnp.int32, (heads, LANES), 0) % per
        == lax.broadcasted_iota(jnp.int32, (heads, LANES), 1) // head
    ).astype(F32)
    d0 = den_rows.astype(BF16)
    rest = den_rows - d0.astype(F32)
    d1 = rest.astype(BF16)
    d2 = (rest - d1.astype(F32)).astype(BF16)
    spread = spread.astype(BF16)
    den = dot_tn(
        jnp.concatenate([d0.astype(F32), d1.astype(F32), d2.astype(F32)], axis=0).astype(BF16),
        jnp.concatenate([spread.astype(F32)] * 3, axis=0).astype(BF16),
    )
    clip_inverse = 1.0 / jnp.maximum(den, 1.0)
    tokens = num * clip_inverse
    tokens_out[...] = tokens
    maps = (maps_high[...], maps_low[...])
    qkv = dot3(dot, split(tokens), maps)
    wide = (LANES, per * slices)
    lane_mask = head_mask(wide, head, slices)
    row_mask = head_mask((per * slices, LANES), slices, head)

    def spread_heads(a):
        doubled = jnp.concatenate([a] * (LANES // slices), axis=0).T
        doubled = jnp.concatenate([doubled] * (per * slices // LANES), axis=1)
        return split(jnp.where(lane_mask, doubled, 0.0))

    def fold_heads(a):
        kept = jnp.where(row_mask, a, 0.0)
        out = kept[:slices]
        for j in range(1, per):
            out = out + kept[j * slices : (j + 1) * slices]
        return kept, out

    mixed_blocks, query_grads, key_grads, value_grads = [], [], [], []
    for g in range(groups):
        cut = slice(g * slices, (g + 1) * slices)
        q, k, v = (qkv[cut, i * LANES : (i + 1) * LANES] for i in range(3))
        gm = mixed_cotangent[cut]
        q_blocks, gm_blocks = spread_heads(q), spread_heads(gm)
        k2, v2 = split(k), split(v)
        scores = dot3(dot, k2, q_blocks) * scale
        g_attn = dot3(dot, v2, gm_blocks)
        e = jnp.exp(scores - jnp.max(scores, axis=0, keepdims=True))
        attn = e / jnp.sum(e, axis=0, keepdims=True)
        g_scores = attn * (g_attn - jnp.sum(g_attn * attn, axis=0, keepdims=True)) * scale
        attn2, gs2 = split(attn), split(g_scores)
        value_grads.append(dot3(dot_nt, attn2, gm_blocks))
        key_grads.append(dot3(dot_nt, gs2, q_blocks))
        attn_t, gs_t = split(attn.T), split(g_scores.T)
        query_grads.append(fold_heads(dot3(dot, gs_t, k2))[1])
        mixed_blocks.append(fold_heads(dot3(dot, attn_t, v2))[0].astype(BF16))
    grads = jnp.concatenate(
        [
            jnp.concatenate(query_grads, axis=0),
            jnp.concatenate(key_grads, axis=0),
            jnp.concatenate(value_grads, axis=0),
        ],
        axis=1,
    )
    grads_out[...] = grads
    token_cotangent = dot3(dot_nt, split(grads), maps)
    num_cotangent = token_cotangent * clip_inverse
    den_terms = jnp.where(den > 1.0, -token_cotangent * tokens * clip_inverse, 0.0)

    owners = grad_rows.shape[0]
    owner_rows = width // owners
    slice_sum = jnp.zeros((head, per * slices), F32)
    slice_mask = head_mask((LANES, per * slices), head, slices)
    temps = []
    for g in range(groups):
        cut = slice(g * slices, (g + 1) * slices)
        big = slice(g * per * slices, (g + 1) * per * slices)
        small = slice(g * LANES, (g + 1) * LANES)
        num_block = jnp.where(
            row_mask, jnp.concatenate([num_cotangent[cut]] * per, axis=0), 0.0
        ).astype(BF16)
        den_column = jnp.sum(
            jnp.where(row_mask, jnp.concatenate([den_terms[cut]] * per, axis=0), 0.0),
            axis=1,
            keepdims=True,
        )
        table = jnp.concatenate([mixed_blocks[g], num_block], axis=1)
        w = weights[big, :]
        xm_g = xmt[small, :]
        both = dot_tn(table, w)
        merged = both[:LANES].astype(BF16)
        grad_exit = dot(merged, rc[...])
        g_w = dot(table, jnp.concatenate([got[small, :], xm_g], axis=0)) + den_column
        raw = dot(cluster_rows[...], xm_g)
        g_raw = []
        for j in range(per):
            h = g * per + j
            part = slice(j * slices, (j + 1) * slices)
            lp = live_probs[h * slices : (h + 1) * slices, :]
            t = g_w[part] * lp
            g_logits = t - lp * jnp.sum(t, axis=0, keepdims=True)
            inverse = inverse_row(sharp, h, points)
            row = jnp.sum(g_logits * raw[part], axis=0, keepdims=True) * (inverse * inverse)
            temps.append(-row)
            g_raw.append((g_logits * inverse).astype(BF16))
        g_raw = jnp.concatenate(g_raw, axis=0)
        g_xm = (both[LANES:] + dot_tn(cluster_rows[...], g_raw)).astype(BF16)
        gxmt[small, :] = g_xm
        grad_entry = dot(g_xm, x[...]).T
        block = jnp.where(slice_mask, dot_nt(xm_g, g_raw), 0.0)
        for j in range(per):
            slice_sum = slice_sum + block[j * head : (j + 1) * head]
        for o in range(owners):
            grad_rows[o, :owner_rows, small] = grad_entry[
                o * owner_rows : (o + 1) * owner_rows
            ].astype(BF16)
        for r in range(g * LANES // owner_rows, (g + 1) * LANES // owner_rows):
            start = r * owner_rows - g * LANES
            grad_rows[r, owner_rows:, :] = grad_exit[start : start + owner_rows].astype(BF16)
    folded = slice_sum[:, :LANES]
    for i in range(1, per * slices // LANES):
        folded = folded + slice_sum[:, i * LANES : (i + 1) * LANES]
    half = head // 2
    temp = jnp.sum(jnp.concatenate(temps, axis=0), axis=1, keepdims=True)
    temp = jnp.broadcast_to(temp, (heads, width))
    temp_high = temp.astype(BF16).astype(F32)
    extra = jnp.concatenate(
        [jnp.concatenate([folded[:half], folded[half:]], axis=1), temp_high, temp - temp_high],
        axis=0,
    ).astype(BF16)
    odd = lax.axis_index("grp") % 2
    chunk = 2 * owner_rows
    for i in range(owners // 2):
        keep[i * chunk : (i + 1) * chunk, :] = grad_rows[2 * i + odd]
        send[i * chunk : (i + 1) * chunk, :] = grad_rows[2 * i + 1 - odd]
    keep[owners // 2 * chunk :, :] = extra
    send[owners // 2 * chunk :, :] = extra


def features_kernel(gxmt, entry, tokens, grads, x_grad, token_grads):
    x_grad[...] = dot_nt(gxmt[...].T, entry[...]).astype(BF16)
    maps, head = token_grads.shape[:2]
    per = LANES // head
    full = dot3(dot, split(tokens[...].T), split(grads[...]))
    for i in range(maps):
        part = full[:, i * LANES : (i + 1) * LANES]
        part = jnp.where(head_mask((LANES, LANES), head, head), part, 0.0)
        out = part[:head]
        for j in range(1, per):
            out = out + part[j * head : (j + 1) * head]
        shift = LANES // 2
        while shift >= head:
            out = out + pltpu.roll(out, shift, 1)
            shift //= 2
        token_grads[i] = out[:, :head]


def finish_kernel(mine, other, weight_grads, slice_grad, temp_grad):
    total = mine[...].astype(F32) + other[...].astype(F32)
    owner_rows = weight_grads.shape[1]
    head, slices = slice_grad.shape
    weight_grads[0] = total[:owner_rows]
    weight_grads[1] = total[owner_rows : 2 * owner_rows]
    half = head // 2
    extra = total[2 * owner_rows :]
    folded = jnp.concatenate([extra[:half, :LANES], extra[:half, LANES : 2 * LANES]], axis=0)
    shift = LANES // 2
    while shift >= slices:
        folded = folded + pltpu.roll(folded, shift, 1)
        shift //= 2
    slice_grad[...] = folded[:, :slices]
    heads = temp_grad.shape[1]
    temp = (extra[half : half + heads] + extra[half + heads : half + 2 * heads])[:, :LANES]
    temp = jnp.where(head_mask(temp.shape, 1, 1), temp, 0.0)
    temp_grad[...] = jnp.sum(temp, axis=0, keepdims=True)[:, :heads]


def call(kernel, shapes, in_smem, count, scratch=(), space=pltpu.VMEM, limit=VMEM_LIMIT):
    smem = pl.BlockSpec(memory_space=pltpu.SMEM)
    vmem = pl.BlockSpec(memory_space=pltpu.VMEM)
    rest = pl.BlockSpec(memory_space=space)
    return pl.pallas_call(
        kernel,
        out_shape=[jax.ShapeDtypeStruct(s, d) for s, d in shapes],
        in_specs=[smem] * in_smem + [rest] * (count - in_smem),
        out_specs=[vmem] * len(shapes),
        scratch_shapes=list(scratch),
        compiler_params=pltpu.CompilerParams(vmem_limit_bytes=limit),
    )


def exchange(a, mask):
    devices = lax.axis_size("pts") * lax.axis_size("grp")
    return lax.ppermute(a, ALL, [(i, i ^ mask) for i in range(devices)])


def halves(total, start):
    pair = total[start:]
    n = pair.shape[0] // 2
    pair = pair[:n] + pair[n:]
    high = lax.reduce_precision(pair, 8, 7)
    return jnp.concatenate([total[:start], high, pair - high], axis=0).astype(BF16)


def local(x, rc, entry, exit_, cluster, sharp, maps, tally):
    points, width = x.shape
    heads = sharp.shape[0]
    head, slices = cluster.shape
    owners = lax.axis_size("grp")
    devices = lax.axis_size("pts") * owners
    per = LANES // head
    rows = heads // per * slices
    token_rows = 2 * rows + 2 * heads
    (payload,) = call(
        points_kernel,
        [((token_rows, LANES), BF16)],
        0,
        7,
        scratch=[
            pltpu.SMEM(tally.shape, tally.dtype),
            pltpu.SMEM(sharp.shape, sharp.dtype),
            *(pltpu.VMEM(a.shape, a.dtype) for a in (x, rc, entry, exit_, cluster)),
            pltpu.VMEM((width, points), BF16),
            pltpu.VMEM((heads * slices, points), BF16),
            pltpu.SemaphoreType.DMA((7,)),
        ],
        space=pltpu.HBM,
        limit=POINTS_LIMIT,
    )(tally, sharp, x, rc, entry, exit_, cluster)
    other = exchange(payload, 8)
    mine, xmt, got, weights, live_probs, maps_high, maps_low, cluster_rows = call(
        shadow_kernel,
        [
            ((token_rows, LANES), BF16),
            ((width, points), BF16),
            ((width, points), BF16),
            ((heads * slices, points), BF16),
            ((heads * slices, points), F32),
            ((LANES, 3 * LANES), BF16),
            ((LANES, 3 * LANES), BF16),
            ((per * slices, LANES), BF16),
        ],
        2,
        9,
    )(tally, sharp, x, rc, entry, exit_, cluster, maps, payload)
    mine = halves(mine.astype(F32) + other.astype(F32), 2 * rows)
    mask = 16
    while mask < devices:
        other = exchange(mine, mask)
        mine = halves(mine.astype(F32) + other.astype(F32), 2 * rows)
        mask *= 2
    far, b, a = exchange(mine, 6), exchange(mine, 2), exchange(mine, 4)
    mine = halves(
        (mine.astype(F32) + a.astype(F32)) + (b.astype(F32) + far.astype(F32)), 2 * rows
    )
    other = exchange(mine, 1)

    owner_rows = width // owners
    chunk = 2 * owner_rows
    extra = head // 2 + 2 * heads
    keep, send, gxmt, tokens, grads = call(
        middle_kernel,
        [
            ((owners // 2 * chunk + extra, width), BF16),
            ((owners // 2 * chunk + extra, width), BF16),
            ((width, points), BF16),
            ((rows, LANES), F32),
            ((rows, 3 * LANES), F32),
        ],
        1,
        12,
        scratch=[pltpu.VMEM((owners, chunk, width), BF16)],
    )(
        sharp,
        mine,
        other,
        maps_high,
        maps_low,
        cluster_rows,
        xmt,
        got,
        weights,
        live_probs,
        x,
        rc,
    )

    got_half = exchange(send, 1)
    x_grad, token_grads = call(
        features_kernel,
        [((points, width), BF16), (maps.shape, F32)],
        0,
        4,
    )(gxmt, entry, tokens, grads)
    total = keep.astype(F32) + got_half.astype(F32)
    total = halves(total, total.shape[0] - 2 * heads)
    half = lax.axis_index("grp") // 2
    common = total[owners // 2 * chunk :]
    mine = jnp.concatenate(
        [lax.dynamic_slice_in_dim(total, half * chunk, chunk), common], axis=0
    )
    theirs = jnp.concatenate(
        [lax.dynamic_slice_in_dim(total, (1 - half) * chunk, chunk), common], axis=0
    )
    far, b, a = exchange(theirs, 6), exchange(theirs, 2), exchange(mine, 4)
    total = (mine.astype(F32) + a.astype(F32)) + (b.astype(F32) + far.astype(F32))
    mine = halves(total, total.shape[0] - 2 * heads)
    mask = 8
    while 2 * mask < devices:
        other = exchange(mine, mask)
        total = mine.astype(F32) + other.astype(F32)
        mine = halves(total, total.shape[0] - 2 * heads)
        mask *= 2
    other = exchange(mine, mask)
    weight_grads, slice_grad, temp_grad = call(
        finish_kernel,
        [
            ((2, owner_rows, width), F32),
            ((head, slices), F32),
            ((1, heads), F32),
        ],
        0,
        2,
    )(mine, other)
    return x_grad, weight_grads, slice_grad, temp_grad.reshape(heads), token_grads


def solution(mesh):
    return jax.shard_map(
        local,
        mesh=mesh,
        in_specs=(P(ALL, None), P(ALL, None), P(), P(), P(), P(), P(), P()),
        out_specs=(P(ALL, None), P(None, "grp", None), P(), P(), P()),
        check_vma=False,
    )
```

time: 259 us -> 47.8 us (0.18)
  blocking collectives: 122 us -> 0 us
  waiting for transfers between devices: 83.2 us -> 17.1 us
  starting transfers between devices: 0.08 us -> 18.3 us
  matrix products: 16.7 us -> 0 us
  between operations: 15.1 us -> 0.95 us
  local copies, waits for them, and re-layouts: 13.9 us -> 1.02 us
  Pallas kernels: 0 us -> 9.92 us
  other arithmetic: 6.62 us -> 0.29 us
    psum x3 -> x0, blocking collectives: 122 us -> none  [the longest x1 42.5 us: local(): summed = lax.psum(local_grads, 'pts')]
    psum x1 -> x0, waiting for transfers between devices: 83.2 us -> none  [local(): lax.psum((partial_sums[0], partial_sums[1], partial_sums[2]), ('pts', 'gr...]
    ppermute x0 -> x12, starting transfers between devices: none -> 18.3 us  [exchange(): return lax.ppermute(a, ALL, [(i, i ^ mask) for i in range(devices)])]
    ppermute x0 -> x12, waiting for transfers between devices: none -> 17.1 us  [exchange(): return lax.ppermute(a, ALL, [(i, i ^ mask) for i in range(devices)])]
    dot_general x28 -> x0, matrix products: 16.2 us -> none  [the longest x1 1.34 us: segment_forward_sweep(): jnp.dot(xm, slice_wide_weights, preferred_element_type=jnp.float32)]
    pallas_call x0 -> x5, Pallas kernels: none -> 9.92 us  [the longest x1 3.69 us: local(): call(middle_kernel, [((owners // 2 * chunk + extra, width), BF16), ((owne...]
    unnamed x50 -> x18, local copies, waits for them, and re-layouts: 7.11 us -> 0.93 us
    mul x6 -> x0, local copies, waits for them, and re-layouts: 4.41 us -> none  [block_diagonal(): spread_out = unit_matrix[:, None, :, None] * parts[:, :, None, :]]
  transfers between devices with their start and end apart: 2 -> 12, of which waited for: 1 -> 11; matrix products, arithmetic and copies ran while one was open for 1% -> 0% of each run, Pallas kernels for 0% -> 5%
where the time goes in v1:
time: 47.8 us; the launch traced here: 47.6 us
  starting transfers between devices  18.3 us (38%)
  waiting for transfers between devices  17.1 us (36%)
  Pallas kernels  9.92 us (21%)
  local copies, waits for them, and re-layouts  1.02 us (2%)
  between operations  0.95 us (2%)
    ppermute x12, starting transfers between devices, exchange(): return lax.ppermute(a, ALL, [(i, i ^ mask) for i in range(devices)])  18.3 us
    ppermute x12, waiting for transfers between devices, exchange(): return lax.ppermute(a, ALL, [(i, i ^ mask) for i in range(devices)])  17.1 us
    pallas_call x1, Pallas kernels, local(): call(middle_kernel, [((owners // 2 * chunk + extra, width), BF16), ((owne...  3.69 us
    pallas_call x1, Pallas kernels, local(): call(points_kernel, [((token_rows, LANES), BF16)], 0, 7, scratch=[pltpu.S...  2.97 us
    pallas_call x1, Pallas kernels, local(): call(shadow_kernel, [((token_rows, LANES), BF16), ((width, points), BF16)...  1.46 us
    pallas_call x1, Pallas kernels, local(): call(features_kernel, [((points, width), BF16), (maps.shape, F32)], 0, 4)  1.12 us
  transfers between devices with their start and end apart: 12, of which 11 were waited for; matrix products, arithmetic and copies ran while one was open for 0% of the time, Pallas kernels for 5%

profile of v1, /device:TPU:0, one launch (start us, length us, event | category | flops | bytes accessed | tf_op | source)
XLA Modules:
  0.0 47.6 jit_solution(11206937293302202269)
XLA Ops:
  0.7 3.0 %shard_map.119.payload_in = bf16[272,128]{1,0:T(8,128)(2,1)} custom-call(s32[32]{0:T(128)} %tally.1, f32[8]{0:T(128)} %sharp.3, bf16[512,256]{1,0:T(8,128)(2,1)} %x.3, bf16[512,256]{1,0:T(8,128)(2,1)} %rc.3, bf16[256,256]{1,0:T(8,128)(2,1)} %entry.3, bf16[256,256]{1,0:T(8,128)(2,1)} %exit_.1, bf16[32,64]{1,0:T(8,128)(2,1)} %cluster.1), custom_call_target="tpu_custom_call" | custom-call | tf_op jit(solution)/shard_map/pallas_call | solution.py:424
  3.7 3.1 %collective-permute-start = (bf16[272,128]{1,0:T(8,128)(2,1)}, bf16[272,128]{1,0:T(8,128)(2,1)S(1)}, u32[]{:S(2)}, u32[]{:S(2)}) collective-permute-start(bf16[272,128]{1,0:T(8,128)(2,1)} %shard_map.119.payload_in), channel_id=1, source_target_pairs={{0,8},{1,9},{2,10},{3,11},{4,12},{5,13},{6,14},{7,15},{8,0},{9,1},... | collective-permute-start | bytes 208904 | tf_op jit(solution)/shard_map/ppermute | solution.py:404
  6.9 0.9 %copy-done.4 = bf16[272,128]{1,0:T(8,128)(2,1)S(1)} copy-done((bf16[272,128]{1,0:T(8,128)(2,1)S(1)}, bf16[272,128]{1,0:T(8,128)(2,1)}, u32[]{:S(2)}) %copy-start.4) | copy-done | bytes 69656
  7.7 1.5 %shard_map.120 = (bf16[272,128]{1,0:T(8,128)(2,1)S(1)}, bf16[256,512]{1,0:T(8,128)(2,1)S(1)}, bf16[256,512]{1,0:T(8,128)(2,1)S(1)}, bf16[512,512]{1,0:T(8,128)(2...) custom-call(s32[32]{0:T(128)S(1)} %copy-done.8, ...), custom_call_target="tpu_custom_call" | custom-call | tf_op jit(solution)/shard_map/pallas_call | solution.py:441
  9.4 3.1 %collective-permute-start.1 = (bf16[272,128]{1,0:T(8,128)(2,1)S(1)}, bf16[272,128]{1,0:T(8,128)(2,1)S(1)}, u32[]{:S(2)}, u32[]{:S(2)}) collective-permute-start(bf16[272,128]{1,0:T(8,128)(2,1)S(1)} %pad_maximum_fusion.5), channel_id=1, source_target_pairs={{0,16},{1,17},{2,18},{3,19},{4,20},{5,21},{6,22},{7,23},{8,24},{9,... | collective-permute-start | bytes 208904 | tf_op jit(solution)/shard_map/ppermute | solution.py:404
  12.5 2.3 %collective-permute-done.1 = bf16[272,128]{1,0:T(8,128)(2,1)S(1)} collective-permute-done((bf16[272,128]{1,0:T(8,128)(2,1)S(1)}, bf16[272,128]{1,0:T(8,128)(2,1)S(1)}, u32[]{:S(2)}, u32[]{:S(2)}) %collective-permute-start.1) | collective-permute-done | bytes 69664 | tf_op jit(solution)/shard_map/ppermute | solution.py:404
  14.8 1.9 %collective-permute-start.2 = (bf16[272,128]{1,0:T(8,128)(2,1)S(1)}, bf16[272,128]{1,0:T(8,128)(2,1)S(1)}, u32[]{:S(2)}, u32[]{:S(2)}) collective-permute-start(bf16[272,128]{1,0:T(8,128)(2,1)S(1)} %pad_maximum_fusion.6), channel_id=1, source_target_pairs={{0,4},{1,5},{2,6},{3,7},{4,0},{5,1},{6,2},{7,3},{8,12},{9,13},{10,... | collective-permute-start | bytes 208904 | tf_op jit(solution)/shard_map/ppermute | solution.py:404
  16.7 1.5 %collective-permute-start.3 = (bf16[272,128]{1,0:T(8,128)(2,1)S(1)}, bf16[272,128]{1,0:T(8,128)(2,1)S(1)}, u32[]{:S(2)}, u32[]{:S(2)}) collective-permute-start(bf16[272,128]{1,0:T(8,128)(2,1)S(1)} %pad_maximum_fusion.6), channel_id=1, source_target_pairs={{0,2},{1,3},{2,0},{3,1},{4,6},{5,7},{6,4},{7,5},{8,10},{9,11},{10,... | collective-permute-start | bytes 208904 | tf_op jit(solution)/shard_map/ppermute | solution.py:404
  18.4 1.2 %collective-permute-done.2 = bf16[272,128]{1,0:T(8,128)(2,1)S(1)} collective-permute-done((bf16[272,128]{1,0:T(8,128)(2,1)S(1)}, bf16[272,128]{1,0:T(8,128)(2,1)S(1)}, u32[]{:S(2)}, u32[]{:S(2)}) %collective-permute-start.2) | collective-permute-done | bytes 69664 | tf_op jit(solution)/shard_map/ppermute | solution.py:404
  19.6 1.4 %collective-permute-done.3 = bf16[272,128]{1,0:T(8,128)(2,1)S(1)} collective-permute-done((bf16[272,128]{1,0:T(8,128)(2,1)S(1)}, bf16[272,128]{1,0:T(8,128)(2,1)S(1)}, u32[]{:S(2)}, u32[]{:S(2)}) %collective-permute-start.3) | collective-permute-done | bytes 69664 | tf_op jit(solution)/shard_map/ppermute | solution.py:404
  21.0 2.4 %collective-permute-done.4 = bf16[272,128]{1,0:T(8,128)(2,1)S(1)} collective-permute-done((bf16[272,128]{1,0:T(8,128)(2,1)S(1)}, bf16[272,128]{1,0:T(8,128)(2,1)S(1)}, u32[]{:S(2)}, u32[]{:S(2)}) %collective-permute-start.4) | collective-permute-done | bytes 69664 | tf_op jit(solution)/shard_map/ppermute | solution.py:404
  23.6 1.2 %collective-permute-done.5.other = bf16[272,128]{1,0:T(8,128)(2,1)S(1)} collective-permute-done((bf16[272,128]{1,0:T(8,128)(2,1)S(1)}, bf16[272,128]{1,0:T(8,128)(2,1)S(1)}, u32[]{:S(2)}, u32[]{:S(2)}) %collective-permute-start.5) | collective-permute-done | bytes 69664 | tf_op jit(solution)/shard_map/ppermute | solution.py:404
  24.8 3.7 %shard_map.121 = (bf16[288,256]{1,0:T(8,128)(2,1)S(1)}, bf16[288,256]{1,0:T(8,128)(2,1)S(1)}, bf16[256,512]{1,0:T(8,128)(2,1)S(1)}, f32[128,128]{1,0:T(8,128)S(1)}, f32[128,384]{1,0:T(8,128)S(1)}) custom-call(f32[8]{0:T(128)S(1)} %copy-done.7, bf16[272,128]{1,0:T(8,128)(2,1)S(1)} %pad_maximum_fusion.7.mine, ...), custom_call_target="tpu_custom_call" | custom-call | tf_op jit(solution)/shard_map/pallas_call | solution.py:471
  28.8 1.2 %collective-permute-done.6 = bf16[288,256]{1,0:T(8,128)(2,1)S(1)} collective-permute-done((bf16[288,256]{1,0:T(8,128)(2,1)S(1)}, bf16[288,256]{1,0:T(8,128)(2,1)S(1)}, u32[]{:S(2)}, u32[]{:S(2)}) %collective-permute-start.6) | collective-permute-done | bytes 147488 | tf_op jit(solution)/shard_map/ppermute | solution.py:404
  30.1 0.6 %collective-permute-start.7 = (bf16[160,256]{1,0:T(8,128)(2,1)S(1)}, bf16[160,256]{1,0:T(8,128)(2,1)S(1)}, u32[]{:S(2)}, u32[]{:S(2)}) collective-permute-start(bf16[160,256]{1,0:T(8,128)(2,1)S(1)} %get-tuple-element.55), channel_id=1, source_target_pairs={{0,4},{1,5},{2,6},{3,7},{4,0},{5,1},{6,2},{7,3},{8,12},{9,13},{10,... | collective-permute-start | bytes 245768 | tf_op jit(solution)/shard_map/ppermute | solution.py:404
  30.9 2.8 %collective-permute-start.9 = (bf16[160,256]{1,0:T(8,128)(2,1)S(1)}, bf16[160,256]{1,0:T(8,128)(2,1)S(1)}, u32[]{:S(2)}, u32[]{:S(2)}) collective-permute-start(bf16[160,256]{1,0:T(8,128)(2,1)S(1)} %get-tuple-element.56), channel_id=1, source_target_pairs={{0,6},{1,7},{2,4},{3,5},{4,2},{5,3},{6,0},{7,1},{8,14},{9,15},{10,... | collective-permute-start | bytes 245768 | tf_op jit(solution)/shard_map/ppermute | solution.py:404
  33.7 1.4 %collective-permute-done.7 = bf16[160,256]{1,0:T(8,128)(2,1)S(1)} collective-permute-done((bf16[160,256]{1,0:T(8,128)(2,1)S(1)}, bf16[160,256]{1,0:T(8,128)(2,1)S(1)}, u32[]{:S(2)}, u32[]{:S(2)}) %collective-permute-start.7) | collective-permute-done | bytes 81952 | tf_op jit(solution)/shard_map/ppermute | solution.py:404
  35.1 1.7 %collective-permute-done.8 = bf16[160,256]{1,0:T(8,128)(2,1)S(1)} collective-permute-done((bf16[160,256]{1,0:T(8,128)(2,1)S(1)}, bf16[160,256]{1,0:T(8,128)(2,1)S(1)}, u32[]{:S(2)}, u32[]{:S(2)}) %collective-permute-start.8) | collective-permute-done | bytes 81952 | tf_op jit(solution)/shard_map/ppermute | solution.py:404
  36.9 1.8 %collective-permute-start.10 = (bf16[160,256]{1,0:T(8,128)(2,1)S(1)}, bf16[160,256]{1,0:T(8,128)(2,1)S(1)}, u32[]{:S(2)}, u32[]{:S(2)}) collective-permute-start(bf16[160,256]{1,0:T(8,128)(2,1)S(1)} %pad_maximum_fusion.3), channel_id=1, source_target_pairs={{0,8},{1,9},{2,10},{3,11},{4,12},{5,13},{6,14},{7,15},{8,0},{9,1},... | collective-permute-start | bytes 245768 | tf_op jit(solution)/shard_map/ppermute | solution.py:404
  38.7 2.8 %collective-permute-done.10 = bf16[160,256]{1,0:T(8,128)(2,1)S(1)} collective-permute-done((bf16[160,256]{1,0:T(8,128)(2,1)S(1)}, bf16[160,256]{1,0:T(8,128)(2,1)S(1)}, u32[]{:S(2)}, u32[]{:S(2)}) %collective-permute-start.10) | collective-permute-done | bytes 81952 | tf_op jit(solution)/shard_map/ppermute | solution.py:404
  41.5 3.0 %collective-permute-start.11 = (bf16[160,256]{1,0:T(8,128)(2,1)S(1)}, bf16[160,256]{1,0:T(8,128)(2,1)S(1)}, u32[]{:S(2)}, u32[]{:S(2)}) collective-permute-start(bf16[160,256]{1,0:T(8,128)(2,1)S(1)} %pad_maximum_fusion.4.mine), channel_id=1, source_target_pairs={{0,16},{1,17},{2,18},{3,19},{4,20},{5,21},{6,22},{7,23},{8,24},{9,... | collective-permute-start | bytes 245768 | tf_op jit(solution)/shard_map/ppermute | solution.py:404
  44.5 1.1 %shard_map.122 = (bf16[512,256]{1,0:T(8,128)(2,1)}, f32[3,32,32]{2,1,0:T(8,128)}) custom-call(bf16[256,512]{1,0:T(8,128)(2,1)S(1)} %get-tuple-element.31.gxmt, bf16[256,256]{1,0:T(8,128)(2,1)S(1)} %copy-done.2, f32[128,128]{1,0:T(8,128)S(1)} %get-tuple-element.32.tokens, f32[128,384]{1,0:T(8,128)S(1)} %get-tuple-element.33.grads), custom_call_target="tpu_custom_call" | custom-call | tf_op jit(solution)/shard_map/pallas_call | solution.py:499
  45.6 1.3 %collective-permute-done.11.other = bf16[160,256]{1,0:T(8,128)(2,1)S(1)} collective-permute-done((bf16[160,256]{1,0:T(8,128)(2,1)S(1)}, bf16[160,256]{1,0:T(8,128)(2,1)S(1)}, u32[]{:S(2)}, u32[]{:S(2)}) %collective-permute-start.11) | collective-permute-done | bytes 81952 | tf_op jit(solution)/shard_map/ppermute | solution.py:404
  46.9 0.7 %shard_map.123 = (f32[2,64,256]{2,1,0:T(8,128)}, f32[32,64]{1,0:T(8,128)}, f32[1,8]{1,0:T(1,128)}) custom-call(bf16[160,256]{1,0:T(8,128)(2,1)S(1)} %pad_maximum_fusion.4.mine, bf16[160,256]{1,0:T(8,128)(2,1)S(1)} %collective-permute-done.11.other), custom_call_target="tpu_custom_call" | custom-call | tf_op jit(solution)/shard_map/pallas_call | solution.py:525
  (50 shorter events, 1.1 us)
Async XLA Ops:
  0.6 6.2 %copy-start.2 = (bf16[256,256]{1,0:T(8,128)(2,1)S(1)}, bf16[256,256]{1,0:T(8,128)(2,1)}, u32[]{:S(2)}) copy-start(bf16[256,256]{1,0:T(8,128)(2,1)} %entry.3) | copy-start | bytes 393220
  0.6 6.1 %copy-start.3 = (bf16[256,256]{1,0:T(8,128)(2,1)S(1)}, bf16[256,256]{1,0:T(8,128)(2,1)}, u32[]{:S(2)}) copy-start(bf16[256,256]{1,0:T(8,128)(2,1)} %exit_.1) | copy-start | bytes 393220
  0.7 6.1 %copy-start.6 = (bf16[32,64]{1,0:T(8,128)(2,1)S(1)}, bf16[32,64]{1,0:T(8,128)(2,1)}, u32[]{:S(2)}) copy-start(bf16[32,64]{1,0:T(8,128)(2,1)} %cluster.1) | copy-start | bytes 12292
  0.7 6.1 %copy-start.7 = (f32[8]{0:T(128)S(1)}, f32[8]{0:T(128)}, u32[]{:S(2)}) copy-start(f32[8]{0:T(128)} %sharp.3) | copy-start | bytes 100
  0.7 6.1 %copy-start.8 = (s32[32]{0:T(128)S(1)}, s32[32]{0:T(128)}, u32[]{:S(2)}) copy-start(s32[32]{0:T(128)} %tally.1) | copy-start | bytes 388
  0.7 6.1 %copy-start = (bf16[512,256]{1,0:T(8,128)(2,1)S(1)}, bf16[512,256]{1,0:T(8,128)(2,1)}, u32[]{:S(2)}) copy-start(bf16[512,256]{1,0:T(8,128)(2,1)} %x.3) | copy-start | bytes 786436
  0.7 6.1 %copy-start.1 = (bf16[512,256]{1,0:T(8,128)(2,1)S(1)}, bf16[512,256]{1,0:T(8,128)(2,1)}, u32[]{:S(2)}) copy-start(bf16[512,256]{1,0:T(8,128)(2,1)} %rc.3) | copy-start | bytes 786436
  0.7 6.1 %copy-start.5 = (f32[3,32,32]{2,1,0:T(8,128)S(1)}, f32[3,32,32]{2,1,0:T(8,128)}, u32[]{:S(2)}) copy-start(f32[3,32,32]{2,1,0:T(8,128)} %maps.1) | copy-start | bytes 36868
  3.7 5.6 %collective-permute-start = (bf16[272,128]{1,0:T(8,128)(2,1)}, bf16[272,128]{1,0:T(8,128)(2,1)S(1)}, u32[]{:S(2)}, u32[]{:S(2)}) collective-permute-start(bf16[272,128]{1,0:T(8,128)(2,1)} %shard_map.119.payload_in), channel_id=1, source_target_pairs={{0,8},{1,9},{2,10},{3,11},{4,12},{5,13},{6,14},{7,15},{8,0},{9,1},... | collective-permute-start | bytes 208904 | tf_op jit(solution)/shard_map/ppermute | solution.py:404
  6.8 0.9 %copy-start.4 = (bf16[272,128]{1,0:T(8,128)(2,1)S(1)}, bf16[272,128]{1,0:T(8,128)(2,1)}, u32[]{:S(2)}) copy-start(bf16[272,128]{1,0:T(8,128)(2,1)} %shard_map.119.payload_in) | copy-start | bytes 208900
  9.4 5.4 %collective-permute-start.1 = (bf16[272,128]{1,0:T(8,128)(2,1)S(1)}, bf16[272,128]{1,0:T(8,128)(2,1)S(1)}, u32[]{:S(2)}, u32[]{:S(2)}) collective-permute-start(bf16[272,128]{1,0:T(8,128)(2,1)S(1)} %pad_maximum_fusion.5), channel_id=1, source_target_pairs={{0,16},{1,17},{2,18},{3,19},{4,20},{5,21},{6,22},{7,23},{8,24},{9,... | collective-permute-start | bytes 208904 | tf_op jit(solution)/shard_map/ppermute | solution.py:404
  14.8 4.8 %collective-permute-start.2 = (bf16[272,128]{1,0:T(8,128)(2,1)S(1)}, bf16[272,128]{1,0:T(8,128)(2,1)S(1)}, u32[]{:S(2)}, u32[]{:S(2)}) collective-permute-start(bf16[272,128]{1,0:T(8,128)(2,1)S(1)} %pad_maximum_fusion.6), channel_id=1, source_target_pairs={{0,4},{1,5},{2,6},{3,7},{4,0},{5,1},{6,2},{7,3},{8,12},{9,13},{10,... | collective-permute-start | bytes 208904 | tf_op jit(solution)/shard_map/ppermute | solution.py:404
  16.7 4.3 %collective-permute-start.3 = (bf16[272,128]{1,0:T(8,128)(2,1)S(1)}, bf16[272,128]{1,0:T(8,128)(2,1)S(1)}, u32[]{:S(2)}, u32[]{:S(2)}) collective-permute-start(bf16[272,128]{1,0:T(8,128)(2,1)S(1)} %pad_maximum_fusion.6), channel_id=1, source_target_pairs={{0,2},{1,3},{2,0},{3,1},{4,6},{5,7},{6,4},{7,5},{8,10},{9,11},{10,... | collective-permute-start | bytes 208904 | tf_op jit(solution)/shard_map/ppermute | solution.py:404
  18.2 5.2 %collective-permute-start.4 = (bf16[272,128]{1,0:T(8,128)(2,1)S(1)}, bf16[272,128]{1,0:T(8,128)(2,1)S(1)}, u32[]{:S(2)}, u32[]{:S(2)}) collective-permute-start(bf16[272,128]{1,0:T(8,128)(2,1)S(1)} %pad_maximum_fusion.6), channel_id=1, source_target_pairs={{0,6},{1,7},{2,4},{3,5},{4,2},{5,3},{6,0},{7,1},{8,14},{9,15},{10,... | collective-permute-start | bytes 208904 | tf_op jit(solution)/shard_map/ppermute | solution.py:404
  23.5 1.3 %collective-permute-start.5 = (bf16[272,128]{1,0:T(8,128)(2,1)S(1)}, bf16[272,128]{1,0:T(8,128)(2,1)S(1)}, u32[]{:S(2)}, u32[]{:S(2)}) collective-permute-start(bf16[272,128]{1,0:T(8,128)(2,1)S(1)} %pad_maximum_fusion.7.mine), channel_id=1, source_target_pairs={{0,1},{1,0},{2,3},{3,2},{4,5},{5,4},{6,7},{7,6},{8,9},{9,8},{10,11... | collective-permute-start | bytes 208904 | tf_op jit(solution)/shard_map/ppermute | solution.py:404
  28.5 1.4 %collective-permute-start.6 = (bf16[288,256]{1,0:T(8,128)(2,1)S(1)}, bf16[288,256]{1,0:T(8,128)(2,1)S(1)}, u32[]{:S(2)}, u32[]{:S(2)}) collective-permute-start(bf16[288,256]{1,0:T(8,128)(2,1)S(1)} %get-tuple-element.36), channel_id=1, source_target_pairs={{0,1},{1,0},{2,3},{3,2},{4,5},{5,4},{6,7},{7,6},{8,9},{9,8},{10,11... | collective-permute-start | bytes 442376 | tf_op jit(solution)/shard_map/ppermute | solution.py:404
  30.1 4.9 %collective-permute-start.7 = (bf16[160,256]{1,0:T(8,128)(2,1)S(1)}, bf16[160,256]{1,0:T(8,128)(2,1)S(1)}, u32[]{:S(2)}, u32[]{:S(2)}) collective-permute-start(bf16[160,256]{1,0:T(8,128)(2,1)S(1)} %get-tuple-element.55), channel_id=1, source_target_pairs={{0,4},{1,5},{2,6},{3,7},{4,0},{5,1},{6,2},{7,3},{8,12},{9,13},{10,... | collective-permute-start | bytes 245768 | tf_op jit(solution)/shard_map/ppermute | solution.py:404
  30.7 6.1 %collective-permute-start.8 = (bf16[160,256]{1,0:T(8,128)(2,1)S(1)}, bf16[160,256]{1,0:T(8,128)(2,1)S(1)}, u32[]{:S(2)}, u32[]{:S(2)}) collective-permute-start(bf16[160,256]{1,0:T(8,128)(2,1)S(1)} %get-tuple-element.56), channel_id=1, source_target_pairs={{0,2},{1,3},{2,0},{3,1},{4,6},{5,7},{6,4},{7,5},{8,10},{9,11},{10,... | collective-permute-start | bytes 245768 | tf_op jit(solution)/shard_map/ppermute | solution.py:404
  30.9 5.9 %collective-permute-start.9 = (bf16[160,256]{1,0:T(8,128)(2,1)S(1)}, bf16[160,256]{1,0:T(8,128)(2,1)S(1)}, u32[]{:S(2)}, u32[]{:S(2)}) collective-permute-start(bf16[160,256]{1,0:T(8,128)(2,1)S(1)} %get-tuple-element.56), channel_id=1, source_target_pairs={{0,6},{1,7},{2,4},{3,5},{4,2},{5,3},{6,0},{7,1},{8,14},{9,15},{10,... | collective-permute-start | bytes 245768 | tf_op jit(solution)/shard_map/ppermute | solution.py:404
  36.9 4.5 %collective-permute-start.10 = (bf16[160,256]{1,0:T(8,128)(2,1)S(1)}, bf16[160,256]{1,0:T(8,128)(2,1)S(1)}, u32[]{:S(2)}, u32[]{:S(2)}) collective-permute-start(bf16[160,256]{1,0:T(8,128)(2,1)S(1)} %pad_maximum_fusion.3), channel_id=1, source_target_pairs={{0,8},{1,9},{2,10},{3,11},{4,12},{5,13},{6,14},{7,15},{8,0},{9,1},... | collective-permute-start | bytes 245768 | tf_op jit(solution)/shard_map/ppermute | solution.py:404
  41.5 5.4 %collective-permute-start.11 = (bf16[160,256]{1,0:T(8,128)(2,1)S(1)}, bf16[160,256]{1,0:T(8,128)(2,1)S(1)}, u32[]{:S(2)}, u32[]{:S(2)}) collective-permute-start(bf16[160,256]{1,0:T(8,128)(2,1)S(1)} %pad_maximum_fusion.4.mine), channel_id=1, source_target_pairs={{0,16},{1,17},{2,18},{3,19},{4,20},{5,21},{6,22},{7,23},{8,24},{9,... | collective-permute-start | bytes 245768 | tf_op jit(solution)/shard_map/ppermute | solution.py:404

commit v2 on v1

--- a/solution.py
+++ b/solution.py
@@ -1,3 +1,5 @@
+import math
+
 import jax
 import jax.numpy as jnp
 from jax import lax
@@ -404,6 +406,33 @@
     return lax.ppermute(a, ALL, [(i, i ^ mask) for i in range(devices)])
 
 
+def exchanges(a, masks):
+    return [exchange(a, mask) for mask in masks]
+
+
+def gather(mine, others):
+    mine, others = mine.astype(F32), [a.astype(F32) for a in others]
+    if len(others) == 1:
+        return mine + others[0]
+    return (mine + others[0]) + (others[1] + others[2])
+
+
+def token_pack(values, start, root_scale, den_scale):
+    sums, pair = values[:start], values[start:]
+    n = pair.shape[0] // 2
+    pair = (pair[:n] + pair[n:]) * den_scale
+    high = lax.reduce_precision(pair, 8, 7)
+    roots = jnp.sqrt(jnp.abs(sums)) * root_scale
+    roots = jnp.where(sums < 0.0, -roots, roots)
+    return jnp.concatenate([roots, high, pair - high], axis=0).astype(jnp.float16)
+
+
+def token_unpack(packed, start, root_scale, den_scale):
+    packed = packed.astype(F32)
+    row = lax.broadcasted_iota(jnp.int32, packed.shape, 0)
+    return packed * jnp.where(row < start, jnp.abs(packed) * root_scale**-2, 1.0 / den_scale)
+
+
 def halves(total, start):
     pair = total[start:]
     n = pair.shape[0] // 2
@@ -421,6 +450,7 @@
     per = LANES // head
     rows = heads // per * slices
     token_rows = 2 * rows + 2 * heads
+    far = [1 << bit for bit in range(4, devices.bit_length() - 1)]
     (payload,) = call(
         points_kernel,
         [((token_rows, LANES), BF16)],
@@ -437,7 +467,11 @@
         space=pltpu.HBM,
         limit=POINTS_LIMIT,
     )(tally, sharp, x, rc, entry, exit_, cluster)
-    other = exchange(payload, 8)
+    steps = ((8,), *((mask,) for mask in far), (2, 4, 6), (1,))
+    all_points = devices * points
+    root_scale = 2.0 ** math.floor(math.log2(65000.0 / math.sqrt(all_points * width * 2.25)))
+    den_scale = 2.0 ** -max(0, math.ceil(math.log2(all_points / 2.0**15)))
+    others = exchanges(payload, steps[0])
     mine, xmt, got, weights, live_probs, maps_high, maps_low, cluster_rows = call(
         shadow_kernel,
         [
@@ -453,17 +487,16 @@
         2,
         9,
     )(tally, sharp, x, rc, entry, exit_, cluster, maps, payload)
-    mine = halves(mine.astype(F32) + other.astype(F32), 2 * rows)
-    mask = 16
-    while mask < devices:
-        other = exchange(mine, mask)
-        mine = halves(mine.astype(F32) + other.astype(F32), 2 * rows)
-        mask *= 2
-    far, b, a = exchange(mine, 6), exchange(mine, 2), exchange(mine, 4)
-    mine = halves(
-        (mine.astype(F32) + a.astype(F32)) + (b.astype(F32) + far.astype(F32)), 2 * rows
-    )
-    other = exchange(mine, 1)
+    total = gather(mine, others)
+    for masks in steps[1:-1]:
+        mine = token_pack(total, 2 * rows, root_scale, den_scale)
+        others = exchanges(mine, masks)
+        mine, *others = (
+            token_unpack(a, 2 * rows, root_scale, den_scale) for a in (mine, *others)
+        )
+        total = gather(mine, others)
+    mine = total
+    (other,) = exchanges(mine, steps[-1])
 
     owner_rows = width // owners
     chunk = 2 * owner_rows
@@ -512,16 +545,13 @@
     theirs = jnp.concatenate(
         [lax.dynamic_slice_in_dim(total, (1 - half) * chunk, chunk), common], axis=0
     )
-    far, b, a = exchange(theirs, 6), exchange(theirs, 2), exchange(mine, 4)
-    total = (mine.astype(F32) + a.astype(F32)) + (b.astype(F32) + far.astype(F32))
+    others = [exchange(mine, 4), exchange(theirs, 2), exchange(theirs, 6)]
+    total = gather(mine, others)
     mine = halves(total, total.shape[0] - 2 * heads)
-    mask = 8
-    while 2 * mask < devices:
-        other = exchange(mine, mask)
-        total = mine.astype(F32) + other.astype(F32)
+    for mask in (8, *far[:-1]):
+        total = gather(mine, exchanges(mine, (mask,)))
         mine = halves(total, total.shape[0] - 2 * heads)
-        mask *= 2
-    other = exchange(mine, mask)
+    other = exchange(mine, far[-1])
     weight_grads, slice_grad, temp_grad = call(
         finish_kernel,
         [

time: 47.8 us -> 48.3 us (1.010)
  waiting for transfers between devices: 17.1 us -> 17.6 us
where the time goes in v2:
time: 48.3 us; the launch traced here: 48.1 us
  starting transfers between devices  18.1 us (37%)
  waiting for transfers between devices  17.6 us (36%)
  Pallas kernels  9.91 us (21%)
  local copies, waits for them, and re-layouts  0.99 us (2%)
  between operations  0.93 us (2%)
  other arithmetic  0.67 us (1%)
    ppermute x12, starting transfers between devices, exchange(): return lax.ppermute(a, ALL, [(i, i ^ mask) for i in range(devices)])  18.1 us
    ppermute x12, waiting for transfers between devices, exchange(): return lax.ppermute(a, ALL, [(i, i ^ mask) for i in range(devices)])  17.6 us
    pallas_call x1, Pallas kernels, local(): call(middle_kernel, [((owners // 2 * chunk + extra, width), BF16), ((owne...  3.69 us
    pallas_call x1, Pallas kernels, local(): call(points_kernel, [((token_rows, LANES), BF16)], 0, 7, scratch=[pltpu.S...  2.97 us
    pallas_call x1, Pallas kernels, local(): call(shadow_kernel, [((token_rows, LANES), BF16), ((width, points), BF16)...  1.46 us
    pallas_call x1, Pallas kernels, local(): call(features_kernel, [((points, width), BF16), (maps.shape, F32)], 0, 4)  1.12 us
  transfers between devices with their start and end apart: 12, of which 11 were waited for; matrix products, arithmetic and copies ran while one was open for 0% of the time, Pallas kernels for 5%

profile of v2, /device:TPU:0, one launch (start us, length us, event | category | flops | bytes accessed | tf_op | source)
XLA Modules:
  0.0 48.1 jit_solution(753303469000645442)
XLA Ops:
  0.7 3.0 %shard_map.119.payload_in = bf16[272,128]{1,0:T(8,128)(2,1)} custom-call(s32[32]{0:T(128)} %tally.1, f32[8]{0:T(128)} %sharp.3, bf16[512,256]{1,0:T(8,128)(2,1)} %x.3, bf16[512,256]{1,0:T(8,128)(2,1)} %rc.3, bf16[256,256]{1,0:T(8,128)(2,1)} %entry.3, bf16[256,256]{1,0:T(8,128)(2,1)} %exit_.1, bf16[32,64]{1,0:T(8,128)(2,1)} %cluster.1), custom_call_target="tpu_custom_call" | custom-call | tf_op jit(solution)/shard_map/pallas_call | solution.py:454
  3.7 3.1 %collective-permute-start = (bf16[272,128]{1,0:T(8,128)(2,1)}, bf16[272,128]{1,0:T(8,128)(2,1)S(1)}, u32[]{:S(2)}, u32[]{:S(2)}) collective-permute-start(bf16[272,128]{1,0:T(8,128)(2,1)} %shard_map.119.payload_in), channel_id=1, source_target_pairs={{0,8},{1,9},{2,10},{3,11},{4,12},{5,13},{6,14},{7,15},{8,0},{9,1},... | collective-permute-start | bytes 208904 | tf_op jit(solution)/shard_map/ppermute | solution.py:406
  6.9 0.9 %copy-done.4 = bf16[272,128]{1,0:T(8,128)(2,1)S(1)} copy-done((bf16[272,128]{1,0:T(8,128)(2,1)S(1)}, bf16[272,128]{1,0:T(8,128)(2,1)}, u32[]{:S(2)}) %copy-start.4) | copy-done | bytes 69656
  7.7 1.5 %shard_map.120 = (bf16[272,128]{1,0:T(8,128)(2,1)S(1)}, bf16[256,512]{1,0:T(8,128)(2,1)S(1)}, bf16[256,512]{1,0:T(8,128)(2,1)S(1)}, bf16[512,512]{1,0:T(8,128)(2...) custom-call(s32[32]{0:T(128)S(1)} %copy-done.8, ...), custom_call_target="tpu_custom_call" | custom-call | tf_op jit(solution)/shard_map/pallas_call | solution.py:475
  9.4 3.1 %collective-permute-start.1 = (f16[272,128]{1,0:T(8,128)(2,1)S(1)}, f16[272,128]{1,0:T(8,128)(2,1)S(1)}, u32[]{:S(2)}, u32[]{:S(2)}) collective-permute-start(f16[272,128]{1,0:T(8,128)(2,1)S(1)} %pad_maximum_fusion.5), channel_id=1, source_target_pairs={{0,16},{1,17},{2,18},{3,19},{4,20},{5,21},{6,22},{7,23},{8,24},{9,... | collective-permute-start | bytes 208904 | tf_op jit(solution)/shard_map/ppermute | solution.py:406
  12.5 2.3 %collective-permute-done.1 = f16[272,128]{1,0:T(8,128)(2,1)S(1)} collective-permute-done((f16[272,128]{1,0:T(8,128)(2,1)S(1)}, f16[272,128]{1,0:T(8,128)(2,1)S(1)}, u32[]{:S(2)}, u32[]{:S(2)}) %collective-permute-start.1) | collective-permute-done | bytes 69664 | tf_op jit(solution)/shard_map/ppermute | solution.py:406
  15.1 1.9 %collective-permute-start.2 = (f16[272,128]{1,0:T(8,128)(2,1)S(1)}, f16[272,128]{1,0:T(8,128)(2,1)S(1)}, u32[]{:S(2)}, u32[]{:S(2)}) collective-permute-start(f16[272,128]{1,0:T(8,128)(2,1)S(1)} %pad_maximum_fusion.6), channel_id=1, source_target_pairs={{0,2},{1,3},{2,0},{3,1},{4,6},{5,7},{6,4},{7,5},{8,10},{9,11},{10,... | collective-permute-start | bytes 208904 | tf_op jit(solution)/shard_map/ppermute | solution.py:406
  17.0 1.5 %collective-permute-start.3 = (f16[272,128]{1,0:T(8,128)(2,1)S(1)}, f16[272,128]{1,0:T(8,128)(2,1)S(1)}, u32[]{:S(2)}, u32[]{:S(2)}) collective-permute-start(f16[272,128]{1,0:T(8,128)(2,1)S(1)} %pad_maximum_fusion.6), channel_id=1, source_target_pairs={{0,4},{1,5},{2,6},{3,7},{4,0},{5,1},{6,2},{7,3},{8,12},{9,13},{10,... | collective-permute-start | bytes 208904 | tf_op jit(solution)/shard_map/ppermute | solution.py:406
  18.6 1.6 %collective-permute-done.2 = f16[272,128]{1,0:T(8,128)(2,1)S(1)} collective-permute-done((f16[272,128]{1,0:T(8,128)(2,1)S(1)}, f16[272,128]{1,0:T(8,128)(2,1)S(1)}, u32[]{:S(2)}, u32[]{:S(2)}) %collective-permute-start.2) | collective-permute-done | bytes 69664 | tf_op jit(solution)/shard_map/ppermute | solution.py:406
  20.2 1.1 %collective-permute-done.3 = f16[272,128]{1,0:T(8,128)(2,1)S(1)} collective-permute-done((f16[272,128]{1,0:T(8,128)(2,1)S(1)}, f16[272,128]{1,0:T(8,128)(2,1)S(1)}, u32[]{:S(2)}, u32[]{:S(2)}) %collective-permute-start.3) | collective-permute-done | bytes 69664 | tf_op jit(solution)/shard_map/ppermute | solution.py:406
  21.3 2.4 %collective-permute-done.4 = f16[272,128]{1,0:T(8,128)(2,1)S(1)} collective-permute-done((f16[272,128]{1,0:T(8,128)(2,1)S(1)}, f16[272,128]{1,0:T(8,128)(2,1)S(1)}, u32[]{:S(2)}, u32[]{:S(2)}) %collective-permute-start.4) | collective-permute-done | bytes 69664 | tf_op jit(solution)/shard_map/ppermute | solution.py:406
  23.9 1.3 %collective-permute-done.5.other = f32[272,128]{1,0:T(8,128)S(1)} collective-permute-done((f32[272,128]{1,0:T(8,128)S(1)}, f32[272,128]{1,0:T(8,128)S(1)}, u32[]{:S(2)}, u32[]{:S(2)}) %collective-permute-start.5) | collective-permute-done | bytes 139296 | tf_op jit(solution)/shard_map/ppermute | solution.py:406
  25.3 3.7 %shard_map.121 = (bf16[288,256]{1,0:T(8,128)(2,1)S(1)}, bf16[288,256]{1,0:T(8,128)(2,1)S(1)}, bf16[256,512]{1,0:T(8,128)(2,1)S(1)}, f32[128,128]{1,0:T(8,128)S(1)}, f32[128,384]{1,0:T(8,128)S(1)}) custom-call(f32[8]{0:T(128)S(1)} %copy-done.7, f32[272,128]{1,0:T(8,128)S(1)} %fusion.8.mine, f32[272,128]{1,0:T(8,128)S(1)} %collective-permute-done.5.other, ...), custom_call_target="tpu_custom_call" | custom-call | tf_op jit(solution)/shard_map/pallas_call | solution.py:504
  29.2 1.2 %collective-permute-done.6 = bf16[288,256]{1,0:T(8,128)(2,1)S(1)} collective-permute-done((bf16[288,256]{1,0:T(8,128)(2,1)S(1)}, bf16[288,256]{1,0:T(8,128)(2,1)S(1)}, u32[]{:S(2)}, u32[]{:S(2)}) %collective-permute-start.6) | collective-permute-done | bytes 147488 | tf_op jit(solution)/shard_map/ppermute | solution.py:406
  31.2 0.8 %collective-permute-start.8 = (bf16[160,256]{1,0:T(8,128)(2,1)S(1)}, bf16[160,256]{1,0:T(8,128)(2,1)S(1)}, u32[]{:S(2)}, u32[]{:S(2)}) collective-permute-start(bf16[160,256]{1,0:T(8,128)(2,1)S(1)} %get-tuple-element.54), channel_id=1, source_target_pairs={{0,2},{1,3},{2,0},{3,1},{4,6},{5,7},{6,4},{7,5},{8,10},{9,11},{10,... | collective-permute-start | bytes 245768 | tf_op jit(solution)/shard_map/ppermute | solution.py:406
  31.9 2.2 %collective-permute-start.9 = (bf16[160,256]{1,0:T(8,128)(2,1)S(1)}, bf16[160,256]{1,0:T(8,128)(2,1)S(1)}, u32[]{:S(2)}, u32[]{:S(2)}) collective-permute-start(bf16[160,256]{1,0:T(8,128)(2,1)S(1)} %get-tuple-element.54), channel_id=1, source_target_pairs={{0,6},{1,7},{2,4},{3,5},{4,2},{5,3},{6,0},{7,1},{8,14},{9,15},{10,... | collective-permute-start | bytes 245768 | tf_op jit(solution)/shard_map/ppermute | solution.py:406
  34.1 1.4 %collective-permute-done.7 = bf16[160,256]{1,0:T(8,128)(2,1)S(1)} collective-permute-done((bf16[160,256]{1,0:T(8,128)(2,1)S(1)}, bf16[160,256]{1,0:T(8,128)(2,1)S(1)}, u32[]{:S(2)}, u32[]{:S(2)}) %collective-permute-start.7) | collective-permute-done | bytes 81952 | tf_op jit(solution)/shard_map/ppermute | solution.py:406
  35.5 1.9 %collective-permute-done.8 = bf16[160,256]{1,0:T(8,128)(2,1)S(1)} collective-permute-done((bf16[160,256]{1,0:T(8,128)(2,1)S(1)}, bf16[160,256]{1,0:T(8,128)(2,1)S(1)}, u32[]{:S(2)}, u32[]{:S(2)}) %collective-permute-start.8) | collective-permute-done | bytes 81952 | tf_op jit(solution)/shard_map/ppermute | solution.py:406
  37.5 1.6 %collective-permute-start.10 = (bf16[160,256]{1,0:T(8,128)(2,1)S(1)}, bf16[160,256]{1,0:T(8,128)(2,1)S(1)}, u32[]{:S(2)}, u32[]{:S(2)}) collective-permute-start(bf16[160,256]{1,0:T(8,128)(2,1)S(1)} %pad_maximum_fusion.3), channel_id=1, source_target_pairs={{0,8},{1,9},{2,10},{3,11},{4,12},{5,13},{6,14},{7,15},{8,0},{9,1},... | collective-permute-start | bytes 245768 | tf_op jit(solution)/shard_map/ppermute | solution.py:406
  39.1 2.9 %collective-permute-done.10 = bf16[160,256]{1,0:T(8,128)(2,1)S(1)} collective-permute-done((bf16[160,256]{1,0:T(8,128)(2,1)S(1)}, bf16[160,256]{1,0:T(8,128)(2,1)S(1)}, u32[]{:S(2)}, u32[]{:S(2)}) %collective-permute-start.10) | collective-permute-done | bytes 81952 | tf_op jit(solution)/shard_map/ppermute | solution.py:406
  42.0 2.8 %collective-permute-start.11 = (bf16[160,256]{1,0:T(8,128)(2,1)S(1)}, bf16[160,256]{1,0:T(8,128)(2,1)S(1)}, u32[]{:S(2)}, u32[]{:S(2)}) collective-permute-start(bf16[160,256]{1,0:T(8,128)(2,1)S(1)} %pad_maximum_fusion.4.mine), channel_id=1, source_target_pairs={{0,16},{1,17},{2,18},{3,19},{4,20},{5,21},{6,22},{7,23},{8,24},{9,... | collective-permute-start | bytes 245768 | tf_op jit(solution)/shard_map/ppermute | solution.py:406
  44.9 1.1 %shard_map.122 = (bf16[512,256]{1,0:T(8,128)(2,1)}, f32[3,32,32]{2,1,0:T(8,128)}) custom-call(bf16[256,512]{1,0:T(8,128)(2,1)S(1)} %get-tuple-element.31.gxmt, bf16[256,256]{1,0:T(8,128)(2,1)S(1)} %copy-done.2, f32[128,128]{1,0:T(8,128)S(1)} %get-tuple-element.32.tokens, f32[128,384]{1,0:T(8,128)S(1)} %get-tuple-element.33.grads), custom_call_target="tpu_custom_call" | custom-call | tf_op jit(solution)/shard_map/pallas_call | solution.py:532
  46.0 1.4 %collective-permute-done.11.other = bf16[160,256]{1,0:T(8,128)(2,1)S(1)} collective-permute-done((bf16[160,256]{1,0:T(8,128)(2,1)S(1)}, bf16[160,256]{1,0:T(8,128)(2,1)S(1)}, u32[]{:S(2)}, u32[]{:S(2)}) %collective-permute-start.11) | collective-permute-done | bytes 81952 | tf_op jit(solution)/shard_map/ppermute | solution.py:406
  47.4 0.7 %shard_map.123 = (f32[2,64,256]{2,1,0:T(8,128)}, f32[32,64]{1,0:T(8,128)}, f32[1,8]{1,0:T(1,128)}) custom-call(bf16[160,256]{1,0:T(8,128)(2,1)S(1)} %pad_maximum_fusion.4.mine, bf16[160,256]{1,0:T(8,128)(2,1)S(1)} %collective-permute-done.11.other), custom_call_target="tpu_custom_call" | custom-call | tf_op jit(solution)/shard_map/pallas_call | solution.py:555
  (48 shorter events, 1.9 us)
Async XLA Ops:
  0.6 6.2 %copy-start.2 = (bf16[256,256]{1,0:T(8,128)(2,1)S(1)}, bf16[256,256]{1,0:T(8,128)(2,1)}, u32[]{:S(2)}) copy-start(bf16[256,256]{1,0:T(8,128)(2,1)} %entry.3) | copy-start | bytes 393220
  0.6 6.1 %copy-start.3 = (bf16[256,256]{1,0:T(8,128)(2,1)S(1)}, bf16[256,256]{1,0:T(8,128)(2,1)}, u32[]{:S(2)}) copy-start(bf16[256,256]{1,0:T(8,128)(2,1)} %exit_.1) | copy-start | bytes 393220
  0.7 6.1 %copy-start.6 = (bf16[32,64]{1,0:T(8,128)(2,1)S(1)}, bf16[32,64]{1,0:T(8,128)(2,1)}, u32[]{:S(2)}) copy-start(bf16[32,64]{1,0:T(8,128)(2,1)} %cluster.1) | copy-start | bytes 12292
  0.7 6.1 %copy-start.7 = (f32[8]{0:T(128)S(1)}, f32[8]{0:T(128)}, u32[]{:S(2)}) copy-start(f32[8]{0:T(128)} %sharp.3) | copy-start | bytes 100
  0.7 6.1 %copy-start.8 = (s32[32]{0:T(128)S(1)}, s32[32]{0:T(128)}, u32[]{:S(2)}) copy-start(s32[32]{0:T(128)} %tally.1) | copy-start | bytes 388
  0.7 6.1 %copy-start = (bf16[512,256]{1,0:T(8,128)(2,1)S(1)}, bf16[512,256]{1,0:T(8,128)(2,1)}, u32[]{:S(2)}) copy-start(bf16[512,256]{1,0:T(8,128)(2,1)} %x.3) | copy-start | bytes 786436
  0.7 6.1 %copy-start.1 = (bf16[512,256]{1,0:T(8,128)(2,1)S(1)}, bf16[512,256]{1,0:T(8,128)(2,1)}, u32[]{:S(2)}) copy-start(bf16[512,256]{1,0:T(8,128)(2,1)} %rc.3) | copy-start | bytes 786436
  0.7 6.1 %copy-start.5 = (f32[3,32,32]{2,1,0:T(8,128)S(1)}, f32[3,32,32]{2,1,0:T(8,128)}, u32[]{:S(2)}) copy-start(f32[3,32,32]{2,1,0:T(8,128)} %maps.1) | copy-start | bytes 36868
  3.7 5.6 %collective-permute-start = (bf16[272,128]{1,0:T(8,128)(2,1)}, bf16[272,128]{1,0:T(8,128)(2,1)S(1)}, u32[]{:S(2)}, u32[]{:S(2)}) collective-permute-start(bf16[272,128]{1,0:T(8,128)(2,1)} %shard_map.119.payload_in), channel_id=1, source_target_pairs={{0,8},{1,9},{2,10},{3,11},{4,12},{5,13},{6,14},{7,15},{8,0},{9,1},... | collective-permute-start | bytes 208904 | tf_op jit(solution)/shard_map/ppermute | solution.py:406
  6.8 0.9 %copy-start.4 = (bf16[272,128]{1,0:T(8,128)(2,1)S(1)}, bf16[272,128]{1,0:T(8,128)(2,1)}, u32[]{:S(2)}) copy-start(bf16[272,128]{1,0:T(8,128)(2,1)} %shard_map.119.payload_in) | copy-start | bytes 208900
  9.4 5.4 %collective-permute-start.1 = (f16[272,128]{1,0:T(8,128)(2,1)S(1)}, f16[272,128]{1,0:T(8,128)(2,1)S(1)}, u32[]{:S(2)}, u32[]{:S(2)}) collective-permute-start(f16[272,128]{1,0:T(8,128)(2,1)S(1)} %pad_maximum_fusion.5), channel_id=1, source_target_pairs={{0,16},{1,17},{2,18},{3,19},{4,20},{5,21},{6,22},{7,23},{8,24},{9,... | collective-permute-start | bytes 208904 | tf_op jit(solution)/shard_map/ppermute | solution.py:406
  15.1 5.1 %collective-permute-start.2 = (f16[272,128]{1,0:T(8,128)(2,1)S(1)}, f16[272,128]{1,0:T(8,128)(2,1)S(1)}, u32[]{:S(2)}, u32[]{:S(2)}) collective-permute-start(f16[272,128]{1,0:T(8,128)(2,1)S(1)} %pad_maximum_fusion.6), channel_id=1, source_target_pairs={{0,2},{1,3},{2,0},{3,1},{4,6},{5,7},{6,4},{7,5},{8,10},{9,11},{10,... | collective-permute-start | bytes 208904 | tf_op jit(solution)/shard_map/ppermute | solution.py:406
  17.0 4.3 %collective-permute-start.3 = (f16[272,128]{1,0:T(8,128)(2,1)S(1)}, f16[272,128]{1,0:T(8,128)(2,1)S(1)}, u32[]{:S(2)}, u32[]{:S(2)}) collective-permute-start(f16[272,128]{1,0:T(8,128)(2,1)S(1)} %pad_maximum_fusion.6), channel_id=1, source_target_pairs={{0,4},{1,5},{2,6},{3,7},{4,0},{5,1},{6,2},{7,3},{8,12},{9,13},{10,... | collective-permute-start | bytes 208904 | tf_op jit(solution)/shard_map/ppermute | solution.py:406
  18.5 5.2 %collective-permute-start.4 = (f16[272,128]{1,0:T(8,128)(2,1)S(1)}, f16[272,128]{1,0:T(8,128)(2,1)S(1)}, u32[]{:S(2)}, u32[]{:S(2)}) collective-permute-start(f16[272,128]{1,0:T(8,128)(2,1)S(1)} %pad_maximum_fusion.6), channel_id=1, source_target_pairs={{0,6},{1,7},{2,4},{3,5},{4,2},{5,3},{6,0},{7,1},{8,14},{9,15},{10,... | collective-permute-start | bytes 208904 | tf_op jit(solution)/shard_map/ppermute | solution.py:406
  23.8 1.4 %collective-permute-start.5 = (f32[272,128]{1,0:T(8,128)S(1)}, f32[272,128]{1,0:T(8,128)S(1)}, u32[]{:S(2)}, u32[]{:S(2)}) collective-permute-start(f32[272,128]{1,0:T(8,128)S(1)} %fusion.8.mine), channel_id=1, source_target_pairs={{0,1},{1,0},{2,3},{3,2},{4,5},{5,4},{6,7},{7,6},{8,9},{9,8},{10,11... | collective-permute-start | bytes 417800 | tf_op jit(solution)/shard_map/ppermute | solution.py:406
  28.9 1.4 %collective-permute-start.6 = (bf16[288,256]{1,0:T(8,128)(2,1)S(1)}, bf16[288,256]{1,0:T(8,128)(2,1)S(1)}, u32[]{:S(2)}, u32[]{:S(2)}) collective-permute-start(bf16[288,256]{1,0:T(8,128)(2,1)S(1)} %get-tuple-element.36), channel_id=1, source_target_pairs={{0,1},{1,0},{2,3},{3,2},{4,5},{5,4},{6,7},{7,6},{8,9},{9,8},{10,11... | collective-permute-start | bytes 442376 | tf_op jit(solution)/shard_map/ppermute | solution.py:406
  30.5 4.9 %collective-permute-start.7 = (bf16[160,256]{1,0:T(8,128)(2,1)S(1)}, bf16[160,256]{1,0:T(8,128)(2,1)S(1)}, u32[]{:S(2)}, u32[]{:S(2)}) collective-permute-start(bf16[160,256]{1,0:T(8,128)(2,1)S(1)} %get-tuple-element.53), channel_id=1, source_target_pairs={{0,4},{1,5},{2,6},{3,7},{4,0},{5,1},{6,2},{7,3},{8,12},{9,13},{10,... | collective-permute-start | bytes 245768 | tf_op jit(solution)/shard_map/ppermute | solution.py:406
  31.2 6.2 %collective-permute-start.8 = (bf16[160,256]{1,0:T(8,128)(2,1)S(1)}, bf16[160,256]{1,0:T(8,128)(2,1)S(1)}, u32[]{:S(2)}, u32[]{:S(2)}) collective-permute-start(bf16[160,256]{1,0:T(8,128)(2,1)S(1)} %get-tuple-element.54), channel_id=1, source_target_pairs={{0,2},{1,3},{2,0},{3,1},{4,6},{5,7},{6,4},{7,5},{8,10},{9,11},{10,... | collective-permute-start | bytes 245768 | tf_op jit(solution)/shard_map/ppermute | solution.py:406
  31.9 5.4 %collective-permute-start.9 = (bf16[160,256]{1,0:T(8,128)(2,1)S(1)}, bf16[160,256]{1,0:T(8,128)(2,1)S(1)}, u32[]{:S(2)}, u32[]{:S(2)}) collective-permute-start(bf16[160,256]{1,0:T(8,128)(2,1)S(1)} %get-tuple-element.54), channel_id=1, source_target_pairs={{0,6},{1,7},{2,4},{3,5},{4,2},{5,3},{6,0},{7,1},{8,14},{9,15},{10,... | collective-permute-start | bytes 245768 | tf_op jit(solution)/shard_map/ppermute | solution.py:406
  37.5 4.5 %collective-permute-start.10 = (bf16[160,256]{1,0:T(8,128)(2,1)S(1)}, bf16[160,256]{1,0:T(8,128)(2,1)S(1)}, u32[]{:S(2)}, u32[]{:S(2)}) collective-permute-start(bf16[160,256]{1,0:T(8,128)(2,1)S(1)} %pad_maximum_fusion.3), channel_id=1, source_target_pairs={{0,8},{1,9},{2,10},{3,11},{4,12},{5,13},{6,14},{7,15},{8,0},{9,1},... | collective-permute-start | bytes 245768 | tf_op jit(solution)/shard_map/ppermute | solution.py:406
  42.0 5.4 %collective-permute-start.11 = (bf16[160,256]{1,0:T(8,128)(2,1)S(1)}, bf16[160,256]{1,0:T(8,128)(2,1)S(1)}, u32[]{:S(2)}, u32[]{:S(2)}) collective-permute-start(bf16[160,256]{1,0:T(8,128)(2,1)S(1)} %pad_maximum_fusion.4.mine), channel_id=1, source_target_pairs={{0,16},{1,17},{2,18},{3,19},{4,20},{5,21},{6,22},{7,23},{8,24},{9,... | collective-permute-start | bytes 245768 | tf_op jit(solution)/shard_map/ppermute | solution.py:406

commit v3 on v2

--- a/solution.py
+++ b/solution.py
@@ -332,12 +332,21 @@
     folded = slice_sum[:, :LANES]
     for i in range(1, per * slices // LANES):
         folded = folded + slice_sum[:, i * LANES : (i + 1) * LANES]
-    half = head // 2
+    folded = folded + pltpu.roll(folded, LANES // 2, 1)
+    part = head * slices // width
+    low = lax.broadcasted_iota(jnp.int32, (part, LANES), 1) < slices
+    slice_rows = [
+        jnp.where(low, folded[i * part : (i + 1) * part], folded[(i + 1) * part : (i + 2) * part])
+        for i in range(0, head // part, 2)
+    ]
     temp = jnp.sum(jnp.concatenate(temps, axis=0), axis=1, keepdims=True)
-    temp = jnp.broadcast_to(temp, (heads, width))
+    temp = jnp.broadcast_to(temp, (heads, width // 2))
     temp_high = temp.astype(BF16).astype(F32)
     extra = jnp.concatenate(
-        [jnp.concatenate([folded[:half], folded[half:]], axis=1), temp_high, temp - temp_high],
+        [
+            jnp.concatenate(slice_rows, axis=1),
+            jnp.concatenate([temp_high, temp - temp_high], axis=1),
+        ],
         axis=0,
     ).astype(BF16)
     odd = lax.axis_index("grp") % 2
@@ -373,16 +382,17 @@
     head, slices = slice_grad.shape
     weight_grads[0] = total[:owner_rows]
     weight_grads[1] = total[owner_rows : 2 * owner_rows]
-    half = head // 2
     extra = total[2 * owner_rows :]
-    folded = jnp.concatenate([extra[:half, :LANES], extra[:half, LANES : 2 * LANES]], axis=0)
-    shift = LANES // 2
-    while shift >= slices:
-        folded = folded + pltpu.roll(folded, shift, 1)
-        shift //= 2
-    slice_grad[...] = folded[:, :slices]
+    part = head * slices // extra.shape[1]
+    for i in range(head // part):
+        tile = extra[:part, i // 2 * LANES : (i // 2 + 1) * LANES]
+        if i % 2:
+            tile = pltpu.roll(tile, LANES // 2, 1)
+        slice_grad[i * part : (i + 1) * part, :] = tile[:, :slices]
     heads = temp_grad.shape[1]
-    temp = (extra[half : half + heads] + extra[half + heads : half + 2 * heads])[:, :LANES]
+    temp = extra[part:]
+    middle = temp.shape[1] // 2
+    temp = (temp[:, :middle] + temp[:, middle:])[:, :LANES]
     temp = jnp.where(head_mask(temp.shape, 1, 1), temp, 0.0)
     temp_grad[...] = jnp.sum(temp, axis=0, keepdims=True)[:, :heads]
 
@@ -435,10 +445,11 @@
 
 def halves(total, start):
     pair = total[start:]
-    n = pair.shape[0] // 2
-    pair = pair[:n] + pair[n:]
+    n = pair.shape[1] // 2
+    pair = pair[:, :n] + pair[:, n:]
     high = lax.reduce_precision(pair, 8, 7)
-    return jnp.concatenate([total[:start], high, pair - high], axis=0).astype(BF16)
+    pair = jnp.concatenate([high, pair - high], axis=1)
+    return jnp.concatenate([total[:start], pair], axis=0).astype(BF16)
 
 
 def local(x, rc, entry, exit_, cluster, sharp, maps, tally):
@@ -500,7 +511,7 @@
 
     owner_rows = width // owners
     chunk = 2 * owner_rows
-    extra = head // 2 + 2 * heads
+    extra = head * slices // width + heads
     keep, send, gxmt, tokens, grads = call(
         middle_kernel,
         [
@@ -536,7 +547,7 @@
         4,
     )(gxmt, entry, tokens, grads)
     total = keep.astype(F32) + got_half.astype(F32)
-    total = halves(total, total.shape[0] - 2 * heads)
+    total = halves(total, total.shape[0] - heads)
     half = lax.axis_index("grp") // 2
     common = total[owners // 2 * chunk :]
     mine = jnp.concatenate(
@@ -547,10 +558,10 @@
     )
     others = [exchange(mine, 4), exchange(theirs, 2), exchange(theirs, 6)]
     total = gather(mine, others)
-    mine = halves(total, total.shape[0] - 2 * heads)
+    mine = halves(total, total.shape[0] - heads)
     for mask in (8, *far[:-1]):
         total = gather(mine, exchanges(mine, (mask,)))
-        mine = halves(total, total.shape[0] - 2 * heads)
+        mine = halves(total, total.shape[0] - heads)
     other = exchange(mine, far[-1])
     weight_grads, slice_grad, temp_grad = call(
         finish_kernel,

time: 48.3 us -> 47.9 us (level)
  transfers between devices with their start and end apart: 12 -> 12, of which waited for: 11 -> 12; matrix products, arithmetic and copies ran while one was open for 0% -> 0% of each run, Pallas kernels for 5% -> 5%
where the time goes in v3:
time: 47.9 us; the launch traced here: 47.7 us
  starting transfers between devices  18.1 us (38%)
  waiting for transfers between devices  17.2 us (36%)
  Pallas kernels  9.93 us (21%)
  local copies, waits for them, and re-layouts  0.98 us (2%)
  between operations  0.93 us (2%)
  other arithmetic  0.66 us (1%)
    ppermute x12, starting transfers between devices, exchange(): return lax.ppermute(a, ALL, [(i, i ^ mask) for i in range(devices)])  18.1 us
    ppermute x12, waiting for transfers between devices, exchange(): return lax.ppermute(a, ALL, [(i, i ^ mask) for i in range(devices)])  17.2 us
    pallas_call x1, Pallas kernels, local(): call(middle_kernel, [((owners // 2 * chunk + extra, width), BF16), ((owne...  3.7 us
    pallas_call x1, Pallas kernels, local(): call(points_kernel, [((token_rows, LANES), BF16)], 0, 7, scratch=[pltpu.S...  2.97 us
    pallas_call x1, Pallas kernels, local(): call(shadow_kernel, [((token_rows, LANES), BF16), ((width, points), BF16)...  1.46 us
    pallas_call x1, Pallas kernels, local(): call(features_kernel, [((points, width), BF16), (maps.shape, F32)], 0, 4)  1.12 us
  transfers between devices with their start and end apart: 12, of which 12 were waited for; matrix products, arithmetic and copies ran while one was open for 0% of the time, Pallas kernels for 5%

profile of v3, /device:TPU:0, one launch (start us, length us, event | category | flops | bytes accessed | tf_op | source)
XLA Modules:
  0.0 47.7 jit_solution(10477440822886883980)
XLA Ops:
  0.7 3.0 %shard_map.119.payload_in = bf16[272,128]{1,0:T(8,128)(2,1)} custom-call(s32[32]{0:T(128)} %tally.1, f32[8]{0:T(128)} %sharp.3, bf16[512,256]{1,0:T(8,128)(2,1)} %x.3, bf16[512,256]{1,0:T(8,128)(2,1)} %rc.3, bf16[256,256]{1,0:T(8,128)(2,1)} %entry.3, bf16[256,256]{1,0:T(8,128)(2,1)} %exit_.1, bf16[32,64]{1,0:T(8,128)(2,1)} %cluster.1), custom_call_target="tpu_custom_call" | custom-call | tf_op jit(solution)/shard_map/pallas_call | solution.py:465
  3.7 3.1 %collective-permute-start = (bf16[272,128]{1,0:T(8,128)(2,1)}, bf16[272,128]{1,0:T(8,128)(2,1)S(1)}, u32[]{:S(2)}, u32[]{:S(2)}) collective-permute-start(bf16[272,128]{1,0:T(8,128)(2,1)} %shard_map.119.payload_in), channel_id=1, source_target_pairs={{0,8},{1,9},{2,10},{3,11},{4,12},{5,13},{6,14},{7,15},{8,0},{9,1},... | collective-permute-start | bytes 208904 | tf_op jit(solution)/shard_map/ppermute | solution.py:416
  6.9 0.9 %copy-done.4 = bf16[272,128]{1,0:T(8,128)(2,1)S(1)} copy-done((bf16[272,128]{1,0:T(8,128)(2,1)S(1)}, bf16[272,128]{1,0:T(8,128)(2,1)}, u32[]{:S(2)}) %copy-start.4) | copy-done | bytes 69656
  7.7 1.5 %shard_map.120 = (bf16[272,128]{1,0:T(8,128)(2,1)S(1)}, bf16[256,512]{1,0:T(8,128)(2,1)S(1)}, bf16[256,512]{1,0:T(8,128)(2,1)S(1)}, bf16[512,512]{1,0:T(8,128)(2...) custom-call(s32[32]{0:T(128)S(1)} %copy-done.8, ...), custom_call_target="tpu_custom_call" | custom-call | tf_op jit(solution)/shard_map/pallas_call | solution.py:486
  9.4 3.1 %collective-permute-start.1 = (f16[272,128]{1,0:T(8,128)(2,1)S(1)}, f16[272,128]{1,0:T(8,128)(2,1)S(1)}, u32[]{:S(2)}, u32[]{:S(2)}) collective-permute-start(f16[272,128]{1,0:T(8,128)(2,1)S(1)} %pad_maximum_fusion.2), channel_id=1, source_target_pairs={{0,16},{1,17},{2,18},{3,19},{4,20},{5,21},{6,22},{7,23},{8,24},{9,... | collective-permute-start | bytes 208904 | tf_op jit(solution)/shard_map/ppermute | solution.py:416
  12.5 2.3 %collective-permute-done.1 = f16[272,128]{1,0:T(8,128)(2,1)S(1)} collective-permute-done((f16[272,128]{1,0:T(8,128)(2,1)S(1)}, f16[272,128]{1,0:T(8,128)(2,1)S(1)}, u32[]{:S(2)}, u32[]{:S(2)}) %collective-permute-start.1) | collective-permute-done | bytes 69664 | tf_op jit(solution)/shard_map/ppermute | solution.py:416
  15.1 1.9 %collective-permute-start.2 = (f16[272,128]{1,0:T(8,128)(2,1)S(1)}, f16[272,128]{1,0:T(8,128)(2,1)S(1)}, u32[]{:S(2)}, u32[]{:S(2)}) collective-permute-start(f16[272,128]{1,0:T(8,128)(2,1)S(1)} %pad_maximum_fusion.3), channel_id=1, source_target_pairs={{0,2},{1,3},{2,0},{3,1},{4,6},{5,7},{6,4},{7,5},{8,10},{9,11},{10,... | collective-permute-start | bytes 208904 | tf_op jit(solution)/shard_map/ppermute | solution.py:416
  17.0 1.5 %collective-permute-start.3 = (f16[272,128]{1,0:T(8,128)(2,1)S(1)}, f16[272,128]{1,0:T(8,128)(2,1)S(1)}, u32[]{:S(2)}, u32[]{:S(2)}) collective-permute-start(f16[272,128]{1,0:T(8,128)(2,1)S(1)} %pad_maximum_fusion.3), channel_id=1, source_target_pairs={{0,4},{1,5},{2,6},{3,7},{4,0},{5,1},{6,2},{7,3},{8,12},{9,13},{10,... | collective-permute-start | bytes 208904 | tf_op jit(solution)/shard_map/ppermute | solution.py:416
  18.6 1.6 %collective-permute-done.2 = f16[272,128]{1,0:T(8,128)(2,1)S(1)} collective-permute-done((f16[272,128]{1,0:T(8,128)(2,1)S(1)}, f16[272,128]{1,0:T(8,128)(2,1)S(1)}, u32[]{:S(2)}, u32[]{:S(2)}) %collective-permute-start.2) | collective-permute-done | bytes 69664 | tf_op jit(solution)/shard_map/ppermute | solution.py:416
  20.2 1.1 %collective-permute-done.3 = f16[272,128]{1,0:T(8,128)(2,1)S(1)} collective-permute-done((f16[272,128]{1,0:T(8,128)(2,1)S(1)}, f16[272,128]{1,0:T(8,128)(2,1)S(1)}, u32[]{:S(2)}, u32[]{:S(2)}) %collective-permute-start.3) | collective-permute-done | bytes 69664 | tf_op jit(solution)/shard_map/ppermute | solution.py:416
  21.3 2.4 %collective-permute-done.4 = f16[272,128]{1,0:T(8,128)(2,1)S(1)} collective-permute-done((f16[272,128]{1,0:T(8,128)(2,1)S(1)}, f16[272,128]{1,0:T(8,128)(2,1)S(1)}, u32[]{:S(2)}, u32[]{:S(2)}) %collective-permute-start.4) | collective-permute-done | bytes 69664 | tf_op jit(solution)/shard_map/ppermute | solution.py:416
  23.9 1.3 %collective-permute-done.5.other = f32[272,128]{1,0:T(8,128)S(1)} collective-permute-done((f32[272,128]{1,0:T(8,128)S(1)}, f32[272,128]{1,0:T(8,128)S(1)}, u32[]{:S(2)}, u32[]{:S(2)}) %collective-permute-start.5) | collective-permute-done | bytes 139296 | tf_op jit(solution)/shard_map/ppermute | solution.py:416
  25.3 3.7 %shard_map.121 = (bf16[272,256]{1,0:T(8,128)(2,1)S(1)}, bf16[272,256]{1,0:T(8,128)(2,1)S(1)}, bf16[256,512]{1,0:T(8,128)(2,1)S(1)}, f32[128,128]{1,0:T(8,128)S(1)}, f32[128,384]{1,0:T(8,128)S(1)}) custom-call(f32[8]{0:T(128)S(1)} %copy-done.7, f32[272,128]{1,0:T(8,128)S(1)} %fusion.8.mine, f32[272,128]{1,0:T(8,128)S(1)} %collective-permute-done.5.other, ...), custom_call_target="tpu_custom_call" | custom-call | tf_op jit(solution)/shard_map/pallas_call | solution.py:515
  29.2 1.2 %collective-permute-done.6 = bf16[272,256]{1,0:T(8,128)(2,1)S(1)} collective-permute-done((bf16[272,256]{1,0:T(8,128)(2,1)S(1)}, bf16[272,256]{1,0:T(8,128)(2,1)S(1)}, u32[]{:S(2)}, u32[]{:S(2)}) %collective-permute-start.6) | collective-permute-done | bytes 139296 | tf_op jit(solution)/shard_map/ppermute | solution.py:416
  31.1 0.8 %collective-permute-start.8 = (bf16[144,256]{1,0:T(8,128)(2,1)S(1)}, bf16[144,256]{1,0:T(8,128)(2,1)S(1)}, u32[]{:S(2)}, u32[]{:S(2)}) collective-permute-start(bf16[144,256]{1,0:T(8,128)(2,1)S(1)} %get-tuple-element.54), channel_id=1, source_target_pairs={{0,2},{1,3},{2,0},{3,1},{4,6},{5,7},{6,4},{7,5},{8,10},{9,11},{10,... | collective-permute-start | bytes 221192 | tf_op jit(solution)/shard_map/ppermute | solution.py:416
  31.9 2.2 %collective-permute-start.9 = (bf16[144,256]{1,0:T(8,128)(2,1)S(1)}, bf16[144,256]{1,0:T(8,128)(2,1)S(1)}, u32[]{:S(2)}, u32[]{:S(2)}) collective-permute-start(bf16[144,256]{1,0:T(8,128)(2,1)S(1)} %get-tuple-element.54), channel_id=1, source_target_pairs={{0,6},{1,7},{2,4},{3,5},{4,2},{5,3},{6,0},{7,1},{8,14},{9,15},{10,... | collective-permute-start | bytes 221192 | tf_op jit(solution)/shard_map/ppermute | solution.py:416
  34.1 1.1 %collective-permute-done.7 = bf16[144,256]{1,0:T(8,128)(2,1)S(1)} collective-permute-done((bf16[144,256]{1,0:T(8,128)(2,1)S(1)}, bf16[144,256]{1,0:T(8,128)(2,1)S(1)}, u32[]{:S(2)}, u32[]{:S(2)}) %collective-permute-start.7) | collective-permute-done | bytes 73760 | tf_op jit(solution)/shard_map/ppermute | solution.py:416
  35.2 1.1 %collective-permute-done.8 = bf16[144,256]{1,0:T(8,128)(2,1)S(1)} collective-permute-done((bf16[144,256]{1,0:T(8,128)(2,1)S(1)}, bf16[144,256]{1,0:T(8,128)(2,1)S(1)}, u32[]{:S(2)}, u32[]{:S(2)}) %collective-permute-start.8) | collective-permute-done | bytes 73760 | tf_op jit(solution)/shard_map/ppermute | solution.py:416
  36.3 0.9 %collective-permute-done.9 = bf16[144,256]{1,0:T(8,128)(2,1)S(1)} collective-permute-done((bf16[144,256]{1,0:T(8,128)(2,1)S(1)}, bf16[144,256]{1,0:T(8,128)(2,1)S(1)}, u32[]{:S(2)}, u32[]{:S(2)}) %collective-permute-start.9) | collective-permute-done | bytes 73760 | tf_op jit(solution)/shard_map/ppermute | solution.py:416
  37.3 1.6 %collective-permute-start.10 = (bf16[144,256]{1,0:T(8,128)(2,1)S(1)}, bf16[144,256]{1,0:T(8,128)(2,1)S(1)}, u32[]{:S(2)}, u32[]{:S(2)}) collective-permute-start(bf16[144,256]{1,0:T(8,128)(2,1)S(1)} %maximum_maximum_fusion.1), channel_id=1, source_target_pairs={{0,8},{1,9},{2,10},{3,11},{4,12},{5,13},{6,14},{7,15},{8,0},{9,1},... | collective-permute-start | bytes 221192 | tf_op jit(solution)/shard_map/ppermute | solution.py:416
  38.9 2.8 %collective-permute-done.10 = bf16[144,256]{1,0:T(8,128)(2,1)S(1)} collective-permute-done((bf16[144,256]{1,0:T(8,128)(2,1)S(1)}, bf16[144,256]{1,0:T(8,128)(2,1)S(1)}, u32[]{:S(2)}, u32[]{:S(2)}) %collective-permute-start.10) | collective-permute-done | bytes 73760 | tf_op jit(solution)/shard_map/ppermute | solution.py:416
  41.8 2.8 %collective-permute-start.11 = (bf16[144,256]{1,0:T(8,128)(2,1)S(1)}, bf16[144,256]{1,0:T(8,128)(2,1)S(1)}, u32[]{:S(2)}, u32[]{:S(2)}) collective-permute-start(bf16[144,256]{1,0:T(8,128)(2,1)S(1)} %maximum_maximum_fusion.2.mine), channel_id=1, source_target_pairs={{0,16},{1,17},{2,18},{3,19},{4,20},{5,21},{6,22},{7,23},{8,24},{9,... | collective-permute-start | bytes 221192 | tf_op jit(solution)/shard_map/ppermute | solution.py:416
  44.6 1.1 %shard_map.122 = (bf16[512,256]{1,0:T(8,128)(2,1)}, f32[3,32,32]{2,1,0:T(8,128)}) custom-call(bf16[256,512]{1,0:T(8,128)(2,1)S(1)} %get-tuple-element.31.gxmt, bf16[256,256]{1,0:T(8,128)(2,1)S(1)} %copy-done.2, f32[128,128]{1,0:T(8,128)S(1)} %get-tuple-element.32.tokens, f32[128,384]{1,0:T(8,128)S(1)} %get-tuple-element.33.grads), custom_call_target="tpu_custom_call" | custom-call | tf_op jit(solution)/shard_map/pallas_call | solution.py:543
  45.7 1.4 %collective-permute-done.11.other = bf16[144,256]{1,0:T(8,128)(2,1)S(1)} collective-permute-done((bf16[144,256]{1,0:T(8,128)(2,1)S(1)}, bf16[144,256]{1,0:T(8,128)(2,1)S(1)}, u32[]{:S(2)}, u32[]{:S(2)}) %collective-permute-start.11) | collective-permute-done | bytes 73760 | tf_op jit(solution)/shard_map/ppermute | solution.py:416
  (48 shorter events, 2.6 us)
Async XLA Ops:
  0.6 6.2 %copy-start.2 = (bf16[256,256]{1,0:T(8,128)(2,1)S(1)}, bf16[256,256]{1,0:T(8,128)(2,1)}, u32[]{:S(2)}) copy-start(bf16[256,256]{1,0:T(8,128)(2,1)} %entry.3) | copy-start | bytes 393220
  0.6 6.1 %copy-start.3 = (bf16[256,256]{1,0:T(8,128)(2,1)S(1)}, bf16[256,256]{1,0:T(8,128)(2,1)}, u32[]{:S(2)}) copy-start(bf16[256,256]{1,0:T(8,128)(2,1)} %exit_.1) | copy-start | bytes 393220
  0.7 6.1 %copy-start.6 = (bf16[32,64]{1,0:T(8,128)(2,1)S(1)}, bf16[32,64]{1,0:T(8,128)(2,1)}, u32[]{:S(2)}) copy-start(bf16[32,64]{1,0:T(8,128)(2,1)} %cluster.1) | copy-start | bytes 12292
  0.7 6.1 %copy-start.7 = (f32[8]{0:T(128)S(1)}, f32[8]{0:T(128)}, u32[]{:S(2)}) copy-start(f32[8]{0:T(128)} %sharp.3) | copy-start | bytes 100
  0.7 6.1 %copy-start.8 = (s32[32]{0:T(128)S(1)}, s32[32]{0:T(128)}, u32[]{:S(2)}) copy-start(s32[32]{0:T(128)} %tally.1) | copy-start | bytes 388
  0.7 6.1 %copy-start = (bf16[512,256]{1,0:T(8,128)(2,1)S(1)}, bf16[512,256]{1,0:T(8,128)(2,1)}, u32[]{:S(2)}) copy-start(bf16[512,256]{1,0:T(8,128)(2,1)} %x.3) | copy-start | bytes 786436
  0.7 6.1 %copy-start.1 = (bf16[512,256]{1,0:T(8,128)(2,1)S(1)}, bf16[512,256]{1,0:T(8,128)(2,1)}, u32[]{:S(2)}) copy-start(bf16[512,256]{1,0:T(8,128)(2,1)} %rc.3) | copy-start | bytes 786436
  0.7 6.1 %copy-start.5 = (f32[3,32,32]{2,1,0:T(8,128)S(1)}, f32[3,32,32]{2,1,0:T(8,128)}, u32[]{:S(2)}) copy-start(f32[3,32,32]{2,1,0:T(8,128)} %maps.1) | copy-start | bytes 36868
  3.7 5.6 %collective-permute-start = (bf16[272,128]{1,0:T(8,128)(2,1)}, bf16[272,128]{1,0:T(8,128)(2,1)S(1)}, u32[]{:S(2)}, u32[]{:S(2)}) collective-permute-start(bf16[272,128]{1,0:T(8,128)(2,1)} %shard_map.119.payload_in), channel_id=1, source_target_pairs={{0,8},{1,9},{2,10},{3,11},{4,12},{5,13},{6,14},{7,15},{8,0},{9,1},... | collective-permute-start | bytes 208904 | tf_op jit(solution)/shard_map/ppermute | solution.py:416
  6.8 0.9 %copy-start.4 = (bf16[272,128]{1,0:T(8,128)(2,1)S(1)}, bf16[272,128]{1,0:T(8,128)(2,1)}, u32[]{:S(2)}) copy-start(bf16[272,128]{1,0:T(8,128)(2,1)} %shard_map.119.payload_in) | copy-start | bytes 208900
  9.4 5.4 %collective-permute-start.1 = (f16[272,128]{1,0:T(8,128)(2,1)S(1)}, f16[272,128]{1,0:T(8,128)(2,1)S(1)}, u32[]{:S(2)}, u32[]{:S(2)}) collective-permute-start(f16[272,128]{1,0:T(8,128)(2,1)S(1)} %pad_maximum_fusion.2), channel_id=1, source_target_pairs={{0,16},{1,17},{2,18},{3,19},{4,20},{5,21},{6,22},{7,23},{8,24},{9,... | collective-permute-start | bytes 208904 | tf_op jit(solution)/shard_map/ppermute | solution.py:416
  15.1 5.1 %collective-permute-start.2 = (f16[272,128]{1,0:T(8,128)(2,1)S(1)}, f16[272,128]{1,0:T(8,128)(2,1)S(1)}, u32[]{:S(2)}, u32[]{:S(2)}) collective-permute-start(f16[272,128]{1,0:T(8,128)(2,1)S(1)} %pad_maximum_fusion.3), channel_id=1, source_target_pairs={{0,2},{1,3},{2,0},{3,1},{4,6},{5,7},{6,4},{7,5},{8,10},{9,11},{10,... | collective-permute-start | bytes 208904 | tf_op jit(solution)/shard_map/ppermute | solution.py:416
  17.0 4.3 %collective-permute-start.3 = (f16[272,128]{1,0:T(8,128)(2,1)S(1)}, f16[272,128]{1,0:T(8,128)(2,1)S(1)}, u32[]{:S(2)}, u32[]{:S(2)}) collective-permute-start(f16[272,128]{1,0:T(8,128)(2,1)S(1)} %pad_maximum_fusion.3), channel_id=1, source_target_pairs={{0,4},{1,5},{2,6},{3,7},{4,0},{5,1},{6,2},{7,3},{8,12},{9,13},{10,... | collective-permute-start | bytes 208904 | tf_op jit(solution)/shard_map/ppermute | solution.py:416
  18.5 5.2 %collective-permute-start.4 = (f16[272,128]{1,0:T(8,128)(2,1)S(1)}, f16[272,128]{1,0:T(8,128)(2,1)S(1)}, u32[]{:S(2)}, u32[]{:S(2)}) collective-permute-start(f16[272,128]{1,0:T(8,128)(2,1)S(1)} %pad_maximum_fusion.3), channel_id=1, source_target_pairs={{0,6},{1,7},{2,4},{3,5},{4,2},{5,3},{6,0},{7,1},{8,14},{9,15},{10,... | collective-permute-start | bytes 208904 | tf_op jit(solution)/shard_map/ppermute | solution.py:416
  23.8 1.4 %collective-permute-start.5 = (f32[272,128]{1,0:T(8,128)S(1)}, f32[272,128]{1,0:T(8,128)S(1)}, u32[]{:S(2)}, u32[]{:S(2)}) collective-permute-start(f32[272,128]{1,0:T(8,128)S(1)} %fusion.8.mine), channel_id=1, source_target_pairs={{0,1},{1,0},{2,3},{3,2},{4,5},{5,4},{6,7},{7,6},{8,9},{9,8},{10,11... | collective-permute-start | bytes 417800 | tf_op jit(solution)/shard_map/ppermute | solution.py:416
  29.0 1.4 %collective-permute-start.6 = (bf16[272,256]{1,0:T(8,128)(2,1)S(1)}, bf16[272,256]{1,0:T(8,128)(2,1)S(1)}, u32[]{:S(2)}, u32[]{:S(2)}) collective-permute-start(bf16[272,256]{1,0:T(8,128)(2,1)S(1)} %get-tuple-element.36), channel_id=1, source_target_pairs={{0,1},{1,0},{2,3},{3,2},{4,5},{5,4},{6,7},{7,6},{8,9},{9,8},{10,11... | collective-permute-start | bytes 417800 | tf_op jit(solution)/shard_map/ppermute | solution.py:416
  30.5 4.6 %collective-permute-start.7 = (bf16[144,256]{1,0:T(8,128)(2,1)S(1)}, bf16[144,256]{1,0:T(8,128)(2,1)S(1)}, u32[]{:S(2)}, u32[]{:S(2)}) collective-permute-start(bf16[144,256]{1,0:T(8,128)(2,1)S(1)} %get-tuple-element.53), channel_id=1, source_target_pairs={{0,4},{1,5},{2,6},{3,7},{4,0},{5,1},{6,2},{7,3},{8,12},{9,13},{10,... | collective-permute-start | bytes 221192 | tf_op jit(solution)/shard_map/ppermute | solution.py:416
  31.1 5.1 %collective-permute-start.8 = (bf16[144,256]{1,0:T(8,128)(2,1)S(1)}, bf16[144,256]{1,0:T(8,128)(2,1)S(1)}, u32[]{:S(2)}, u32[]{:S(2)}) collective-permute-start(bf16[144,256]{1,0:T(8,128)(2,1)S(1)} %get-tuple-element.54), channel_id=1, source_target_pairs={{0,2},{1,3},{2,0},{3,1},{4,6},{5,7},{6,4},{7,5},{8,10},{9,11},{10,... | collective-permute-start | bytes 221192 | tf_op jit(solution)/shard_map/ppermute | solution.py:416
  31.9 5.3 %collective-permute-start.9 = (bf16[144,256]{1,0:T(8,128)(2,1)S(1)}, bf16[144,256]{1,0:T(8,128)(2,1)S(1)}, u32[]{:S(2)}, u32[]{:S(2)}) collective-permute-start(bf16[144,256]{1,0:T(8,128)(2,1)S(1)} %get-tuple-element.54), channel_id=1, source_target_pairs={{0,6},{1,7},{2,4},{3,5},{4,2},{5,3},{6,0},{7,1},{8,14},{9,15},{10,... | collective-permute-start | bytes 221192 | tf_op jit(solution)/shard_map/ppermute | solution.py:416
  37.3 4.4 %collective-permute-start.10 = (bf16[144,256]{1,0:T(8,128)(2,1)S(1)}, bf16[144,256]{1,0:T(8,128)(2,1)S(1)}, u32[]{:S(2)}, u32[]{:S(2)}) collective-permute-start(bf16[144,256]{1,0:T(8,128)(2,1)S(1)} %maximum_maximum_fusion.1), channel_id=1, source_target_pairs={{0,8},{1,9},{2,10},{3,11},{4,12},{5,13},{6,14},{7,15},{8,0},{9,1},... | collective-permute-start | bytes 221192 | tf_op jit(solution)/shard_map/ppermute | solution.py:416
  41.8 5.3 %collective-permute-start.11 = (bf16[144,256]{1,0:T(8,128)(2,1)S(1)}, bf16[144,256]{1,0:T(8,128)(2,1)S(1)}, u32[]{:S(2)}, u32[]{:S(2)}) collective-permute-start(bf16[144,256]{1,0:T(8,128)(2,1)S(1)} %maximum_maximum_fusion.2.mine), channel_id=1, source_target_pairs={{0,16},{1,17},{2,18},{3,19},{4,20},{5,21},{6,22},{7,23},{8,24},{9,... | collective-permute-start | bytes 221192 | tf_op jit(solution)/shard_map/ppermute | solution.py:416

commit v4 on v3

--- a/solution.py
+++ b/solution.py
@@ -12,7 +12,7 @@
 ALL = ("pts", "grp")
 LANES = 128
 VMEM_LIMIT = 48 * 1024 * 1024
-POINTS_LIMIT = 60 * 1024 * 1024
+OPENING_FLOPS = 3_000_000_000
 
 
 def dot(a, b):
@@ -70,49 +70,19 @@
     return tally[lax.axis_index("pts") * lax.axis_size("grp") + lax.axis_index("grp")]
 
 
+def opening_kernel(out):
+    out[...] = jnp.zeros_like(out)
+
+
 def points_kernel(
-    tally_in,
-    sharp_in,
-    x_in,
-    rc_in,
-    entry_in,
-    exit_in,
-    cluster_in,
-    payload,
-    tally,
-    sharp,
-    x,
-    rc,
-    entry,
-    exit_,
-    cluster,
-    xmt,
-    weights,
-    arrived,
+    tally, sharp, x, rc, entry, exit_, cluster, opening, payload, xmt, weights
 ):
-    pairs = [
-        (entry_in, entry),
-        (x_in, x),
-        (cluster_in, cluster),
-        (sharp_in, sharp),
-        (tally_in, tally),
-        (exit_in, exit_),
-        (rc_in, rc),
-    ]
-    copies = [
-        pltpu.make_async_copy(source, target, arrived.at[i])
-        for i, (source, target) in enumerate(pairs)
-    ]
-    for copy in copies:
-        copy.start()
     points, width = x.shape
     heads = sharp.shape[0]
     head = width // heads
     slices = cluster.shape[1]
     per = LANES // head
     groups = heads // per
-    for copy in copies:
-        copy.wait()
     go = dot_nt(rc[...], exit_[...]).astype(BF16)
     xm = assign(sharp, x, entry, cluster, valid_points(tally), xmt, weights, None)
     rows = groups * slices
@@ -397,7 +367,7 @@
     temp_grad[...] = jnp.sum(temp, axis=0, keepdims=True)[:, :heads]
 
 
-def call(kernel, shapes, in_smem, count, scratch=(), space=pltpu.VMEM, limit=VMEM_LIMIT):
+def call(kernel, shapes, in_smem, count, scratch=(), space=pltpu.VMEM, limit=VMEM_LIMIT, flops=0):
     smem = pl.BlockSpec(memory_space=pltpu.SMEM)
     vmem = pl.BlockSpec(memory_space=pltpu.VMEM)
     rest = pl.BlockSpec(memory_space=space)
@@ -408,6 +378,9 @@
         out_specs=[vmem] * len(shapes),
         scratch_shapes=list(scratch),
         compiler_params=pltpu.CompilerParams(vmem_limit_bytes=limit),
+        cost_estimate=pl.CostEstimate(flops=flops, bytes_accessed=0, transcendentals=0)
+        if flops
+        else None,
     )
 
 
@@ -462,22 +435,17 @@
     rows = heads // per * slices
     token_rows = 2 * rows + 2 * heads
     far = [1 << bit for bit in range(4, devices.bit_length() - 1)]
+    (opening,) = call(opening_kernel, [((8, LANES), F32)], 0, 0, flops=OPENING_FLOPS)()
     (payload,) = call(
         points_kernel,
         [((token_rows, LANES), BF16)],
-        0,
-        7,
+        2,
+        8,
         scratch=[
-            pltpu.SMEM(tally.shape, tally.dtype),
-            pltpu.SMEM(sharp.shape, sharp.dtype),
-            *(pltpu.VMEM(a.shape, a.dtype) for a in (x, rc, entry, exit_, cluster)),
             pltpu.VMEM((width, points), BF16),
             pltpu.VMEM((heads * slices, points), BF16),
-            pltpu.SemaphoreType.DMA((7,)),
         ],
-        space=pltpu.HBM,
-        limit=POINTS_LIMIT,
-    )(tally, sharp, x, rc, entry, exit_, cluster)
+    )(tally, sharp, x, rc, entry, exit_, cluster, opening)
     steps = ((8,), *((mask,) for mask in far), (2, 4, 6), (1,))
     all_points = devices * points
     root_scale = 2.0 ** math.floor(math.log2(65000.0 / math.sqrt(all_points * width * 2.25)))

time: 47.9 us -> 47.4 us (0.990)
  Pallas kernels: 9.93 us -> 8.53 us
  waiting for transfers between devices: 17.2 us -> 17.9 us
    pallas_call x1 -> x2, Pallas kernels: 2.97 us -> 1.54 us  [the longest x1 1.54 us: local(): call(points_kernel, [((token_rows, LANES), BF16)], 2, 8, scratch=[pltpu.V...]
    ppermute x12, waiting for transfers between devices: 17.2 us -> 17.9 us  [exchange(): return lax.ppermute(a, ALL, [(i, i ^ mask) for i in range(devices)])]
    unnamed x18 -> x16, local copies, waits for them, and re-layouts: 0.93 us -> 1.16 us
where the time goes in v4:
time: 47.4 us; the launch traced here: 47.2 us
  starting transfers between devices  18 us (38%)
  waiting for transfers between devices  17.9 us (38%)
  Pallas kernels  8.53 us (18%)
  local copies, waits for them, and re-layouts  1.22 us (3%)
  between operations  0.88 us (2%)
  other arithmetic  0.65 us (1%)
    ppermute x12, starting transfers between devices, exchange(): return lax.ppermute(a, ALL, [(i, i ^ mask) for i in range(devices)])  18 us
    ppermute x12, waiting for transfers between devices, exchange(): return lax.ppermute(a, ALL, [(i, i ^ mask) for i in range(devices)])  17.9 us
    pallas_call x1, Pallas kernels, local(): call(middle_kernel, [((owners // 2 * chunk + extra, width), BF16), ((owne...  3.72 us
    pallas_call x1, Pallas kernels, local(): call(points_kernel, [((token_rows, LANES), BF16)], 2, 8, scratch=[pltpu.V...  1.54 us
    pallas_call x1, Pallas kernels, local(): call(shadow_kernel, [((token_rows, LANES), BF16), ((width, points), BF16)...  1.47 us
    unnamed x16, local copies, waits for them, and re-layouts  1.16 us
    pallas_call x1, Pallas kernels, local(): call(features_kernel, [((points, width), BF16), (maps.shape, F32)], 0, 4)  1.12 us
  transfers between devices with their start and end apart: 12, of which 12 were waited for; matrix products, arithmetic and copies ran while one was open for 0% of the time, Pallas kernels for 5%

profile of v4, /device:TPU:0, one launch (start us, length us, event | category | flops | bytes accessed | tf_op | source)
XLA Modules:
  0.0 47.2 jit_solution(3599675235426745868)
XLA Ops:
  0.7 0.8 %copy-done.2 = bf16[256,256]{1,0:T(8,128)(2,1)S(1)} copy-done((bf16[256,256]{1,0:T(8,128)(2,1)S(1)}, bf16[256,256]{1,0:T(8,128)(2,1)}, u32[]{:S(2)}) %copy-start.2) | copy-done | bytes 131096
  1.9 1.5 %shard_map.120.payload_in = bf16[272,128]{1,0:T(8,128)(2,1)S(1)} custom-call(s32[32]{0:T(128)S(1)} %copy-done.7, f32[8]{0:T(128)S(1)} %copy-done.6, bf16[512,256]{1,0:T(8,128)(2,1)S(1)} %copy-done, bf16[512,256]{1,0:T(8,128)(2,1)S(1)} %copy-done.1, bf16[256,256]{1,0:T(8,128)(2,1)S(1)} %copy-done.2, bf16[256,256]{1,0:T(8,128)(2,1)S(1)} %copy-done.3, ...), custom_call_target="tpu_custom_call" | custom-call | tf_op jit(solution)/shard_map/pallas_call | solution.py:439
  3.4 3.0 %collective-permute-start = (bf16[272,128]{1,0:T(8,128)(2,1)S(1)}, bf16[272,128]{1,0:T(8,128)(2,1)S(1)}, u32[]{:S(2)}, u32[]{:S(2)}) collective-permute-start(bf16[272,128]{1,0:T(8,128)(2,1)S(1)} %shard_map.120.payload_in), channel_id=1, source_target_pairs={{0,8},{1,9},{2,10},{3,11},{4,12},{5,13},{6,14},{7,15},{8,0},{9,1},... | collective-permute-start | bytes 208904 | tf_op jit(solution)/shard_map/ppermute | solution.py:389
  6.4 1.5 %shard_map.121 = (bf16[272,128]{1,0:T(8,128)(2,1)S(1)}, bf16[256,512]{1,0:T(8,128)(2,1)S(1)}, bf16[256,512]{1,0:T(8,128)(2,1)S(1)}, bf16[512,512]{1,0:T(8,128)(2...) custom-call(s32[32]{0:T(128)S(1)} %copy-done.7, ...), custom_call_target="tpu_custom_call" | custom-call | tf_op jit(solution)/shard_map/pallas_call | solution.py:454
  7.9 0.8 %collective-permute-done = bf16[272,128]{1,0:T(8,128)(2,1)S(1)} collective-permute-done((bf16[272,128]{1,0:T(8,128)(2,1)S(1)}, bf16[272,128]{1,0:T(8,128)(2,1)S(1)}, u32[]{:S(2)}, u32[]{:S(2)}) %collective-permute-start) | collective-permute-done | bytes 69664 | tf_op jit(solution)/shard_map/ppermute | solution.py:389
  8.9 3.1 %collective-permute-start.1 = (f16[272,128]{1,0:T(8,128)(2,1)S(1)}, f16[272,128]{1,0:T(8,128)(2,1)S(1)}, u32[]{:S(2)}, u32[]{:S(2)}) collective-permute-start(f16[272,128]{1,0:T(8,128)(2,1)S(1)} %pad_maximum_fusion.2), channel_id=1, source_target_pairs={{0,16},{1,17},{2,18},{3,19},{4,20},{5,21},{6,22},{7,23},{8,24},{9,... | collective-permute-start | bytes 208904 | tf_op jit(solution)/shard_map/ppermute | solution.py:389
  12.0 2.3 %collective-permute-done.1 = f16[272,128]{1,0:T(8,128)(2,1)S(1)} collective-permute-done((f16[272,128]{1,0:T(8,128)(2,1)S(1)}, f16[272,128]{1,0:T(8,128)(2,1)S(1)}, u32[]{:S(2)}, u32[]{:S(2)}) %collective-permute-start.1) | collective-permute-done | bytes 69664 | tf_op jit(solution)/shard_map/ppermute | solution.py:389
  14.5 1.9 %collective-permute-start.2 = (f16[272,128]{1,0:T(8,128)(2,1)S(1)}, f16[272,128]{1,0:T(8,128)(2,1)S(1)}, u32[]{:S(2)}, u32[]{:S(2)}) collective-permute-start(f16[272,128]{1,0:T(8,128)(2,1)S(1)} %pad_maximum_fusion.3), channel_id=1, source_target_pairs={{0,2},{1,3},{2,0},{3,1},{4,6},{5,7},{6,4},{7,5},{8,10},{9,11},{10,... | collective-permute-start | bytes 208904 | tf_op jit(solution)/shard_map/ppermute | solution.py:389
  16.4 1.5 %collective-permute-start.3 = (f16[272,128]{1,0:T(8,128)(2,1)S(1)}, f16[272,128]{1,0:T(8,128)(2,1)S(1)}, u32[]{:S(2)}, u32[]{:S(2)}) collective-permute-start(f16[272,128]{1,0:T(8,128)(2,1)S(1)} %pad_maximum_fusion.3), channel_id=1, source_target_pairs={{0,4},{1,5},{2,6},{3,7},{4,0},{5,1},{6,2},{7,3},{8,12},{9,13},{10,... | collective-permute-start | bytes 208904 | tf_op jit(solution)/shard_map/ppermute | solution.py:389
  18.0 1.6 %collective-permute-done.2 = f16[272,128]{1,0:T(8,128)(2,1)S(1)} collective-permute-done((f16[272,128]{1,0:T(8,128)(2,1)S(1)}, f16[272,128]{1,0:T(8,128)(2,1)S(1)}, u32[]{:S(2)}, u32[]{:S(2)}) %collective-permute-start.2) | collective-permute-done | bytes 69664 | tf_op jit(solution)/shard_map/ppermute | solution.py:389
  19.6 1.1 %collective-permute-done.3 = f16[272,128]{1,0:T(8,128)(2,1)S(1)} collective-permute-done((f16[272,128]{1,0:T(8,128)(2,1)S(1)}, f16[272,128]{1,0:T(8,128)(2,1)S(1)}, u32[]{:S(2)}, u32[]{:S(2)}) %collective-permute-start.3) | collective-permute-done | bytes 69664 | tf_op jit(solution)/shard_map/ppermute | solution.py:389
  20.7 2.4 %collective-permute-done.4 = f16[272,128]{1,0:T(8,128)(2,1)S(1)} collective-permute-done((f16[272,128]{1,0:T(8,128)(2,1)S(1)}, f16[272,128]{1,0:T(8,128)(2,1)S(1)}, u32[]{:S(2)}, u32[]{:S(2)}) %collective-permute-start.4) | collective-permute-done | bytes 69664 | tf_op jit(solution)/shard_map/ppermute | solution.py:389
  23.4 1.3 %collective-permute-done.5.other = f32[272,128]{1,0:T(8,128)S(1)} collective-permute-done((f32[272,128]{1,0:T(8,128)S(1)}, f32[272,128]{1,0:T(8,128)S(1)}, u32[]{:S(2)}, u32[]{:S(2)}) %collective-permute-start.5) | collective-permute-done | bytes 139296 | tf_op jit(solution)/shard_map/ppermute | solution.py:389
  24.7 3.7 %shard_map.122 = (bf16[272,256]{1,0:T(8,128)(2,1)S(1)}, bf16[272,256]{1,0:T(8,128)(2,1)S(1)}, bf16[256,512]{1,0:T(8,128)(2,1)S(1)}, f32[128,128]{1,0:T(8,128)S(1)}, f32[128,384]{1,0:T(8,128)S(1)}) custom-call(f32[8]{0:T(128)S(1)} %copy-done.6, f32[272,128]{1,0:T(8,128)S(1)} %fusion.8.mine, f32[272,128]{1,0:T(8,128)S(1)} %collective-permute-done.5.other, ...), custom_call_target="tpu_custom_call" | custom-call | tf_op jit(solution)/shard_map/pallas_call | solution.py:483
  28.6 1.2 %collective-permute-done.6 = bf16[272,256]{1,0:T(8,128)(2,1)S(1)} collective-permute-done((bf16[272,256]{1,0:T(8,128)(2,1)S(1)}, bf16[272,256]{1,0:T(8,128)(2,1)S(1)}, u32[]{:S(2)}, u32[]{:S(2)}) %collective-permute-start.6) | collective-permute-done | bytes 139296 | tf_op jit(solution)/shard_map/ppermute | solution.py:389
  31.4 2.2 %collective-permute-start.9 = (bf16[144,256]{1,0:T(8,128)(2,1)S(1)}, bf16[144,256]{1,0:T(8,128)(2,1)S(1)}, u32[]{:S(2)}, u32[]{:S(2)}) collective-permute-start(bf16[144,256]{1,0:T(8,128)(2,1)S(1)} %get-tuple-element.54), channel_id=1, source_target_pairs={{0,6},{1,7},{2,4},{3,5},{4,2},{5,3},{6,0},{7,1},{8,14},{9,15},{10,... | collective-permute-start | bytes 221192 | tf_op jit(solution)/shard_map/ppermute | solution.py:389
  33.6 1.1 %collective-permute-done.7 = bf16[144,256]{1,0:T(8,128)(2,1)S(1)} collective-permute-done((bf16[144,256]{1,0:T(8,128)(2,1)S(1)}, bf16[144,256]{1,0:T(8,128)(2,1)S(1)}, u32[]{:S(2)}, u32[]{:S(2)}) %collective-permute-start.7) | collective-permute-done | bytes 73760 | tf_op jit(solution)/shard_map/ppermute | solution.py:389
  34.6 1.1 %collective-permute-done.8 = bf16[144,256]{1,0:T(8,128)(2,1)S(1)} collective-permute-done((bf16[144,256]{1,0:T(8,128)(2,1)S(1)}, bf16[144,256]{1,0:T(8,128)(2,1)S(1)}, u32[]{:S(2)}, u32[]{:S(2)}) %collective-permute-start.8) | collective-permute-done | bytes 73760 | tf_op jit(solution)/shard_map/ppermute | solution.py:389
  35.7 0.9 %collective-permute-done.9 = bf16[144,256]{1,0:T(8,128)(2,1)S(1)} collective-permute-done((bf16[144,256]{1,0:T(8,128)(2,1)S(1)}, bf16[144,256]{1,0:T(8,128)(2,1)S(1)}, u32[]{:S(2)}, u32[]{:S(2)}) %collective-permute-start.9) | collective-permute-done | bytes 73760 | tf_op jit(solution)/shard_map/ppermute | solution.py:389
  36.7 1.6 %collective-permute-start.10 = (bf16[144,256]{1,0:T(8,128)(2,1)S(1)}, bf16[144,256]{1,0:T(8,128)(2,1)S(1)}, u32[]{:S(2)}, u32[]{:S(2)}) collective-permute-start(bf16[144,256]{1,0:T(8,128)(2,1)S(1)} %maximum_maximum_fusion.1), channel_id=1, source_target_pairs={{0,8},{1,9},{2,10},{3,11},{4,12},{5,13},{6,14},{7,15},{8,0},{9,1},... | collective-permute-start | bytes 221192 | tf_op jit(solution)/shard_map/ppermute | solution.py:389
  38.4 2.8 %collective-permute-done.10 = bf16[144,256]{1,0:T(8,128)(2,1)S(1)} collective-permute-done((bf16[144,256]{1,0:T(8,128)(2,1)S(1)}, bf16[144,256]{1,0:T(8,128)(2,1)S(1)}, u32[]{:S(2)}, u32[]{:S(2)}) %collective-permute-start.10) | collective-permute-done | bytes 73760 | tf_op jit(solution)/shard_map/ppermute | solution.py:389
  41.2 2.8 %collective-permute-start.11 = (bf16[144,256]{1,0:T(8,128)(2,1)S(1)}, bf16[144,256]{1,0:T(8,128)(2,1)S(1)}, u32[]{:S(2)}, u32[]{:S(2)}) collective-permute-start(bf16[144,256]{1,0:T(8,128)(2,1)S(1)} %maximum_maximum_fusion.2.mine), channel_id=1, source_target_pairs={{0,16},{1,17},{2,18},{3,19},{4,20},{5,21},{6,22},{7,23},{8,24},{9,... | collective-permute-start | bytes 221192 | tf_op jit(solution)/shard_map/ppermute | solution.py:389
  44.0 1.1 %shard_map.123 = (bf16[512,256]{1,0:T(8,128)(2,1)}, f32[3,32,32]{2,1,0:T(8,128)}) custom-call(bf16[256,512]{1,0:T(8,128)(2,1)S(1)} %get-tuple-element.31.gxmt, bf16[256,256]{1,0:T(8,128)(2,1)S(1)} %copy-done.2, f32[128,128]{1,0:T(8,128)S(1)} %get-tuple-element.32.tokens, f32[128,384]{1,0:T(8,128)S(1)} %get-tuple-element.33.grads), custom_call_target="tpu_custom_call" | custom-call | tf_op jit(solution)/shard_map/pallas_call | solution.py:511
  45.2 1.4 %collective-permute-done.11.other = bf16[144,256]{1,0:T(8,128)(2,1)S(1)} collective-permute-done((bf16[144,256]{1,0:T(8,128)(2,1)S(1)}, bf16[144,256]{1,0:T(8,128)(2,1)S(1)}, u32[]{:S(2)}, u32[]{:S(2)}) %collective-permute-start.11) | collective-permute-done | bytes 73760 | tf_op jit(solution)/shard_map/ppermute | solution.py:389
  (47 shorter events, 3.5 us)
Async XLA Ops:
  0.6 0.9 %copy-start.2 = (bf16[256,256]{1,0:T(8,128)(2,1)S(1)}, bf16[256,256]{1,0:T(8,128)(2,1)}, u32[]{:S(2)}) copy-start(bf16[256,256]{1,0:T(8,128)(2,1)} %entry.5) | copy-start | bytes 393220
  0.6 1.0 %copy-start.3 = (bf16[256,256]{1,0:T(8,128)(2,1)S(1)}, bf16[256,256]{1,0:T(8,128)(2,1)}, u32[]{:S(2)}) copy-start(bf16[256,256]{1,0:T(8,128)(2,1)} %exit_.3) | copy-start | bytes 393220
  0.7 1.0 %copy-start.5 = (bf16[32,64]{1,0:T(8,128)(2,1)S(1)}, bf16[32,64]{1,0:T(8,128)(2,1)}, u32[]{:S(2)}) copy-start(bf16[32,64]{1,0:T(8,128)(2,1)} %cluster.3) | copy-start | bytes 12292
  0.7 0.9 %copy-start.6 = (f32[8]{0:T(128)S(1)}, f32[8]{0:T(128)}, u32[]{:S(2)}) copy-start(f32[8]{0:T(128)} %sharp.5) | copy-start | bytes 100
  0.7 0.9 %copy-start.7 = (s32[32]{0:T(128)S(1)}, s32[32]{0:T(128)}, u32[]{:S(2)}) copy-start(s32[32]{0:T(128)} %tally.3) | copy-start | bytes 388
  0.7 1.1 %copy-start = (bf16[512,256]{1,0:T(8,128)(2,1)S(1)}, bf16[512,256]{1,0:T(8,128)(2,1)}, u32[]{:S(2)}) copy-start(bf16[512,256]{1,0:T(8,128)(2,1)} %x.5) | copy-start | bytes 786436
  0.7 1.2 %copy-start.1 = (bf16[512,256]{1,0:T(8,128)(2,1)S(1)}, bf16[512,256]{1,0:T(8,128)(2,1)}, u32[]{:S(2)}) copy-start(bf16[512,256]{1,0:T(8,128)(2,1)} %rc.5) | copy-start | bytes 786436
  1.9 4.6 %copy-start.4 = (f32[3,32,32]{2,1,0:T(8,128)S(1)}, f32[3,32,32]{2,1,0:T(8,128)}, u32[]{:S(2)}) copy-start(f32[3,32,32]{2,1,0:T(8,128)} %maps.1) | copy-start | bytes 36868
  3.4 5.3 %collective-permute-start = (bf16[272,128]{1,0:T(8,128)(2,1)S(1)}, bf16[272,128]{1,0:T(8,128)(2,1)S(1)}, u32[]{:S(2)}, u32[]{:S(2)}) collective-permute-start(bf16[272,128]{1,0:T(8,128)(2,1)S(1)} %shard_map.120.payload_in), channel_id=1, source_target_pairs={{0,8},{1,9},{2,10},{3,11},{4,12},{5,13},{6,14},{7,15},{8,0},{9,1},... | collective-permute-start | bytes 208904 | tf_op jit(solution)/shard_map/ppermute | solution.py:389
  8.9 5.4 %collective-permute-start.1 = (f16[272,128]{1,0:T(8,128)(2,1)S(1)}, f16[272,128]{1,0:T(8,128)(2,1)S(1)}, u32[]{:S(2)}, u32[]{:S(2)}) collective-permute-start(f16[272,128]{1,0:T(8,128)(2,1)S(1)} %pad_maximum_fusion.2), channel_id=1, source_target_pairs={{0,16},{1,17},{2,18},{3,19},{4,20},{5,21},{6,22},{7,23},{8,24},{9,... | collective-permute-start | bytes 208904 | tf_op jit(solution)/shard_map/ppermute | solution.py:389
  14.5 5.1 %collective-permute-start.2 = (f16[272,128]{1,0:T(8,128)(2,1)S(1)}, f16[272,128]{1,0:T(8,128)(2,1)S(1)}, u32[]{:S(2)}, u32[]{:S(2)}) collective-permute-start(f16[272,128]{1,0:T(8,128)(2,1)S(1)} %pad_maximum_fusion.3), channel_id=1, source_target_pairs={{0,2},{1,3},{2,0},{3,1},{4,6},{5,7},{6,4},{7,5},{8,10},{9,11},{10,... | collective-permute-start | bytes 208904 | tf_op jit(solution)/shard_map/ppermute | solution.py:389
  16.4 4.3 %collective-permute-start.3 = (f16[272,128]{1,0:T(8,128)(2,1)S(1)}, f16[272,128]{1,0:T(8,128)(2,1)S(1)}, u32[]{:S(2)}, u32[]{:S(2)}) collective-permute-start(f16[272,128]{1,0:T(8,128)(2,1)S(1)} %pad_maximum_fusion.3), channel_id=1, source_target_pairs={{0,4},{1,5},{2,6},{3,7},{4,0},{5,1},{6,2},{7,3},{8,12},{9,13},{10,... | collective-permute-start | bytes 208904 | tf_op jit(solution)/shard_map/ppermute | solution.py:389
  17.9 5.2 %collective-permute-start.4 = (f16[272,128]{1,0:T(8,128)(2,1)S(1)}, f16[272,128]{1,0:T(8,128)(2,1)S(1)}, u32[]{:S(2)}, u32[]{:S(2)}) collective-permute-start(f16[272,128]{1,0:T(8,128)(2,1)S(1)} %pad_maximum_fusion.3), channel_id=1, source_target_pairs={{0,6},{1,7},{2,4},{3,5},{4,2},{5,3},{6,0},{7,1},{8,14},{9,15},{10,... | collective-permute-start | bytes 208904 | tf_op jit(solution)/shard_map/ppermute | solution.py:389
  23.3 1.4 %collective-permute-start.5 = (f32[272,128]{1,0:T(8,128)S(1)}, f32[272,128]{1,0:T(8,128)S(1)}, u32[]{:S(2)}, u32[]{:S(2)}) collective-permute-start(f32[272,128]{1,0:T(8,128)S(1)} %fusion.8.mine), channel_id=1, source_target_pairs={{0,1},{1,0},{2,3},{3,2},{4,5},{5,4},{6,7},{7,6},{8,9},{9,8},{10,11... | collective-permute-start | bytes 417800 | tf_op jit(solution)/shard_map/ppermute | solution.py:389
  28.4 1.4 %collective-permute-start.6 = (bf16[272,256]{1,0:T(8,128)(2,1)S(1)}, bf16[272,256]{1,0:T(8,128)(2,1)S(1)}, u32[]{:S(2)}, u32[]{:S(2)}) collective-permute-start(bf16[272,256]{1,0:T(8,128)(2,1)S(1)} %get-tuple-element.36), channel_id=1, source_target_pairs={{0,1},{1,0},{2,3},{3,2},{4,5},{5,4},{6,7},{7,6},{8,9},{9,8},{10,11... | collective-permute-start | bytes 417800 | tf_op jit(solution)/shard_map/ppermute | solution.py:389
  30.0 4.6 %collective-permute-start.7 = (bf16[144,256]{1,0:T(8,128)(2,1)S(1)}, bf16[144,256]{1,0:T(8,128)(2,1)S(1)}, u32[]{:S(2)}, u32[]{:S(2)}) collective-permute-start(bf16[144,256]{1,0:T(8,128)(2,1)S(1)} %get-tuple-element.53), channel_id=1, source_target_pairs={{0,4},{1,5},{2,6},{3,7},{4,0},{5,1},{6,2},{7,3},{8,12},{9,13},{10,... | collective-permute-start | bytes 221192 | tf_op jit(solution)/shard_map/ppermute | solution.py:389
  30.6 5.1 %collective-permute-start.8 = (bf16[144,256]{1,0:T(8,128)(2,1)S(1)}, bf16[144,256]{1,0:T(8,128)(2,1)S(1)}, u32[]{:S(2)}, u32[]{:S(2)}) collective-permute-start(bf16[144,256]{1,0:T(8,128)(2,1)S(1)} %get-tuple-element.54), channel_id=1, source_target_pairs={{0,2},{1,3},{2,0},{3,1},{4,6},{5,7},{6,4},{7,5},{8,10},{9,11},{10,... | collective-permute-start | bytes 221192 | tf_op jit(solution)/shard_map/ppermute | solution.py:389
  31.4 5.3 %collective-permute-start.9 = (bf16[144,256]{1,0:T(8,128)(2,1)S(1)}, bf16[144,256]{1,0:T(8,128)(2,1)S(1)}, u32[]{:S(2)}, u32[]{:S(2)}) collective-permute-start(bf16[144,256]{1,0:T(8,128)(2,1)S(1)} %get-tuple-element.54), channel_id=1, source_target_pairs={{0,6},{1,7},{2,4},{3,5},{4,2},{5,3},{6,0},{7,1},{8,14},{9,15},{10,... | collective-permute-start | bytes 221192 | tf_op jit(solution)/shard_map/ppermute | solution.py:389
  36.7 4.4 %collective-permute-start.10 = (bf16[144,256]{1,0:T(8,128)(2,1)S(1)}, bf16[144,256]{1,0:T(8,128)(2,1)S(1)}, u32[]{:S(2)}, u32[]{:S(2)}) collective-permute-start(bf16[144,256]{1,0:T(8,128)(2,1)S(1)} %maximum_maximum_fusion.1), channel_id=1, source_target_pairs={{0,8},{1,9},{2,10},{3,11},{4,12},{5,13},{6,14},{7,15},{8,0},{9,1},... | collective-permute-start | bytes 221192 | tf_op jit(solution)/shard_map/ppermute | solution.py:389
  41.2 5.3 %collective-permute-start.11 = (bf16[144,256]{1,0:T(8,128)(2,1)S(1)}, bf16[144,256]{1,0:T(8,128)(2,1)S(1)}, u32[]{:S(2)}, u32[]{:S(2)}) collective-permute-start(bf16[144,256]{1,0:T(8,128)(2,1)S(1)} %maximum_maximum_fusion.2.mine), channel_id=1, source_target_pairs={{0,16},{1,17},{2,18},{3,19},{4,20},{5,21},{6,22},{7,23},{8,24},{9,... | collective-permute-start | bytes 221192 | tf_op jit(solution)/shard_map/ppermute | solution.py:389

commit v5 on v4

--- a/solution.py
+++ b/solution.py
@@ -1,3 +1,4 @@
+import functools
 import math
 
 import jax
@@ -401,13 +402,10 @@
 
 
 def token_pack(values, start, root_scale, den_scale):
-    sums, pair = values[:start], values[start:]
-    n = pair.shape[0] // 2
-    pair = (pair[:n] + pair[n:]) * den_scale
-    high = lax.reduce_precision(pair, 8, 7)
-    roots = jnp.sqrt(jnp.abs(sums)) * root_scale
-    roots = jnp.where(sums < 0.0, -roots, roots)
-    return jnp.concatenate([roots, high, pair - high], axis=0).astype(jnp.float16)
+    row = lax.broadcasted_iota(jnp.int32, values.shape, 0)
+    roots = jnp.sqrt(jnp.abs(values)) * root_scale
+    roots = jnp.where(values < 0.0, -roots, roots)
+    return jnp.where(row < start, roots, values * den_scale).astype(jnp.float16)
 
 
 def token_unpack(packed, start, root_scale, den_scale):
@@ -416,13 +414,30 @@
     return packed * jnp.where(row < start, jnp.abs(packed) * root_scale**-2, 1.0 / den_scale)
 
 
-def halves(total, start):
+def store_halves(total, start, target):
     pair = total[start:]
     n = pair.shape[1] // 2
     pair = pair[:, :n] + pair[:, n:]
-    high = lax.reduce_precision(pair, 8, 7)
+    high = pair.astype(BF16).astype(F32)
     pair = jnp.concatenate([high, pair - high], axis=1)
-    return jnp.concatenate([total[:start], pair], axis=0).astype(BF16)
+    target[...] = jnp.concatenate([total[:start], pair], axis=0).astype(BF16)
+
+
+def sum_kernel(heads, *refs):
+    *given, target = refs
+    total = gather(given[0][...], [a[...] for a in given[1:]])
+    store_halves(total, total.shape[0] - heads, target)
+
+
+def part_kernel(heads, chunk, keep, other, mine, theirs):
+    half = lax.axis_index("grp") // 2
+    common = keep.shape[0] - mine.shape[0] + chunk
+    extra = keep[common:, :].astype(F32) + other[common:, :].astype(F32)
+    for target, index in ((mine, half), (theirs, 1 - half)):
+        rows = pl.ds(pl.multiple_of(index * chunk, chunk), chunk)
+        own = keep[rows, :].astype(F32) + other[rows, :].astype(F32)
+        total = jnp.concatenate([own, extra], axis=0)
+        store_halves(total, total.shape[0] - heads, target)
 
 
 def local(x, rc, entry, exit_, cluster, sharp, maps, tally):
@@ -514,23 +529,17 @@
         0,
         4,
     )(gxmt, entry, tokens, grads)
-    total = keep.astype(F32) + got_half.astype(F32)
-    total = halves(total, total.shape[0] - heads)
-    half = lax.axis_index("grp") // 2
-    common = total[owners // 2 * chunk :]
-    mine = jnp.concatenate(
-        [lax.dynamic_slice_in_dim(total, half * chunk, chunk), common], axis=0
-    )
-    theirs = jnp.concatenate(
-        [lax.dynamic_slice_in_dim(total, (1 - half) * chunk, chunk), common], axis=0
-    )
+    part_shape = ((chunk + extra, width), BF16)
+    mine, theirs = call(
+        functools.partial(part_kernel, heads, chunk), [part_shape, part_shape], 0, 2
+    )(keep, got_half)
     others = [exchange(mine, 4), exchange(theirs, 2), exchange(theirs, 6)]
-    total = gather(mine, others)
-    mine = halves(total, total.shape[0] - heads)
-    for mask in (8, *far[:-1]):
-        total = gather(mine, exchanges(mine, (mask,)))
-        mine = halves(total, total.shape[0] - heads)
-    other = exchange(mine, far[-1])
+    for mask in (8, *far):
+        (mine,) = call(
+            functools.partial(sum_kernel, heads), [part_shape], 0, 1 + len(others)
+        )(mine, *others)
+        others = exchanges(mine, (mask,))
+    (other,) = others
     weight_grads, slice_grad, temp_grad = call(
         finish_kernel,
         [

time: 47.4 us -> 46.8 us (0.987)
  transfers between devices with their start and end apart: 12 -> 12, of which waited for: 12 -> 12; matrix products, arithmetic and copies ran while one was open for 0% -> 0% of each run, Pallas kernels for 5% -> 6%
where the time goes in v5:
time: 46.8 us; the launch traced here: 46.6 us
  starting transfers between devices  18.2 us (39%)
  waiting for transfers between devices  17.5 us (37%)
  Pallas kernels  8.64 us (18%)
  local copies, waits for them, and re-layouts  1.12 us (2%)
  between operations  0.76 us (2%)
    ppermute x12, starting transfers between devices, exchange(): return lax.ppermute(a, ALL, [(i, i ^ mask) for i in range(devices)])  18.2 us
    ppermute x12, waiting for transfers between devices, exchange(): return lax.ppermute(a, ALL, [(i, i ^ mask) for i in range(devices)])  17.5 us
    pallas_call x1, Pallas kernels, local(): call(middle_kernel, [((owners // 2 * chunk + extra, width), BF16), ((owne...  3.72 us
    pallas_call x1, Pallas kernels, local(): call(points_kernel, [((token_rows, LANES), BF16)], 2, 8, scratch=[pltpu.V...  1.54 us
    pallas_call x1, Pallas kernels, local(): call(shadow_kernel, [((token_rows, LANES), BF16), ((width, points), BF16)...  1.47 us
    unnamed x16, local copies, waits for them, and re-layouts  1.12 us
    pallas_call x1, Pallas kernels, local(): call(features_kernel, [((points, width), BF16), (maps.shape, F32)], 0, 4)  1.12 us
  transfers between devices with their start and end apart: 12, of which 12 were waited for; matrix products, arithmetic and copies ran while one was open for 0% of the time, Pallas kernels for 6%

profile of v5, /device:TPU:0, one launch (start us, length us, event | category | flops | bytes accessed | tf_op | source)
XLA Modules:
  0.0 46.6 jit_solution(1175977320431032711)
XLA Ops:
  0.7 0.6 %copy-done.6 = f32[8]{0:T(128)S(1)} copy-done((f32[8]{0:T(128)S(1)}, f32[8]{0:T(128)}, u32[]{:S(2)}) %copy-start.6) | copy-done | bytes 56
  1.8 1.5 %shard_map.120.payload_in = bf16[272,128]{1,0:T(8,128)(2,1)S(1)} custom-call(s32[32]{0:T(128)S(1)} %copy-done.7, f32[8]{0:T(128)S(1)} %copy-done.6, bf16[512,256]{1,0:T(8,128)(2,1)S(1)} %copy-done, bf16[512,256]{1,0:T(8,128)(2,1)S(1)} %copy-done.1, bf16[256,256]{1,0:T(8,128)(2,1)S(1)} %copy-done.2, bf16[256,256]{1,0:T(8,128)(2,1)S(1)} %copy-done.3, ...), custom_call_target="tpu_custom_call" | custom-call | tf_op jit(solution)/shard_map/pallas_call | solution.py:454
  3.4 3.0 %collective-permute-start = (bf16[272,128]{1,0:T(8,128)(2,1)S(1)}, bf16[272,128]{1,0:T(8,128)(2,1)S(1)}, u32[]{:S(2)}, u32[]{:S(2)}) collective-permute-start(bf16[272,128]{1,0:T(8,128)(2,1)S(1)} %shard_map.120.payload_in), channel_id=1, source_target_pairs={{0,8},{1,9},{2,10},{3,11},{4,12},{5,13},{6,14},{7,15},{8,0},{9,1},... | collective-permute-start | bytes 208904 | tf_op jit(solution)/shard_map/ppermute | solution.py:390
  6.4 1.5 %shard_map.121 = (bf16[272,128]{1,0:T(8,128)(2,1)S(1)}, bf16[256,512]{1,0:T(8,128)(2,1)S(1)}, bf16[256,512]{1,0:T(8,128)(2,1)S(1)}, bf16[512,512]{1,0:T(8,128)(2...) custom-call(s32[32]{0:T(128)S(1)} %copy-done.7, ...), custom_call_target="tpu_custom_call" | custom-call | tf_op jit(solution)/shard_map/pallas_call | solution.py:469
  7.9 0.8 %collective-permute-done = bf16[272,128]{1,0:T(8,128)(2,1)S(1)} collective-permute-done((bf16[272,128]{1,0:T(8,128)(2,1)S(1)}, bf16[272,128]{1,0:T(8,128)(2,1)S(1)}, u32[]{:S(2)}, u32[]{:S(2)}) %collective-permute-start) | collective-permute-done | bytes 69664 | tf_op jit(solution)/shard_map/ppermute | solution.py:390
  8.8 3.1 %collective-permute-start.1 = (f16[272,128]{1,0:T(8,128)(2,1)S(1)}, f16[272,128]{1,0:T(8,128)(2,1)S(1)}, u32[]{:S(2)}, u32[]{:S(2)}) collective-permute-start(f16[272,128]{1,0:T(8,128)(2,1)S(1)} %fusion.17), channel_id=1, source_target_pairs={{0,16},{1,17},{2,18},{3,19},{4,20},{5,21},{6,22},{7,23},{8,24},{9,... | collective-permute-start | bytes 208904 | tf_op jit(solution)/shard_map/ppermute | solution.py:390
  11.9 2.3 %collective-permute-done.1 = f16[272,128]{1,0:T(8,128)(2,1)S(1)} collective-permute-done((f16[272,128]{1,0:T(8,128)(2,1)S(1)}, f16[272,128]{1,0:T(8,128)(2,1)S(1)}, u32[]{:S(2)}, u32[]{:S(2)}) %collective-permute-start.1) | collective-permute-done | bytes 69664 | tf_op jit(solution)/shard_map/ppermute | solution.py:390
  14.4 2.8 %collective-permute-start.4 = (f16[272,128]{1,0:T(8,128)(2,1)S(1)}, f16[272,128]{1,0:T(8,128)(2,1)S(1)}, u32[]{:S(2)}, u32[]{:S(2)}) collective-permute-start(f16[272,128]{1,0:T(8,128)(2,1)S(1)} %fusion.19), channel_id=1, source_target_pairs={{0,6},{1,7},{2,4},{3,5},{4,2},{5,3},{6,0},{7,1},{8,14},{9,15},{10,... | collective-permute-start | bytes 208904 | tf_op jit(solution)/shard_map/ppermute | solution.py:390
  17.2 0.5 %collective-permute-start.3 = (f16[272,128]{1,0:T(8,128)(2,1)S(1)}, f16[272,128]{1,0:T(8,128)(2,1)S(1)}, u32[]{:S(2)}, u32[]{:S(2)}) collective-permute-start(f16[272,128]{1,0:T(8,128)(2,1)S(1)} %fusion.19), channel_id=1, source_target_pairs={{0,4},{1,5},{2,6},{3,7},{4,0},{5,1},{6,2},{7,3},{8,12},{9,13},{10,... | collective-permute-start | bytes 208904 | tf_op jit(solution)/shard_map/ppermute | solution.py:390
  17.9 1.7 %collective-permute-done.4 = f16[272,128]{1,0:T(8,128)(2,1)S(1)} collective-permute-done((f16[272,128]{1,0:T(8,128)(2,1)S(1)}, f16[272,128]{1,0:T(8,128)(2,1)S(1)}, u32[]{:S(2)}, u32[]{:S(2)}) %collective-permute-start.4) | collective-permute-done | bytes 69664 | tf_op jit(solution)/shard_map/ppermute | solution.py:390
  19.6 1.9 %collective-permute-done.3 = f16[272,128]{1,0:T(8,128)(2,1)S(1)} collective-permute-done((f16[272,128]{1,0:T(8,128)(2,1)S(1)}, f16[272,128]{1,0:T(8,128)(2,1)S(1)}, u32[]{:S(2)}, u32[]{:S(2)}) %collective-permute-start.3) | collective-permute-done | bytes 69664 | tf_op jit(solution)/shard_map/ppermute | solution.py:390
  22.3 1.3 %collective-permute-done.5.other = f32[272,128]{1,0:T(8,128)S(1)} collective-permute-done((f32[272,128]{1,0:T(8,128)S(1)}, f32[272,128]{1,0:T(8,128)S(1)}, u32[]{:S(2)}, u32[]{:S(2)}) %collective-permute-start.5) | collective-permute-done | bytes 139296 | tf_op jit(solution)/shard_map/ppermute | solution.py:390
  23.6 3.7 %shard_map.122 = (bf16[272,256]{1,0:T(8,128)(2,1)S(1)}, bf16[272,256]{1,0:T(8,128)(2,1)S(1)}, bf16[256,512]{1,0:T(8,128)(2,1)S(1)}, f32[128,128]{1,0:T(8,128)S(1)}, f32[128,384]{1,0:T(8,128)S(1)}) custom-call(f32[8]{0:T(128)S(1)} %copy-done.6, f32[272,128]{1,0:T(8,128)S(1)} %fusion.8.mine, f32[272,128]{1,0:T(8,128)S(1)} %collective-permute-done.5.other, ...), custom_call_target="tpu_custom_call" | custom-call | tf_op jit(solution)/shard_map/pallas_call | solution.py:498
  27.6 1.2 %collective-permute-done.6.other = bf16[272,256]{1,0:T(8,128)(2,1)S(1)} collective-permute-done((bf16[272,256]{1,0:T(8,128)(2,1)S(1)}, bf16[272,256]{1,0:T(8,128)(2,1)S(1)}, u32[]{:S(2)}, u32[]{:S(2)}) %collective-permute-start.6) | collective-permute-done | bytes 139296 | tf_op jit(solution)/shard_map/ppermute | solution.py:390
  28.8 1.6 %collective-permute-start.7 = (bf16[144,256]{1,0:T(8,128)(2,1)S(1)}, bf16[144,256]{1,0:T(8,128)(2,1)S(1)}, u32[]{:S(2)}, u32[]{:S(2)}) collective-permute-start(bf16[144,256]{1,0:T(8,128)(2,1)S(1)} %get-tuple-element.39.refs_0_), channel_id=1, source_target_pairs={{0,4},{1,5},{2,6},{3,7},{4,0},{5,1},{6,2},{7,3},{8,12},{9,13},{10,... | collective-permute-start | bytes 221192 | tf_op jit(solution)/shard_map/ppermute | solution.py:390
  30.6 1.8 %collective-permute-start.8 = (bf16[144,256]{1,0:T(8,128)(2,1)S(1)}, bf16[144,256]{1,0:T(8,128)(2,1)S(1)}, u32[]{:S(2)}, u32[]{:S(2)}) collective-permute-start(bf16[144,256]{1,0:T(8,128)(2,1)S(1)} %get-tuple-element.40), channel_id=1, source_target_pairs={{0,2},{1,3},{2,0},{3,1},{4,6},{5,7},{6,4},{7,5},{8,10},{9,11},{10,... | collective-permute-start | bytes 221192 | tf_op jit(solution)/shard_map/ppermute | solution.py:390
  32.4 1.3 %collective-permute-done.7.refs_1_ = bf16[144,256]{1,0:T(8,128)(2,1)S(1)} collective-permute-done((bf16[144,256]{1,0:T(8,128)(2,1)S(1)}, bf16[144,256]{1,0:T(8,128)(2,1)S(1)}, u32[]{:S(2)}, u32[]{:S(2)}) %collective-permute-start.7) | collective-permute-done | bytes 73760 | tf_op jit(solution)/shard_map/ppermute | solution.py:390
  33.7 2.0 %collective-permute-done.9.refs_3_ = bf16[144,256]{1,0:T(8,128)(2,1)S(1)} collective-permute-done((bf16[144,256]{1,0:T(8,128)(2,1)S(1)}, bf16[144,256]{1,0:T(8,128)(2,1)S(1)}, u32[]{:S(2)}, u32[]{:S(2)}) %collective-permute-start.9) | collective-permute-done | bytes 73760 | tf_op jit(solution)/shard_map/ppermute | solution.py:390
  36.2 1.7 %collective-permute-start.10 = (bf16[144,256]{1,0:T(8,128)(2,1)S(1)}, bf16[144,256]{1,0:T(8,128)(2,1)S(1)}, u32[]{:S(2)}, u32[]{:S(2)}) collective-permute-start(bf16[144,256]{1,0:T(8,128)(2,1)S(1)} %shard_map.125.refs_0_), channel_id=1, source_target_pairs={{0,8},{1,9},{2,10},{3,11},{4,12},{5,13},{6,14},{7,15},{8,0},{9,1},... | collective-permute-start | bytes 221192 | tf_op jit(solution)/shard_map/ppermute | solution.py:390
  37.9 2.7 %collective-permute-done.10.refs_1_ = bf16[144,256]{1,0:T(8,128)(2,1)S(1)} collective-permute-done((bf16[144,256]{1,0:T(8,128)(2,1)S(1)}, bf16[144,256]{1,0:T(8,128)(2,1)S(1)}, u32[]{:S(2)}, u32[]{:S(2)}) %collective-permute-start.10) | collective-permute-done | bytes 73760 | tf_op jit(solution)/shard_map/ppermute | solution.py:390
  40.6 2.9 %collective-permute-start.11 = (bf16[144,256]{1,0:T(8,128)(2,1)S(1)}, bf16[144,256]{1,0:T(8,128)(2,1)S(1)}, u32[]{:S(2)}, u32[]{:S(2)}) collective-permute-start(bf16[144,256]{1,0:T(8,128)(2,1)S(1)} %shard_map.126.mine), channel_id=1, source_target_pairs={{0,16},{1,17},{2,18},{3,19},{4,20},{5,21},{6,22},{7,23},{8,24},{9,... | collective-permute-start | bytes 221192 | tf_op jit(solution)/shard_map/ppermute | solution.py:390
  43.6 1.1 %shard_map.123 = (bf16[512,256]{1,0:T(8,128)(2,1)}, f32[3,32,32]{2,1,0:T(8,128)}) custom-call(bf16[256,512]{1,0:T(8,128)(2,1)S(1)} %get-tuple-element.33.gxmt, bf16[256,256]{1,0:T(8,128)(2,1)S(1)} %copy-done.2, f32[128,128]{1,0:T(8,128)S(1)} %get-tuple-element.34.tokens, f32[128,384]{1,0:T(8,128)S(1)} %get-tuple-element.35.grads), custom_call_target="tpu_custom_call" | custom-call | tf_op jit(solution)/shard_map/pallas_call | solution.py:526
  44.7 1.3 %collective-permute-done.11.other = bf16[144,256]{1,0:T(8,128)(2,1)S(1)} collective-permute-done((bf16[144,256]{1,0:T(8,128)(2,1)S(1)}, bf16[144,256]{1,0:T(8,128)(2,1)S(1)}, u32[]{:S(2)}, u32[]{:S(2)}) %collective-permute-start.11) | collective-permute-done | bytes 73760 | tf_op jit(solution)/shard_map/ppermute | solution.py:390
  45.9 0.7 %shard_map.127 = (f32[2,64,256]{2,1,0:T(8,128)}, f32[32,64]{1,0:T(8,128)}, f32[1,8]{1,0:T(1,128)}) custom-call(bf16[144,256]{1,0:T(8,128)(2,1)S(1)} %shard_map.126.mine, bf16[144,256]{1,0:T(8,128)(2,1)S(1)} %collective-permute-done.11.other), custom_call_target="tpu_custom_call" | custom-call | tf_op jit(solution)/shard_map/pallas_call | solution.py:543
  (29 shorter events, 2.7 us)
Async XLA Ops:
  0.6 0.7 %copy-start.6 = (f32[8]{0:T(128)S(1)}, f32[8]{0:T(128)}, u32[]{:S(2)}) copy-start(f32[8]{0:T(128)} %sharp.5) | copy-start | bytes 100
  0.6 0.9 %copy-start.2 = (bf16[256,256]{1,0:T(8,128)(2,1)S(1)}, bf16[256,256]{1,0:T(8,128)(2,1)}, u32[]{:S(2)}) copy-start(bf16[256,256]{1,0:T(8,128)(2,1)} %entry.5) | copy-start | bytes 393220
  0.7 1.0 %copy-start.1 = (bf16[512,256]{1,0:T(8,128)(2,1)S(1)}, bf16[512,256]{1,0:T(8,128)(2,1)}, u32[]{:S(2)}) copy-start(bf16[512,256]{1,0:T(8,128)(2,1)} %rc.5) | copy-start | bytes 786436
  0.7 1.1 %copy-start = (bf16[512,256]{1,0:T(8,128)(2,1)S(1)}, bf16[512,256]{1,0:T(8,128)(2,1)}, u32[]{:S(2)}) copy-start(bf16[512,256]{1,0:T(8,128)(2,1)} %x.5) | copy-start | bytes 786436
  0.7 1.1 %copy-start.7 = (s32[32]{0:T(128)S(1)}, s32[32]{0:T(128)}, u32[]{:S(2)}) copy-start(s32[32]{0:T(128)} %tally.3) | copy-start | bytes 388
  0.7 1.1 %copy-start.5 = (bf16[32,64]{1,0:T(8,128)(2,1)S(1)}, bf16[32,64]{1,0:T(8,128)(2,1)}, u32[]{:S(2)}) copy-start(bf16[32,64]{1,0:T(8,128)(2,1)} %cluster.3) | copy-start | bytes 12292
  0.7 1.1 %copy-start.3 = (bf16[256,256]{1,0:T(8,128)(2,1)S(1)}, bf16[256,256]{1,0:T(8,128)(2,1)}, u32[]{:S(2)}) copy-start(bf16[256,256]{1,0:T(8,128)(2,1)} %exit_.3) | copy-start | bytes 393220
  1.8 4.6 %copy-start.4 = (f32[3,32,32]{2,1,0:T(8,128)S(1)}, f32[3,32,32]{2,1,0:T(8,128)}, u32[]{:S(2)}) copy-start(f32[3,32,32]{2,1,0:T(8,128)} %maps.1) | copy-start | bytes 36868
  3.4 5.3 %collective-permute-start = (bf16[272,128]{1,0:T(8,128)(2,1)S(1)}, bf16[272,128]{1,0:T(8,128)(2,1)S(1)}, u32[]{:S(2)}, u32[]{:S(2)}) collective-permute-start(bf16[272,128]{1,0:T(8,128)(2,1)S(1)} %shard_map.120.payload_in), channel_id=1, source_target_pairs={{0,8},{1,9},{2,10},{3,11},{4,12},{5,13},{6,14},{7,15},{8,0},{9,1},... | collective-permute-start | bytes 208904 | tf_op jit(solution)/shard_map/ppermute | solution.py:390
  8.8 5.4 %collective-permute-start.1 = (f16[272,128]{1,0:T(8,128)(2,1)S(1)}, f16[272,128]{1,0:T(8,128)(2,1)S(1)}, u32[]{:S(2)}, u32[]{:S(2)}) collective-permute-start(f16[272,128]{1,0:T(8,128)(2,1)S(1)} %fusion.17), channel_id=1, source_target_pairs={{0,16},{1,17},{2,18},{3,19},{4,20},{5,21},{6,22},{7,23},{8,24},{9,... | collective-permute-start | bytes 208904 | tf_op jit(solution)/shard_map/ppermute | solution.py:390
  14.4 5.3 %collective-permute-start.4 = (f16[272,128]{1,0:T(8,128)(2,1)S(1)}, f16[272,128]{1,0:T(8,128)(2,1)S(1)}, u32[]{:S(2)}, u32[]{:S(2)}) collective-permute-start(f16[272,128]{1,0:T(8,128)(2,1)S(1)} %fusion.19), channel_id=1, source_target_pairs={{0,6},{1,7},{2,4},{3,5},{4,2},{5,3},{6,0},{7,1},{8,14},{9,15},{10,... | collective-permute-start | bytes 208904 | tf_op jit(solution)/shard_map/ppermute | solution.py:390
  17.2 4.3 %collective-permute-start.3 = (f16[272,128]{1,0:T(8,128)(2,1)S(1)}, f16[272,128]{1,0:T(8,128)(2,1)S(1)}, u32[]{:S(2)}, u32[]{:S(2)}) collective-permute-start(f16[272,128]{1,0:T(8,128)(2,1)S(1)} %fusion.19), channel_id=1, source_target_pairs={{0,4},{1,5},{2,6},{3,7},{4,0},{5,1},{6,2},{7,3},{8,12},{9,13},{10,... | collective-permute-start | bytes 208904 | tf_op jit(solution)/shard_map/ppermute | solution.py:390
  17.7 4.3 %collective-permute-start.2 = (f16[272,128]{1,0:T(8,128)(2,1)S(1)}, f16[272,128]{1,0:T(8,128)(2,1)S(1)}, u32[]{:S(2)}, u32[]{:S(2)}) collective-permute-start(f16[272,128]{1,0:T(8,128)(2,1)S(1)} %fusion.19), channel_id=1, source_target_pairs={{0,2},{1,3},{2,0},{3,1},{4,6},{5,7},{6,4},{7,5},{8,10},{9,11},{10,... | collective-permute-start | bytes 208904 | tf_op jit(solution)/shard_map/ppermute | solution.py:390
  22.2 1.4 %collective-permute-start.5 = (f32[272,128]{1,0:T(8,128)S(1)}, f32[272,128]{1,0:T(8,128)S(1)}, u32[]{:S(2)}, u32[]{:S(2)}) collective-permute-start(f32[272,128]{1,0:T(8,128)S(1)} %fusion.8.mine), channel_id=1, source_target_pairs={{0,1},{1,0},{2,3},{3,2},{4,5},{5,4},{6,7},{7,6},{8,9},{9,8},{10,11... | collective-permute-start | bytes 417800 | tf_op jit(solution)/shard_map/ppermute | solution.py:390
  27.4 1.4 %collective-permute-start.6 = (bf16[272,256]{1,0:T(8,128)(2,1)S(1)}, bf16[272,256]{1,0:T(8,128)(2,1)S(1)}, u32[]{:S(2)}, u32[]{:S(2)}) collective-permute-start(bf16[272,256]{1,0:T(8,128)(2,1)S(1)} %get-tuple-element.38), channel_id=1, source_target_pairs={{0,1},{1,0},{2,3},{3,2},{4,5},{5,4},{6,7},{7,6},{8,9},{9,8},{10,11... | collective-permute-start | bytes 417800 | tf_op jit(solution)/shard_map/ppermute | solution.py:390
  28.8 4.9 %collective-permute-start.7 = (bf16[144,256]{1,0:T(8,128)(2,1)S(1)}, bf16[144,256]{1,0:T(8,128)(2,1)S(1)}, u32[]{:S(2)}, u32[]{:S(2)}) collective-permute-start(bf16[144,256]{1,0:T(8,128)(2,1)S(1)} %get-tuple-element.39.refs_0_), channel_id=1, source_target_pairs={{0,4},{1,5},{2,6},{3,7},{4,0},{5,1},{6,2},{7,3},{8,12},{9,13},{10,... | collective-permute-start | bytes 221192 | tf_op jit(solution)/shard_map/ppermute | solution.py:390
  30.4 5.3 %collective-permute-start.9 = (bf16[144,256]{1,0:T(8,128)(2,1)S(1)}, bf16[144,256]{1,0:T(8,128)(2,1)S(1)}, u32[]{:S(2)}, u32[]{:S(2)}) collective-permute-start(bf16[144,256]{1,0:T(8,128)(2,1)S(1)} %get-tuple-element.40), channel_id=1, source_target_pairs={{0,6},{1,7},{2,4},{3,5},{4,2},{5,3},{6,0},{7,1},{8,14},{9,15},{10,... | collective-permute-start | bytes 221192 | tf_op jit(solution)/shard_map/ppermute | solution.py:390
  30.6 5.6 %collective-permute-start.8 = (bf16[144,256]{1,0:T(8,128)(2,1)S(1)}, bf16[144,256]{1,0:T(8,128)(2,1)S(1)}, u32[]{:S(2)}, u32[]{:S(2)}) collective-permute-start(bf16[144,256]{1,0:T(8,128)(2,1)S(1)} %get-tuple-element.40), channel_id=1, source_target_pairs={{0,2},{1,3},{2,0},{3,1},{4,6},{5,7},{6,4},{7,5},{8,10},{9,11},{10,... | collective-permute-start | bytes 221192 | tf_op jit(solution)/shard_map/ppermute | solution.py:390
  36.2 4.4 %collective-permute-start.10 = (bf16[144,256]{1,0:T(8,128)(2,1)S(1)}, bf16[144,256]{1,0:T(8,128)(2,1)S(1)}, u32[]{:S(2)}, u32[]{:S(2)}) collective-permute-start(bf16[144,256]{1,0:T(8,128)(2,1)S(1)} %shard_map.125.refs_0_), channel_id=1, source_target_pairs={{0,8},{1,9},{2,10},{3,11},{4,12},{5,13},{6,14},{7,15},{8,0},{9,1},... | collective-permute-start | bytes 221192 | tf_op jit(solution)/shard_map/ppermute | solution.py:390
  40.6 5.3 %collective-permute-start.11 = (bf16[144,256]{1,0:T(8,128)(2,1)S(1)}, bf16[144,256]{1,0:T(8,128)(2,1)S(1)}, u32[]{:S(2)}, u32[]{:S(2)}) collective-permute-start(bf16[144,256]{1,0:T(8,128)(2,1)S(1)} %shard_map.126.mine), channel_id=1, source_target_pairs={{0,16},{1,17},{2,18},{3,19},{4,20},{5,21},{6,22},{7,23},{8,24},{9,... | collective-permute-start | bytes 221192 | tf_op jit(solution)/shard_map/ppermute | solution.py:390

commit v6 on v5

--- a/solution.py
+++ b/solution.py
@@ -34,7 +34,9 @@
 
 
 def dot3(product, a, b):
-    return product(a[0], b[0]) + (product(a[1], b[0]) + product(a[0], b[1]))
+    rows = a[0].shape[0]
+    both = product(jnp.concatenate(a, axis=0), b[0])
+    return both[:rows] + (both[rows:] + product(a[0], b[1]))
 
 
 def head_mask(shape, row_size, lane_size):

time: 46.8 us -> 46.7 us (level)
  no operation moved by 1% of the time
where the time goes in v6:
time: 46.7 us; the launch traced here: 46.5 us
  starting transfers between devices  18.2 us (39%)
  waiting for transfers between devices  17.5 us (37%)
  Pallas kernels  8.56 us (18%)
  local copies, waits for them, and re-layouts  1.12 us (2%)
  between operations  0.76 us (2%)
    ppermute x12, starting transfers between devices, exchange(): return lax.ppermute(a, ALL, [(i, i ^ mask) for i in range(devices)])  18.2 us
    ppermute x12, waiting for transfers between devices, exchange(): return lax.ppermute(a, ALL, [(i, i ^ mask) for i in range(devices)])  17.5 us
    pallas_call x1, Pallas kernels, local(): call(middle_kernel, [((owners // 2 * chunk + extra, width), BF16), ((owne...  3.63 us
    pallas_call x1, Pallas kernels, local(): call(points_kernel, [((token_rows, LANES), BF16)], 2, 8, scratch=[pltpu.V...  1.54 us
    pallas_call x1, Pallas kernels, local(): call(shadow_kernel, [((token_rows, LANES), BF16), ((width, points), BF16)...  1.47 us
    unnamed x16, local copies, waits for them, and re-layouts  1.12 us
    pallas_call x1, Pallas kernels, local(): call(features_kernel, [((points, width), BF16), (maps.shape, F32)], 0, 4)  1.12 us
  transfers between devices with their start and end apart: 12, of which 12 were waited for; matrix products, arithmetic and copies ran while one was open for 0% of the time, Pallas kernels for 6%

profile of v6, /device:TPU:0, one launch (start us, length us, event | category | flops | bytes accessed | tf_op | source)
XLA Modules:
  0.0 46.5 jit_solution(4478348876627705339)
XLA Ops:
  0.7 0.6 %copy-done.6 = f32[8]{0:T(128)S(1)} copy-done((f32[8]{0:T(128)S(1)}, f32[8]{0:T(128)}, u32[]{:S(2)}) %copy-start.6) | copy-done | bytes 56
  1.8 1.5 %shard_map.120.payload_in = bf16[272,128]{1,0:T(8,128)(2,1)S(1)} custom-call(s32[32]{0:T(128)S(1)} %copy-done.7, f32[8]{0:T(128)S(1)} %copy-done.6, bf16[512,256]{1,0:T(8,128)(2,1)S(1)} %copy-done, bf16[512,256]{1,0:T(8,128)(2,1)S(1)} %copy-done.1, bf16[256,256]{1,0:T(8,128)(2,1)S(1)} %copy-done.2, bf16[256,256]{1,0:T(8,128)(2,1)S(1)} %copy-done.3, ...), custom_call_target="tpu_custom_call" | custom-call | tf_op jit(solution)/shard_map/pallas_call | solution.py:456
  3.4 3.0 %collective-permute-start = (bf16[272,128]{1,0:T(8,128)(2,1)S(1)}, bf16[272,128]{1,0:T(8,128)(2,1)S(1)}, u32[]{:S(2)}, u32[]{:S(2)}) collective-permute-start(bf16[272,128]{1,0:T(8,128)(2,1)S(1)} %shard_map.120.payload_in), channel_id=1, source_target_pairs={{0,8},{1,9},{2,10},{3,11},{4,12},{5,13},{6,14},{7,15},{8,0},{9,1},... | collective-permute-start | bytes 208904 | tf_op jit(solution)/shard_map/ppermute | solution.py:392
  6.4 1.5 %shard_map.121 = (bf16[272,128]{1,0:T(8,128)(2,1)S(1)}, bf16[256,512]{1,0:T(8,128)(2,1)S(1)}, bf16[256,512]{1,0:T(8,128)(2,1)S(1)}, bf16[512,512]{1,0:T(8,128)(2...) custom-call(s32[32]{0:T(128)S(1)} %copy-done.7, ...), custom_call_target="tpu_custom_call" | custom-call | tf_op jit(solution)/shard_map/pallas_call | solution.py:471
  7.9 0.8 %collective-permute-done = bf16[272,128]{1,0:T(8,128)(2,1)S(1)} collective-permute-done((bf16[272,128]{1,0:T(8,128)(2,1)S(1)}, bf16[272,128]{1,0:T(8,128)(2,1)S(1)}, u32[]{:S(2)}, u32[]{:S(2)}) %collective-permute-start) | collective-permute-done | bytes 69664 | tf_op jit(solution)/shard_map/ppermute | solution.py:392
  8.8 3.1 %collective-permute-start.1 = (f16[272,128]{1,0:T(8,128)(2,1)S(1)}, f16[272,128]{1,0:T(8,128)(2,1)S(1)}, u32[]{:S(2)}, u32[]{:S(2)}) collective-permute-start(f16[272,128]{1,0:T(8,128)(2,1)S(1)} %fusion.17), channel_id=1, source_target_pairs={{0,16},{1,17},{2,18},{3,19},{4,20},{5,21},{6,22},{7,23},{8,24},{9,... | collective-permute-start | bytes 208904 | tf_op jit(solution)/shard_map/ppermute | solution.py:392
  11.9 2.3 %collective-permute-done.1 = f16[272,128]{1,0:T(8,128)(2,1)S(1)} collective-permute-done((f16[272,128]{1,0:T(8,128)(2,1)S(1)}, f16[272,128]{1,0:T(8,128)(2,1)S(1)}, u32[]{:S(2)}, u32[]{:S(2)}) %collective-permute-start.1) | collective-permute-done | bytes 69664 | tf_op jit(solution)/shard_map/ppermute | solution.py:392
  14.4 2.8 %collective-permute-start.4 = (f16[272,128]{1,0:T(8,128)(2,1)S(1)}, f16[272,128]{1,0:T(8,128)(2,1)S(1)}, u32[]{:S(2)}, u32[]{:S(2)}) collective-permute-start(f16[272,128]{1,0:T(8,128)(2,1)S(1)} %fusion.19), channel_id=1, source_target_pairs={{0,6},{1,7},{2,4},{3,5},{4,2},{5,3},{6,0},{7,1},{8,14},{9,15},{10,... | collective-permute-start | bytes 208904 | tf_op jit(solution)/shard_map/ppermute | solution.py:392
  17.2 0.5 %collective-permute-start.3 = (f16[272,128]{1,0:T(8,128)(2,1)S(1)}, f16[272,128]{1,0:T(8,128)(2,1)S(1)}, u32[]{:S(2)}, u32[]{:S(2)}) collective-permute-start(f16[272,128]{1,0:T(8,128)(2,1)S(1)} %fusion.19), channel_id=1, source_target_pairs={{0,4},{1,5},{2,6},{3,7},{4,0},{5,1},{6,2},{7,3},{8,12},{9,13},{10,... | collective-permute-start | bytes 208904 | tf_op jit(solution)/shard_map/ppermute | solution.py:392
  17.9 1.7 %collective-permute-done.4 = f16[272,128]{1,0:T(8,128)(2,1)S(1)} collective-permute-done((f16[272,128]{1,0:T(8,128)(2,1)S(1)}, f16[272,128]{1,0:T(8,128)(2,1)S(1)}, u32[]{:S(2)}, u32[]{:S(2)}) %collective-permute-start.4) | collective-permute-done | bytes 69664 | tf_op jit(solution)/shard_map/ppermute | solution.py:392
  19.6 1.9 %collective-permute-done.3 = f16[272,128]{1,0:T(8,128)(2,1)S(1)} collective-permute-done((f16[272,128]{1,0:T(8,128)(2,1)S(1)}, f16[272,128]{1,0:T(8,128)(2,1)S(1)}, u32[]{:S(2)}, u32[]{:S(2)}) %collective-permute-start.3) | collective-permute-done | bytes 69664 | tf_op jit(solution)/shard_map/ppermute | solution.py:392
  22.3 1.3 %collective-permute-done.5.other = f32[272,128]{1,0:T(8,128)S(1)} collective-permute-done((f32[272,128]{1,0:T(8,128)S(1)}, f32[272,128]{1,0:T(8,128)S(1)}, u32[]{:S(2)}, u32[]{:S(2)}) %collective-permute-start.5) | collective-permute-done | bytes 139296 | tf_op jit(solution)/shard_map/ppermute | solution.py:392
  23.6 3.6 %shard_map.122 = (bf16[272,256]{1,0:T(8,128)(2,1)S(1)}, bf16[272,256]{1,0:T(8,128)(2,1)S(1)}, bf16[256,512]{1,0:T(8,128)(2,1)S(1)}, f32[128,128]{1,0:T(8,128)S(1)}, f32[128,384]{1,0:T(8,128)S(1)}) custom-call(f32[8]{0:T(128)S(1)} %copy-done.6, f32[272,128]{1,0:T(8,128)S(1)} %fusion.8.mine, f32[272,128]{1,0:T(8,128)S(1)} %collective-permute-done.5.other, ...), custom_call_target="tpu_custom_call" | custom-call | tf_op jit(solution)/shard_map/pallas_call | solution.py:500
  27.5 1.2 %collective-permute-done.6.other = bf16[272,256]{1,0:T(8,128)(2,1)S(1)} collective-permute-done((bf16[272,256]{1,0:T(8,128)(2,1)S(1)}, bf16[272,256]{1,0:T(8,128)(2,1)S(1)}, u32[]{:S(2)}, u32[]{:S(2)}) %collective-permute-start.6) | collective-permute-done | bytes 139296 | tf_op jit(solution)/shard_map/ppermute | solution.py:392
  28.8 1.6 %collective-permute-start.7 = (bf16[144,256]{1,0:T(8,128)(2,1)S(1)}, bf16[144,256]{1,0:T(8,128)(2,1)S(1)}, u32[]{:S(2)}, u32[]{:S(2)}) collective-permute-start(bf16[144,256]{1,0:T(8,128)(2,1)S(1)} %get-tuple-element.39.refs_0_), channel_id=1, source_target_pairs={{0,4},{1,5},{2,6},{3,7},{4,0},{5,1},{6,2},{7,3},{8,12},{9,13},{10,... | collective-permute-start | bytes 221192 | tf_op jit(solution)/shard_map/ppermute | solution.py:392
  30.5 1.8 %collective-permute-start.8 = (bf16[144,256]{1,0:T(8,128)(2,1)S(1)}, bf16[144,256]{1,0:T(8,128)(2,1)S(1)}, u32[]{:S(2)}, u32[]{:S(2)}) collective-permute-start(bf16[144,256]{1,0:T(8,128)(2,1)S(1)} %get-tuple-element.40), channel_id=1, source_target_pairs={{0,2},{1,3},{2,0},{3,1},{4,6},{5,7},{6,4},{7,5},{8,10},{9,11},{10,... | collective-permute-start | bytes 221192 | tf_op jit(solution)/shard_map/ppermute | solution.py:392
  32.3 1.3 %collective-permute-done.7.refs_1_ = bf16[144,256]{1,0:T(8,128)(2,1)S(1)} collective-permute-done((bf16[144,256]{1,0:T(8,128)(2,1)S(1)}, bf16[144,256]{1,0:T(8,128)(2,1)S(1)}, u32[]{:S(2)}, u32[]{:S(2)}) %collective-permute-start.7) | collective-permute-done | bytes 73760 | tf_op jit(solution)/shard_map/ppermute | solution.py:392
  33.6 2.0 %collective-permute-done.9.refs_3_ = bf16[144,256]{1,0:T(8,128)(2,1)S(1)} collective-permute-done((bf16[144,256]{1,0:T(8,128)(2,1)S(1)}, bf16[144,256]{1,0:T(8,128)(2,1)S(1)}, u32[]{:S(2)}, u32[]{:S(2)}) %collective-permute-start.9) | collective-permute-done | bytes 73760 | tf_op jit(solution)/shard_map/ppermute | solution.py:392
  36.1 1.7 %collective-permute-start.10 = (bf16[144,256]{1,0:T(8,128)(2,1)S(1)}, bf16[144,256]{1,0:T(8,128)(2,1)S(1)}, u32[]{:S(2)}, u32[]{:S(2)}) collective-permute-start(bf16[144,256]{1,0:T(8,128)(2,1)S(1)} %shard_map.125.refs_0_), channel_id=1, source_target_pairs={{0,8},{1,9},{2,10},{3,11},{4,12},{5,13},{6,14},{7,15},{8,0},{9,1},... | collective-permute-start | bytes 221192 | tf_op jit(solution)/shard_map/ppermute | solution.py:392
  37.8 2.7 %collective-permute-done.10.refs_1_ = bf16[144,256]{1,0:T(8,128)(2,1)S(1)} collective-permute-done((bf16[144,256]{1,0:T(8,128)(2,1)S(1)}, bf16[144,256]{1,0:T(8,128)(2,1)S(1)}, u32[]{:S(2)}, u32[]{:S(2)}) %collective-permute-start.10) | collective-permute-done | bytes 73760 | tf_op jit(solution)/shard_map/ppermute | solution.py:392
  40.5 2.9 %collective-permute-start.11 = (bf16[144,256]{1,0:T(8,128)(2,1)S(1)}, bf16[144,256]{1,0:T(8,128)(2,1)S(1)}, u32[]{:S(2)}, u32[]{:S(2)}) collective-permute-start(bf16[144,256]{1,0:T(8,128)(2,1)S(1)} %shard_map.126.mine), channel_id=1, source_target_pairs={{0,16},{1,17},{2,18},{3,19},{4,20},{5,21},{6,22},{7,23},{8,24},{9,... | collective-permute-start | bytes 221192 | tf_op jit(solution)/shard_map/ppermute | solution.py:392
  43.5 1.1 %shard_map.123 = (bf16[512,256]{1,0:T(8,128)(2,1)}, f32[3,32,32]{2,1,0:T(8,128)}) custom-call(bf16[256,512]{1,0:T(8,128)(2,1)S(1)} %get-tuple-element.33.gxmt, bf16[256,256]{1,0:T(8,128)(2,1)S(1)} %copy-done.2, f32[128,128]{1,0:T(8,128)S(1)} %get-tuple-element.34.tokens, f32[128,384]{1,0:T(8,128)S(1)} %get-tuple-element.35.grads), custom_call_target="tpu_custom_call" | custom-call | tf_op jit(solution)/shard_map/pallas_call | solution.py:528
  44.6 1.3 %collective-permute-done.11.other = bf16[144,256]{1,0:T(8,128)(2,1)S(1)} collective-permute-done((bf16[144,256]{1,0:T(8,128)(2,1)S(1)}, bf16[144,256]{1,0:T(8,128)(2,1)S(1)}, u32[]{:S(2)}, u32[]{:S(2)}) %collective-permute-start.11) | collective-permute-done | bytes 73760 | tf_op jit(solution)/shard_map/ppermute | solution.py:392
  45.9 0.7 %shard_map.127 = (f32[2,64,256]{2,1,0:T(8,128)}, f32[32,64]{1,0:T(8,128)}, f32[1,8]{1,0:T(1,128)}) custom-call(bf16[144,256]{1,0:T(8,128)(2,1)S(1)} %shard_map.126.mine, bf16[144,256]{1,0:T(8,128)(2,1)S(1)} %collective-permute-done.11.other), custom_call_target="tpu_custom_call" | custom-call | tf_op jit(solution)/shard_map/pallas_call | solution.py:545
  (29 shorter events, 2.7 us)
Async XLA Ops:
  0.6 0.7 %copy-start.6 = (f32[8]{0:T(128)S(1)}, f32[8]{0:T(128)}, u32[]{:S(2)}) copy-start(f32[8]{0:T(128)} %sharp.5) | copy-start | bytes 100
  0.6 0.9 %copy-start.2 = (bf16[256,256]{1,0:T(8,128)(2,1)S(1)}, bf16[256,256]{1,0:T(8,128)(2,1)}, u32[]{:S(2)}) copy-start(bf16[256,256]{1,0:T(8,128)(2,1)} %entry.5) | copy-start | bytes 393220
  0.7 1.0 %copy-start.1 = (bf16[512,256]{1,0:T(8,128)(2,1)S(1)}, bf16[512,256]{1,0:T(8,128)(2,1)}, u32[]{:S(2)}) copy-start(bf16[512,256]{1,0:T(8,128)(2,1)} %rc.5) | copy-start | bytes 786436
  0.7 1.1 %copy-start = (bf16[512,256]{1,0:T(8,128)(2,1)S(1)}, bf16[512,256]{1,0:T(8,128)(2,1)}, u32[]{:S(2)}) copy-start(bf16[512,256]{1,0:T(8,128)(2,1)} %x.5) | copy-start | bytes 786436
  0.7 1.1 %copy-start.7 = (s32[32]{0:T(128)S(1)}, s32[32]{0:T(128)}, u32[]{:S(2)}) copy-start(s32[32]{0:T(128)} %tally.3) | copy-start | bytes 388
  0.7 1.1 %copy-start.5 = (bf16[32,64]{1,0:T(8,128)(2,1)S(1)}, bf16[32,64]{1,0:T(8,128)(2,1)}, u32[]{:S(2)}) copy-start(bf16[32,64]{1,0:T(8,128)(2,1)} %cluster.3) | copy-start | bytes 12292
  0.7 1.1 %copy-start.3 = (bf16[256,256]{1,0:T(8,128)(2,1)S(1)}, bf16[256,256]{1,0:T(8,128)(2,1)}, u32[]{:S(2)}) copy-start(bf16[256,256]{1,0:T(8,128)(2,1)} %exit_.3) | copy-start | bytes 393220
  1.8 4.6 %copy-start.4 = (f32[3,32,32]{2,1,0:T(8,128)S(1)}, f32[3,32,32]{2,1,0:T(8,128)}, u32[]{:S(2)}) copy-start(f32[3,32,32]{2,1,0:T(8,128)} %maps.1) | copy-start | bytes 36868
  3.4 5.3 %collective-permute-start = (bf16[272,128]{1,0:T(8,128)(2,1)S(1)}, bf16[272,128]{1,0:T(8,128)(2,1)S(1)}, u32[]{:S(2)}, u32[]{:S(2)}) collective-permute-start(bf16[272,128]{1,0:T(8,128)(2,1)S(1)} %shard_map.120.payload_in), channel_id=1, source_target_pairs={{0,8},{1,9},{2,10},{3,11},{4,12},{5,13},{6,14},{7,15},{8,0},{9,1},... | collective-permute-start | bytes 208904 | tf_op jit(solution)/shard_map/ppermute | solution.py:392
  8.8 5.4 %collective-permute-start.1 = (f16[272,128]{1,0:T(8,128)(2,1)S(1)}, f16[272,128]{1,0:T(8,128)(2,1)S(1)}, u32[]{:S(2)}, u32[]{:S(2)}) collective-permute-start(f16[272,128]{1,0:T(8,128)(2,1)S(1)} %fusion.17), channel_id=1, source_target_pairs={{0,16},{1,17},{2,18},{3,19},{4,20},{5,21},{6,22},{7,23},{8,24},{9,... | collective-permute-start | bytes 208904 | tf_op jit(solution)/shard_map/ppermute | solution.py:392
  14.4 5.3 %collective-permute-start.4 = (f16[272,128]{1,0:T(8,128)(2,1)S(1)}, f16[272,128]{1,0:T(8,128)(2,1)S(1)}, u32[]{:S(2)}, u32[]{:S(2)}) collective-permute-start(f16[272,128]{1,0:T(8,128)(2,1)S(1)} %fusion.19), channel_id=1, source_target_pairs={{0,6},{1,7},{2,4},{3,5},{4,2},{5,3},{6,0},{7,1},{8,14},{9,15},{10,... | collective-permute-start | bytes 208904 | tf_op jit(solution)/shard_map/ppermute | solution.py:392
  17.2 4.3 %collective-permute-start.3 = (f16[272,128]{1,0:T(8,128)(2,1)S(1)}, f16[272,128]{1,0:T(8,128)(2,1)S(1)}, u32[]{:S(2)}, u32[]{:S(2)}) collective-permute-start(f16[272,128]{1,0:T(8,128)(2,1)S(1)} %fusion.19), channel_id=1, source_target_pairs={{0,4},{1,5},{2,6},{3,7},{4,0},{5,1},{6,2},{7,3},{8,12},{9,13},{10,... | collective-permute-start | bytes 208904 | tf_op jit(solution)/shard_map/ppermute | solution.py:392
  17.7 4.3 %collective-permute-start.2 = (f16[272,128]{1,0:T(8,128)(2,1)S(1)}, f16[272,128]{1,0:T(8,128)(2,1)S(1)}, u32[]{:S(2)}, u32[]{:S(2)}) collective-permute-start(f16[272,128]{1,0:T(8,128)(2,1)S(1)} %fusion.19), channel_id=1, source_target_pairs={{0,2},{1,3},{2,0},{3,1},{4,6},{5,7},{6,4},{7,5},{8,10},{9,11},{10,... | collective-permute-start | bytes 208904 | tf_op jit(solution)/shard_map/ppermute | solution.py:392
  22.2 1.4 %collective-permute-start.5 = (f32[272,128]{1,0:T(8,128)S(1)}, f32[272,128]{1,0:T(8,128)S(1)}, u32[]{:S(2)}, u32[]{:S(2)}) collective-permute-start(f32[272,128]{1,0:T(8,128)S(1)} %fusion.8.mine), channel_id=1, source_target_pairs={{0,1},{1,0},{2,3},{3,2},{4,5},{5,4},{6,7},{7,6},{8,9},{9,8},{10,11... | collective-permute-start | bytes 417800 | tf_op jit(solution)/shard_map/ppermute | solution.py:392
  27.3 1.4 %collective-permute-start.6 = (bf16[272,256]{1,0:T(8,128)(2,1)S(1)}, bf16[272,256]{1,0:T(8,128)(2,1)S(1)}, u32[]{:S(2)}, u32[]{:S(2)}) collective-permute-start(bf16[272,256]{1,0:T(8,128)(2,1)S(1)} %get-tuple-element.38), channel_id=1, source_target_pairs={{0,1},{1,0},{2,3},{3,2},{4,5},{5,4},{6,7},{7,6},{8,9},{9,8},{10,11... | collective-permute-start | bytes 417800 | tf_op jit(solution)/shard_map/ppermute | solution.py:392
  28.8 4.9 %collective-permute-start.7 = (bf16[144,256]{1,0:T(8,128)(2,1)S(1)}, bf16[144,256]{1,0:T(8,128)(2,1)S(1)}, u32[]{:S(2)}, u32[]{:S(2)}) collective-permute-start(bf16[144,256]{1,0:T(8,128)(2,1)S(1)} %get-tuple-element.39.refs_0_), channel_id=1, source_target_pairs={{0,4},{1,5},{2,6},{3,7},{4,0},{5,1},{6,2},{7,3},{8,12},{9,13},{10,... | collective-permute-start | bytes 221192 | tf_op jit(solution)/shard_map/ppermute | solution.py:392
  30.3 5.3 %collective-permute-start.9 = (bf16[144,256]{1,0:T(8,128)(2,1)S(1)}, bf16[144,256]{1,0:T(8,128)(2,1)S(1)}, u32[]{:S(2)}, u32[]{:S(2)}) collective-permute-start(bf16[144,256]{1,0:T(8,128)(2,1)S(1)} %get-tuple-element.40), channel_id=1, source_target_pairs={{0,6},{1,7},{2,4},{3,5},{4,2},{5,3},{6,0},{7,1},{8,14},{9,15},{10,... | collective-permute-start | bytes 221192 | tf_op jit(solution)/shard_map/ppermute | solution.py:392
  30.5 5.6 %collective-permute-start.8 = (bf16[144,256]{1,0:T(8,128)(2,1)S(1)}, bf16[144,256]{1,0:T(8,128)(2,1)S(1)}, u32[]{:S(2)}, u32[]{:S(2)}) collective-permute-start(bf16[144,256]{1,0:T(8,128)(2,1)S(1)} %get-tuple-element.40), channel_id=1, source_target_pairs={{0,2},{1,3},{2,0},{3,1},{4,6},{5,7},{6,4},{7,5},{8,10},{9,11},{10,... | collective-permute-start | bytes 221192 | tf_op jit(solution)/shard_map/ppermute | solution.py:392
  36.1 4.4 %collective-permute-start.10 = (bf16[144,256]{1,0:T(8,128)(2,1)S(1)}, bf16[144,256]{1,0:T(8,128)(2,1)S(1)}, u32[]{:S(2)}, u32[]{:S(2)}) collective-permute-start(bf16[144,256]{1,0:T(8,128)(2,1)S(1)} %shard_map.125.refs_0_), channel_id=1, source_target_pairs={{0,8},{1,9},{2,10},{3,11},{4,12},{5,13},{6,14},{7,15},{8,0},{9,1},... | collective-permute-start | bytes 221192 | tf_op jit(solution)/shard_map/ppermute | solution.py:392
  40.5 5.3 %collective-permute-start.11 = (bf16[144,256]{1,0:T(8,128)(2,1)S(1)}, bf16[144,256]{1,0:T(8,128)(2,1)S(1)}, u32[]{:S(2)}, u32[]{:S(2)}) collective-permute-start(bf16[144,256]{1,0:T(8,128)(2,1)S(1)} %shard_map.126.mine), channel_id=1, source_target_pairs={{0,16},{1,17},{2,18},{3,19},{4,20},{5,21},{6,22},{7,23},{8,24},{9,... | collective-permute-start | bytes 221192 | tf_op jit(solution)/shard_map/ppermute | solution.py:392
